TPU v7x, 256 devices: a whole 4x4x8 slice. The times are simulated.
256 devices in a mesh: rows: 32 (over x, z), cols: 8 (over y, core).
Axes of the slice: x: 4, y: 4, z: 8, core: 2. Of those that a mesh axis runs over, the one named last changes fastest.
Arguments:
- vectors: bfloat16 [65536, 768], P('rows'), may hold values from -24 to 24
- centroids: bfloat16 [8192, 768], P('cols'), may hold values from -0.2 to 0.2
Outputs:
- new_centroids: float32 [8192, 768], P('cols')
- row_potential: float32 [65536], P('rows')
- col_potential: float32 [8192], P('cols')
All inputs are finite; a program needn't handle non-finite values.
Results may differ from a plain program's by a relative error of at most 0.0023.
Values sent between devices are 32-bit elements; how exact they have to be, the bound alone decides.
No kernel may reach another device: no remote copies, remote signals or barrier semaphores. Data moves between devices by JAX's collectives and lax.ppermute only.
A program may use at most 64 MiB of HBM per device.

v0:
```python
import math

import jax
import jax.numpy as jnp
from jax import lax
from jax.sharding import PartitionSpec as P

ITERS = 3


def vector_lse(z):
    local_top = jnp.max(z, axis=1)
    top = lax.pmax(local_top, "cols")
    total = lax.psum(jnp.sum(jnp.exp(z - top[:, None]), axis=1), "cols")
    return top + jnp.log(total)


def centroid_lse(z):
    local_top = jnp.max(z, axis=0)
    top = lax.pmax(local_top, "rows")
    total = lax.psum(jnp.sum(jnp.exp(z - top[None, :]), axis=0), "rows")
    return top + jnp.log(total)


def per_device(vectors, centroids):
    total_rows = vectors.shape[0] * lax.axis_size("rows")
    total_cents = centroids.shape[0] * lax.axis_size("cols")
    log_target = math.log(total_rows / total_cents)
    logits = 4.0 * lax.dot_general(
        vectors, centroids, (((1,), (1,)), ((), ())), preferred_element_type=jnp.float32
    )
    col_pot = jnp.zeros((centroids.shape[0],), jnp.float32)
    for step in range(ITERS):
        row_pot = -vector_lse(logits + col_pot[None, :])
        col_pot = log_target - centroid_lse(logits + row_pot[:, None])
    row_pot = -vector_lse(logits + col_pot[None, :])
    plan = jnp.exp(logits + row_pot[:, None] + col_pot[None, :])
    mass = jnp.sum(plan, axis=0)
    plan_b = plan.astype(jnp.bfloat16)
    weighted = lax.dot_general(
        plan_b, vectors, (((0,), (0,)), ((), ())), preferred_element_type=jnp.float32
    )
    full_sum, full_mass = lax.psum((weighted, mass), "rows")
    new_centroids = full_sum / full_mass[:, None]
    return (new_centroids, row_pot, col_pot)


def solution(mesh):
    return jax.shard_map(
        per_device,
        mesh=mesh,
        in_specs=(P("rows", None), P("cols", None)),
        out_specs=(P("cols", None), P("rows"), P("cols")),
        check_vma=False,
    )
```

profile of v0, /device:TPU:8, one launch (start us, length us, event | category | flops | bytes accessed | tf_op | source)
XLA Modules:
  0.0 775.4 jit_solution(16588857388250555818)
XLA Ops:
  7.2 0.0 copy-start
  7.2 0.0 all-reduce.2.cloned.1.call-start
  7.2 1.8 copy-done
  9.1 7.0 fusion.6
  16.1 12.0 %pmax.49 = f32[2048]{0:T(1024)S(1)} all-reduce(f32[2048]{0:T(1024)S(1)} %get-tuple-element.3), channel_id=1, replica_groups=mesh['rows'=32,'cols'=8] {'cols'}, use_global_device_ids=true, to_apply=%region_1.0 | all-reduce | flops 2048 | bytes 16384 | tf_op jit(solution)/shard_map/pmax | solution.py:13
  28.1 4.5 exponential_reduce_fusion.6
  32.7 12.7 %psum.63 = f32[2048]{0:T(1024)S(1)} all-reduce(f32[2048]{0:T(1024)S(1)} %exponential_reduce_fusion.6), channel_id=1, replica_groups=mesh['rows'=32,'cols'=8] {'cols'}, use_global_device_ids=true, to_apply=%region_3.0 | all-reduce | flops 2048 | bytes 16384 | tf_op jit(solution)/shard_map/psum | solution.py:14
  45.4 4.0 add_reduce_fusion.5
  49.4 77.7 %pmax.50 = f32[1024]{0:T(1024)S(1)} all-reduce(f32[1024]{0:T(1024)S(1)} %add_reduce_fusion.5), channel_id=1, replica_groups=mesh['rows'=32,'cols'=8] {'rows'}, use_global_device_ids=true, to_apply=%region_5.0 | all-reduce | flops 1024 | bytes 8192 | tf_op jit(solution)/shard_map/pmax | solution.py:20
  127.1 4.4 exponential_reduce_fusion.5
  131.4 69.6 %psum.64 = f32[1024]{0:T(1024)S(1)} all-reduce(f32[1024]{0:T(1024)S(1)} %exponential_reduce_fusion.5), channel_id=1, replica_groups=mesh['rows'=32,'cols'=8] {'rows'}, use_global_device_ids=true, to_apply=%region_7.0 | all-reduce | flops 1024 | bytes 8192 | tf_op jit(solution)/shard_map/psum | solution.py:21
  201.1 4.0 add_reduce_fusion.4
  205.1 12.7 %pmax.51 = f32[2048]{0:T(1024)S(1)} all-reduce(f32[2048]{0:T(1024)S(1)} %add_reduce_fusion.4), channel_id=1, replica_groups=mesh['rows'=32,'cols'=8] {'cols'}, use_global_device_ids=true, to_apply=%region_9.0 | all-reduce | flops 2048 | bytes 16384 | tf_op jit(solution)/shard_map/pmax | solution.py:13
  217.8 4.3 exponential_reduce_fusion.4
  222.1 13.2 %psum.65 = f32[2048]{0:T(1024)S(1)} all-reduce(f32[2048]{0:T(1024)S(1)} %exponential_reduce_fusion.4), channel_id=1, replica_groups=mesh['rows'=32,'cols'=8] {'cols'}, use_global_device_ids=true, to_apply=%region_11.0 | all-reduce | flops 2048 | bytes 16384 | tf_op jit(solution)/shard_map/psum | solution.py:14
  235.3 4.0 add_reduce_fusion.3
  239.3 71.7 %pmax.52 = f32[1024]{0:T(1024)S(1)} all-reduce(f32[1024]{0:T(1024)S(1)} %add_reduce_fusion.3), channel_id=1, replica_groups=mesh['rows'=32,'cols'=8] {'rows'}, use_global_device_ids=true, to_apply=%region_13.0 | all-reduce | flops 1024 | bytes 8192 | tf_op jit(solution)/shard_map/pmax | solution.py:20
  311.0 4.4 exponential_reduce_fusion.3
  315.3 69.6 %psum.66 = f32[1024]{0:T(1024)S(1)} all-reduce(f32[1024]{0:T(1024)S(1)} %exponential_reduce_fusion.3), channel_id=1, replica_groups=mesh['rows'=32,'cols'=8] {'rows'}, use_global_device_ids=true, to_apply=%region_15.0 | all-reduce | flops 1024 | bytes 8192 | tf_op jit(solution)/shard_map/psum | solution.py:21
  385.0 4.0 add_reduce_fusion.2
  389.0 12.1 %pmax.53 = f32[2048]{0:T(1024)S(1)} all-reduce(f32[2048]{0:T(1024)S(1)} %add_reduce_fusion.2), channel_id=1, replica_groups=mesh['rows'=32,'cols'=8] {'cols'}, use_global_device_ids=true, to_apply=%region_17.0 | all-reduce | flops 2048 | bytes 16384 | tf_op jit(solution)/shard_map/pmax | solution.py:13
  401.1 4.3 exponential_reduce_fusion.2
  405.4 13.2 %psum.67 = f32[2048]{0:T(1024)S(1)} all-reduce(f32[2048]{0:T(1024)S(1)} %exponential_reduce_fusion.2), channel_id=1, replica_groups=mesh['rows'=32,'cols'=8] {'cols'}, use_global_device_ids=true, to_apply=%region_19.0 | all-reduce | flops 2048 | bytes 16384 | tf_op jit(solution)/shard_map/psum | solution.py:14
  418.6 4.0 add_reduce_fusion.1
  422.6 71.7 %pmax.54 = f32[1024]{0:T(1024)S(1)} all-reduce(f32[1024]{0:T(1024)S(1)} %add_reduce_fusion.1), channel_id=1, replica_groups=mesh['rows'=32,'cols'=8] {'rows'}, use_global_device_ids=true, to_apply=%region_21.0 | all-reduce | flops 1024 | bytes 8192 | tf_op jit(solution)/shard_map/pmax | solution.py:20
  494.3 4.4 exponential_reduce_fusion.1
  498.7 69.8 %psum.68 = f32[1024]{0:T(1024)S(1)} all-reduce(f32[1024]{0:T(1024)S(1)} %exponential_reduce_fusion.1), channel_id=1, replica_groups=mesh['rows'=32,'cols'=8] {'rows'}, use_global_device_ids=true, to_apply=%region_23.0 | all-reduce | flops 1024 | bytes 8192 | tf_op jit(solution)/shard_map/psum | solution.py:21
  568.5 0.0 copy-start.1
  568.5 4.0 add_reduce_fusion
  572.5 12.1 %pmax.55 = f32[2048]{0:T(1024)S(1)} all-reduce(f32[2048]{0:T(1024)S(1)} %add_reduce_fusion), channel_id=1, replica_groups=mesh['rows'=32,'cols'=8] {'cols'}, use_global_device_ids=true, to_apply=%region_25.0 | all-reduce | flops 2048 | bytes 16384 | tf_op jit(solution)/shard_map/pmax | solution.py:13
  584.6 4.3 exponential_reduce_fusion
  589.0 13.2 %psum.69 = f32[2048]{0:T(1024)S(1)} all-reduce(f32[2048]{0:T(1024)S(1)} %exponential_reduce_fusion), channel_id=1, replica_groups=mesh['rows'=32,'cols'=8] {'cols'}, use_global_device_ids=true, to_apply=%region_27.0 | all-reduce | flops 2048 | bytes 16384 | tf_op jit(solution)/shard_map/psum | solution.py:14
  602.2 0.0 copy-start.2
  602.2 8.7 %fusion.2 = f32[1024,768]{1,0:T(8,128)} fusion(bf16[2048,768]{1,0:T(8,128)(2,1)S(1)} %copy-done, f32[2048,1024]{0,1:T(8,128)} %get-tuple-element.4, f32[2048]{0:T(1024)S(1)} %add_negate_fusion, f32[1024]{0:T(1024)S(1)} %add_subtract_fusion), kind=kOutput, calls=%fused_computation.17 | convolution fusion | flops 3227516928 | bytes 14692352 | tf_op jit(solution)/shard_map/dot_general | solution.py:40
  610.9 0.0 all-reduce.2.cloned.1.call-update
  610.9 0.0 copy-done.1
  610.9 0.0 copy-done.2
  610.9 4.4 fusion
  615.3 72.0 %psum.71 = f32[1024]{0:T(1024)S(1)} all-reduce(f32[1024]{0:T(1024)S(1)} %fusion), channel_id=1, replica_groups=mesh['rows'=32,'cols'=8] {'rows'}, use_global_device_ids=true, to_apply=%region_30.0 | all-reduce | flops 1024 | bytes 8192 | tf_op jit(solution)/shard_map/psum | solution.py:43
  687.3 77.4 %all-reduce.2.cloned.1.call-done = f32[1024,768]{1,0:T(8,128)} async-done(((f32[1024,768]{1,0:T(8,128)}), f32[1024,768]{1,0:T(8,128)}) %all-reduce.2.cloned.1.call-update) | async-done | bytes 3145744 | tf_op jit(solution)/shard_map/psum | solution.py:43
  764.7 3.8 broadcast_divide_fusion
  (7 shorter events, 0.1 us)
Async XLA Ops:
  7.2 1.9 copy-start
  7.2 757.5 %all-reduce.2.cloned.1.call-start = ((), (), s32[]{:S(2)}) async-start(), calls=%async_computation | async-start | bytes 6291456 | tf_op jit(solution)/shard_map/psum | solution.py:43
  568.5 42.4 %copy-start.1 = (f32[1024]{0:T(1024)}, f32[1024]{0:T(1024)S(1)}, u32[]{:S(2)}) copy-start(f32[1024]{0:T(1024)S(1)} %add_subtract_fusion) | copy-start | bytes 12292
  602.2 8.7 %copy-start.2 = (f32[2048]{0:T(1024)}, f32[2048]{0:T(1024)S(1)}, u32[]{:S(2)}) copy-start(f32[2048]{0:T(1024)S(1)} %add_negate_fusion) | copy-start | bytes 24580
Sparse Core Ops, SparseCore 0:
  611.0 153.6 all-reduce.1
where the time goes:
time: 776 us; the launch traced here: 775 us
  blocking collectives  603 us (78%)
  waiting for transfers between devices  77.5 us (10%)
  other arithmetic  62.9 us (8%)
  matrix products  15.7 us (2%)
  between operations  14.2 us (2%)
    pmax x3, blocking collectives, centroid_lse(): top = lax.pmax(local_top, 'rows')  221 us
    psum x3, blocking collectives, centroid_lse(): total = lax.psum(jnp.sum(jnp.exp(z - top[None, :]), axis=0), 'rows')  209 us
    psum x1, waiting for transfers between devices, per_device(): full_sum, full_mass = lax.psum((weighted, mass), 'rows')  77.4 us
    psum x1, blocking collectives, per_device(): full_sum, full_mass = lax.psum((weighted, mass), 'rows')  72 us
    psum x4, blocking collectives, vector_lse(): total = lax.psum(jnp.sum(jnp.exp(z - top[:, None]), axis=1), 'cols')  52.2 us
    pmax x4, blocking collectives, vector_lse(): top = lax.pmax(local_top, 'cols')  48.9 us
    reduce_sum x4, other arithmetic, vector_lse(): total = lax.psum(jnp.sum(jnp.exp(z - top[:, None]), axis=1), 'cols')  17.5 us
  transfers between devices with their start and end apart: 1, of which 1 were waited for; matrix products, arithmetic and copies ran while one was open for 1% of the time, Pallas kernels for 0%

commit v1 on v0

v1 whole, which is shorter than its diff:
```python
import functools
import math

import jax
import jax.numpy as jnp
from jax import lax
from jax.experimental import pallas as pl
from jax.experimental.pallas import tpu as pltpu
from jax.sharding import PartitionSpec as P

ITERS = 3
LANES = 128
LIM = 40.0
VMEM_LIMIT = 48 * 1024 * 1024
F32 = jnp.float32


def combine_lse(parts):
    top = jnp.max(parts, axis=0)
    return top + jnp.log(jnp.sum(jnp.exp(parts - top[None]), axis=0))


def lane_to_sublane(row):
    return jnp.transpose(jnp.broadcast_to(row, (LANES, LANES)))


def fold(x):
    return jnp.sum(x.reshape(x.shape[0] // 8, 8, x.shape[1]), axis=0)


def lane_group(g):
    return slice(g * LANES, (g + 1) * LANES)


def row_tile(t):
    return pl.ds(pl.multiple_of(t * LANES, LANES), LANES)


def put_copies(out_ref, value):
    for k in range(out_ref.shape[0]):
        out_ref[k] = value


def logit_block(k_ref, ok, t, g):
    block = k_ref[row_tile(t), lane_group(g)]
    return jnp.where(ok != 0, jnp.log(block), block)


def row_lse_exact(k_ref, ok, pot_ref, out_ref):
    tiles, groups = k_ref.shape[0] // LANES, k_ref.shape[1] // LANES

    def shifted(t, g):
        z = logit_block(k_ref, ok, t, g)
        return z if pot_ref is None else z + lane_to_sublane(pot_ref[pl.ds(t, 1), :])

    for g in range(groups):
        def top_of(t, top, g=g):
            return jnp.maximum(top, jnp.max(shifted(t, g), axis=0, keepdims=True))

        top = lax.fori_loop(0, tiles, top_of, jnp.full((1, LANES), -3.0e38, F32))

        def sum_of(t, total, g=g, top=top):
            return total + jnp.sum(jnp.exp(shifted(t, g) - top), axis=0, keepdims=True)

        total = lax.fori_loop(0, tiles, sum_of, jnp.zeros((1, LANES), F32))
        out_ref[g : g + 1, :] = top + jnp.log(total)


def col_lse_exact(k_ref, ok, pot, out_ref):
    tiles, groups = k_ref.shape[0] // LANES, k_ref.shape[1] // LANES

    def tile(t, carry):
        top = jnp.full((LANES, LANES), -3.0e38, F32)
        for g in range(groups):
            top = jnp.maximum(top, logit_block(k_ref, ok, t, g) + pot[g : g + 1, :])
        top = jnp.broadcast_to(jnp.max(top, axis=1, keepdims=True), (LANES, LANES))
        total = jnp.zeros((LANES, LANES), F32)
        for g in range(groups):
            total = total + jnp.exp(logit_block(k_ref, ok, t, g) + pot[g : g + 1, :] - top)
        total = jnp.sum(jnp.transpose(total), axis=0, keepdims=True)
        out_ref[pl.ds(t, 1), :] = jnp.transpose(top)[0:1, :] + jnp.log(total)
        return carry

    lax.fori_loop(0, tiles, tile, 0)


def logits_kernel(cent_ref, vec_ref, k_ref, ok_ref, out_ref, lse_ref):
    cents, rows = k_ref.shape
    groups = rows // LANES
    step = 256

    def logits(t):
        return 4.0 * lax.dot_general(
            cent_ref[t * step : (t + 1) * step, :], vec_ref[...],
            (((1,), (1,)), ((), ())), preferred_element_type=F32,
        )

    sums = [jnp.zeros((8, LANES), F32)] * groups
    peak = jnp.zeros((8, LANES), F32)
    for t in range(cents // step):
        block = logits(t)
        for g in range(groups):
            part = block[:, lane_group(g)]
            size = jnp.abs(part)
            peak = jnp.maximum(peak, jnp.max(size.reshape(step // 8, 8, LANES), axis=0))
            part = jnp.exp(part)
            k_ref[t * step : (t + 1) * step, lane_group(g)] = part
            sums[g] = sums[g] + fold(part)
    for g in range(groups):
        lse_ref[g : g + 1, :] = jnp.log(jnp.sum(sums[g], axis=0, keepdims=True))
    ok = jnp.max(peak) <= LIM
    ok_ref[0, 0] = ok.astype(jnp.int32)

    @pl.when(jnp.logical_not(ok))
    def _():
        def tile(t, carry):
            at = pl.ds(pl.multiple_of(t * LANES, LANES), LANES)
            for g in range(groups):
                k_ref[at, lane_group(g)] = 4.0 * lax.dot_general(
                    cent_ref[at, :], vec_ref[lane_group(g), :],
                    (((1,), (1,)), ((), ())), preferred_element_type=F32,
                )
            return carry

        lax.fori_loop(0, cents // LANES, tile, 0)
        row_lse_exact(k_ref, 0, None, lse_ref)

    put_copies(out_ref, lse_ref[...])


def row_kernel(log_target, got_ref, ok_ref, k_ref, out_ref, pot_ref, lse_ref):
    tiles, groups = k_ref.shape[0] // LANES, k_ref.shape[1] // LANES
    pot = log_target - combine_lse(got_ref[...])
    ok = ok_ref[0, 0]
    fast = jnp.logical_and(ok != 0, jnp.max(jnp.abs(pot)) <= LIM)

    @pl.when(fast)
    def _():
        pot_ref[...] = jnp.exp(pot)

        def tile(t, sums):
            scale = lane_to_sublane(pot_ref[pl.ds(t, 1), :])
            return tuple(
                sums[g] + fold(k_ref[row_tile(t), lane_group(g)] * scale) for g in range(groups)
            )

        sums = lax.fori_loop(0, tiles, tile, (jnp.zeros((8, LANES), F32),) * groups)
        for g in range(groups):
            lse_ref[g : g + 1, :] = jnp.sum(sums[g], axis=0, keepdims=True)
        lse_ref[...] = jnp.log(lse_ref[...])

    @pl.when(jnp.logical_not(fast))
    def _():
        pot_ref[...] = pot
        row_lse_exact(k_ref, ok, pot_ref, lse_ref)

    put_copies(out_ref, lse_ref[...])


def col_kernel(got_ref, ok_ref, k_ref, out_ref, lse_ref):
    tiles, groups = k_ref.shape[0] // LANES, k_ref.shape[1] // LANES
    pot = -combine_lse(got_ref[...])
    ok = ok_ref[0, 0]
    fast = jnp.logical_and(ok != 0, jnp.max(jnp.abs(pot)) <= LIM)

    @pl.when(fast)
    def _():
        scale = jnp.exp(pot)

        def tile(t, carry):
            total = jnp.zeros((LANES, LANES), F32)
            for g in range(groups):
                total = total + k_ref[row_tile(t), lane_group(g)] * scale[g : g + 1, :]
            lse_ref[pl.ds(t, 1), :] = jnp.sum(jnp.transpose(total), axis=0, keepdims=True)
            return carry

        lax.fori_loop(0, tiles, tile, 0)
        lse_ref[...] = jnp.log(lse_ref[...])

    @pl.when(jnp.logical_not(fast))
    def _():
        col_lse_exact(k_ref, ok, pot, lse_ref)

    put_copies(out_ref, lse_ref[...])


def final_kernel(
    log_target, cols_ref, rows_ref, ok_ref, k_ref, vec_ref,
    weighted_ref, mass_ref, row_pot_ref, col_pot_ref, scale_ref, plan_ref,
):
    tiles, groups = k_ref.shape[0] // LANES, k_ref.shape[1] // LANES
    col_pot = log_target - combine_lse(cols_ref[...])
    row_pot = -combine_lse(rows_ref[...])
    col_pot_ref[...] = col_pot
    row_pot_ref[...] = row_pot
    ok = ok_ref[0, 0]
    fast = jnp.logical_and(
        ok != 0, jnp.maximum(jnp.max(jnp.abs(col_pot)), jnp.max(jnp.abs(row_pot))) <= LIM
    )

    def plan_tile(t, block):
        total = jnp.zeros((LANES, LANES), F32)
        for g in range(groups):
            plan = block(g)
            total = total + plan
            plan_ref[row_tile(t), lane_group(g)] = plan.astype(jnp.bfloat16)
        mass_ref[pl.ds(t, 1), :] = jnp.sum(jnp.transpose(total), axis=0, keepdims=True)

    @pl.when(fast)
    def _():
        scale_ref[...] = jnp.exp(col_pot)
        row_scale = jnp.exp(row_pot)

        def tile(t, carry):
            scale = lane_to_sublane(scale_ref[pl.ds(t, 1), :])
            plan_tile(
                t, lambda g: k_ref[row_tile(t), lane_group(g)] * row_scale[g : g + 1, :] * scale
            )
            return carry

        lax.fori_loop(0, tiles, tile, 0)

    @pl.when(jnp.logical_not(fast))
    def _():
        scale_ref[...] = col_pot

        def tile(t, carry):
            shift = lane_to_sublane(scale_ref[pl.ds(t, 1), :])
            plan_tile(
                t, lambda g: jnp.exp(logit_block(k_ref, ok, t, g) + row_pot[g : g + 1, :] + shift)
            )
            return carry

        lax.fori_loop(0, tiles, tile, 0)

    step = 256
    for t in range(k_ref.shape[0] // step):
        at = slice(t * step, (t + 1) * step)
        weighted_ref[at, :] = jnp.dot(plan_ref[at, :], vec_ref[...], preferred_element_type=F32)


def vmem():
    return pl.BlockSpec(memory_space=pltpu.VMEM)


def smem():
    return pl.BlockSpec(memory_space=pltpu.SMEM)


def params():
    return pltpu.CompilerParams(vmem_limit_bytes=VMEM_LIMIT)


def per_device(vectors, centroids):
    n_rows, n_cols = lax.axis_size("rows"), lax.axis_size("cols")
    rows, width = vectors.shape
    cents = centroids.shape[0]
    log_target = math.log(rows * n_rows / (cents * n_cols))
    groups, tiles = rows // LANES, cents // LANES
    kept = jax.ShapeDtypeStruct((cents, rows), F32)
    ok_type = jax.ShapeDtypeStruct((1, 1), jnp.int32)
    row_parts = jax.ShapeDtypeStruct((n_cols, groups, LANES), F32)
    col_parts = jax.ShapeDtypeStruct((n_rows, tiles, LANES), F32)
    row_scratch = pltpu.VMEM((groups, LANES), F32)
    col_scratch = pltpu.VMEM((tiles, LANES), F32)

    kernel, ok, part = pl.pallas_call(
        logits_kernel,
        out_shape=(kept, ok_type, row_parts),
        in_specs=[vmem(), vmem()],
        out_specs=(vmem(), smem(), vmem()),
        scratch_shapes=[row_scratch],
        compiler_params=params(),
        name="logits",
    )(centroids, vectors)

    for step in range(ITERS):
        row_got = lax.all_to_all(part, "cols", 0, 0, tiled=True)
        part = pl.pallas_call(
            col_kernel,
            out_shape=col_parts,
            in_specs=[vmem(), smem(), vmem()],
            out_specs=vmem(),
            scratch_shapes=[col_scratch],
            compiler_params=params(),
            name="col_step",
        )(row_got, ok, kernel)
        col_got = lax.all_to_all(part, "rows", 0, 0, tiled=True)
        part = pl.pallas_call(
            functools.partial(row_kernel, log_target),
            out_shape=row_parts,
            in_specs=[vmem(), smem(), vmem()],
            out_specs=vmem(),
            scratch_shapes=[col_scratch, row_scratch],
            compiler_params=params(),
            name="row_step",
        )(col_got, ok, kernel)
    row_got = lax.all_to_all(part, "cols", 0, 0, tiled=True)

    weighted, mass, row_pot, col_pot = pl.pallas_call(
        functools.partial(final_kernel, log_target),
        out_shape=(
            jax.ShapeDtypeStruct((cents, width), F32),
            jax.ShapeDtypeStruct((tiles, LANES), F32),
            jax.ShapeDtypeStruct((groups, LANES), F32),
            jax.ShapeDtypeStruct((tiles, LANES), F32),
        ),
        in_specs=[vmem(), vmem(), smem(), vmem(), vmem()],
        out_specs=(vmem(), vmem(), vmem(), vmem()),
        scratch_shapes=[col_scratch, pltpu.VMEM((cents, rows), jnp.bfloat16)],
        compiler_params=params(),
        name="weighted_sums",
    )(col_got, row_got, ok, kernel, vectors)

    masses = lax.all_to_all(
        jnp.broadcast_to(mass[None], (n_rows, tiles, LANES)), "rows", 0, 0, tiled=True
    )
    full_mass = jnp.sum(masses, axis=0).reshape(cents)
    full_sum = lax.psum(weighted, "rows")
    new_centroids = full_sum / full_mass[:, None]
    return (new_centroids, row_pot.reshape(rows), col_pot.reshape(cents))


def solution(mesh):
    return jax.shard_map(
        per_device,
        mesh=mesh,
        in_specs=(P("rows", None), P("cols", None)),
        out_specs=(P("cols", None), P("rows"), P("cols")),
        check_vma=False,
    )
```

time: 776 us -> 416 us (0.54)
  blocking collectives: 603 us -> 96.6 us
  Pallas kernels: 0 us -> 159 us
  waiting for transfers between devices: 77.5 us -> 138 us
  other arithmetic: 62.9 us -> 3.86 us
  matrix products: 15.7 us -> 0 us
    psum x8 -> x0, blocking collectives: 333 us -> none  [the longest x3 209 us: centroid_lse(): total = lax.psum(jnp.sum(jnp.exp(z - top[None, :]), axis=0), 'rows')]
    pmax x7 -> x0, blocking collectives: 270 us -> none  [the longest x3 221 us: centroid_lse(): top = lax.pmax(local_top, 'rows')]
    pallas_call x0 -> x8, Pallas kernels: none -> 159 us  [the longest x3 101 us: per_device(): pl.pallas_call(functools.partial(row_kernel, log_target), out_shape=row_p...]
    all_to_all x0 -> x8, blocking collectives: none -> 96.6 us  [the longest x3 49.3 us: per_device(): col_got = lax.all_to_all(part, 'rows', 0, 0, tiled=True)]
    psum x1, waiting for transfers between devices: 77.4 us -> 138 us  [per_device(): full_sum = lax.psum(weighted, 'rows')]
    reduce_sum x8 -> x1, other arithmetic: 34.9 us -> 0.04 us  [per_device(): full_mass = jnp.sum(masses, axis=0).reshape(cents)]
    reduce_max x6 -> x0, other arithmetic: 24 us -> none  [the longest x3 12 us: centroid_lse(): local_top = jnp.max(z, axis=0)]
    dot_general x2 -> x0, matrix products: 15.7 us -> none  [the longest x1 8.68 us: per_device(): lax.dot_general(plan_b, vectors, (((0,), (0,)), ((), ())), preferred_elem...]
  transfers between devices with their start and end apart: 1 -> 1, of which waited for: 1 -> 1; matrix products, arithmetic and copies ran while one was open for 1% -> 0% of each run, Pallas kernels for 0% -> 0%
where the time goes in v1:
time: 416 us; the launch traced here: 415 us
  Pallas kernels  159 us (38%)
  waiting for transfers between devices  138 us (33%)
  blocking collectives  96.6 us (23%)
  between operations  14.1 us (3%)
    psum x1, waiting for transfers between devices, per_device(): full_sum = lax.psum(weighted, 'rows')  138 us
    pallas_call x3, Pallas kernels, per_device(): pl.pallas_call(functools.partial(row_kernel, log_target), out_shape=row_p...  101 us
    all_to_all x3, blocking collectives, per_device(): col_got = lax.all_to_all(part, 'rows', 0, 0, tiled=True)  49.3 us
    all_to_all x4, blocking collectives, per_device(): row_got = lax.all_to_all(part, 'cols', 0, 0, tiled=True)  32.9 us
    pallas_call x3, Pallas kernels, per_device(): pl.pallas_call(col_kernel, out_shape=col_parts, in_specs=[vmem(), smem(),...  22.6 us
    pallas_call x1, Pallas kernels, per_device(): pl.pallas_call(logits_kernel, out_shape=(kept, ok_type, row_parts), in_sp...  21.6 us
    all_to_all x1, blocking collectives, per_device(): lax.all_to_all(jnp.broadcast_to(mass[None], (n_rows, tiles, LANES)), 'row...  14.4 us
    pallas_call x1, Pallas kernels, per_device(): pl.pallas_call(functools.partial(final_kernel, log_target), out_shape=(ja...  13.5 us
  transfers between devices with their start and end apart: 1, of which 1 were waited for; matrix products, arithmetic and copies ran while one was open for 0% of the time, Pallas kernels for 0%

profile of v1, /device:TPU:8, one launch (start us, length us, event | category | flops | bytes accessed | tf_op | source)
XLA Modules:
  0.0 415.0 jit_solution(11581715845382892902)
XLA Ops:
  7.2 0.0 all-reduce.2.cloned.1.call-start
  7.2 0.0 copy-start
  7.2 1.9 copy-done
  9.1 0.0 copy-start.1
  9.1 1.4 copy-done.1
  10.5 21.6 %logits.1 = (f32[1024,2048]{1,0:T(8,128)}, s32[1,1]{1,0:T(1,128)}, f32[8,16,128]{2,1,0:T(8,128)S(1)}) custom-call(bf16[1024,768]{1,0:T(8,128)(2,1)S(1)} %copy-done.1, bf16[2048,768]{1,0:T(8,128)(2,1)S(1)} %copy-done), custom_call_target="tpu_custom_call" | custom-call | tf_op jit(solution)/shard_map/logits/pallas_call | solution.py:267
  32.1 8.9 %all_to_all.40.got_ref = f32[8,16,128]{2,1,0:T(8,128)S(1)} all-to-all(f32[8,16,128]{2,1,0:T(8,128)S(1)} %get-tuple-element.10), channel_id=1, replica_groups=mesh['rows'=32,'cols'=8] {'cols'}, dimensions={0} | all-to-all | bytes 131072 | tf_op jit(solution)/shard_map/all_to_all | solution.py:278
  41.0 7.5 %col_step.3 = f32[32,8,128]{2,1,0:T(8,128)S(1)} custom-call(f32[8,16,128]{2,1,0:T(8,128)S(1)} %all_to_all.40.got_ref, s32[1,1]{1,0:T(1,128)} %get-tuple-element.11.ok_ref, f32[1024,2048]{1,0:T(8,128)} %get-tuple-element.12.k_ref), custom_call_target="tpu_custom_call" | custom-call | tf_op jit(solution)/shard_map/col_step/pallas_call | solution.py:279
  48.5 21.4 %all_to_all.41.got_ref = f32[32,8,128]{2,1,0:T(8,128)S(1)} all-to-all(f32[32,8,128]{2,1,0:T(8,128)S(1)} %col_step.3), channel_id=1, replica_groups=mesh['rows'=32,'cols'=8] {'rows'}, dimensions={0} | all-to-all | bytes 262144 | tf_op jit(solution)/shard_map/all_to_all | solution.py:288
  69.9 33.6 %row_step.3 = f32[8,16,128]{2,1,0:T(8,128)S(1)} custom-call(f32[32,8,128]{2,1,0:T(8,128)S(1)} %all_to_all.41.got_ref, s32[1,1]{1,0:T(1,128)} %get-tuple-element.11.ok_ref, f32[1024,2048]{1,0:T(8,128)} %get-tuple-element.12.k_ref), custom_call_target="tpu_custom_call" | custom-call | tf_op jit(solution)/shard_map/row_step/pallas_call | solution.py:289
  103.6 8.0 %all_to_all.42.got_ref = f32[8,16,128]{2,1,0:T(8,128)S(1)} all-to-all(f32[8,16,128]{2,1,0:T(8,128)S(1)} %row_step.3), channel_id=1, replica_groups=mesh['rows'=32,'cols'=8] {'cols'}, dimensions={0} | all-to-all | bytes 131072 | tf_op jit(solution)/shard_map/all_to_all | solution.py:278
  111.6 7.5 %col_step.4 = f32[32,8,128]{2,1,0:T(8,128)S(1)} custom-call(f32[8,16,128]{2,1,0:T(8,128)S(1)} %all_to_all.42.got_ref, s32[1,1]{1,0:T(1,128)} %get-tuple-element.11.ok_ref, f32[1024,2048]{1,0:T(8,128)} %get-tuple-element.12.k_ref), custom_call_target="tpu_custom_call" | custom-call | tf_op jit(solution)/shard_map/col_step/pallas_call | solution.py:279
  119.1 13.9 %all_to_all.43.got_ref = f32[32,8,128]{2,1,0:T(8,128)S(1)} all-to-all(f32[32,8,128]{2,1,0:T(8,128)S(1)} %col_step.4), channel_id=1, replica_groups=mesh['rows'=32,'cols'=8] {'rows'}, dimensions={0} | all-to-all | bytes 262144 | tf_op jit(solution)/shard_map/all_to_all | solution.py:288
  133.0 33.6 %row_step.4 = f32[8,16,128]{2,1,0:T(8,128)S(1)} custom-call(f32[32,8,128]{2,1,0:T(8,128)S(1)} %all_to_all.43.got_ref, s32[1,1]{1,0:T(1,128)} %get-tuple-element.11.ok_ref, f32[1024,2048]{1,0:T(8,128)} %get-tuple-element.12.k_ref), custom_call_target="tpu_custom_call" | custom-call | tf_op jit(solution)/shard_map/row_step/pallas_call | solution.py:289
  166.6 8.0 %all_to_all.44.got_ref = f32[8,16,128]{2,1,0:T(8,128)S(1)} all-to-all(f32[8,16,128]{2,1,0:T(8,128)S(1)} %row_step.4), channel_id=1, replica_groups=mesh['rows'=32,'cols'=8] {'cols'}, dimensions={0} | all-to-all | bytes 131072 | tf_op jit(solution)/shard_map/all_to_all | solution.py:278
  174.6 7.5 %col_step.5 = f32[32,8,128]{2,1,0:T(8,128)S(1)} custom-call(f32[8,16,128]{2,1,0:T(8,128)S(1)} %all_to_all.44.got_ref, s32[1,1]{1,0:T(1,128)} %get-tuple-element.11.ok_ref, f32[1024,2048]{1,0:T(8,128)} %get-tuple-element.12.k_ref), custom_call_target="tpu_custom_call" | custom-call | tf_op jit(solution)/shard_map/col_step/pallas_call | solution.py:279
  182.1 14.0 %all_to_all.45.got_ref.cols_ref = f32[32,8,128]{2,1,0:T(8,128)S(1)} all-to-all(f32[32,8,128]{2,1,0:T(8,128)S(1)} %col_step.5), channel_id=1, replica_groups=mesh['rows'=32,'cols'=8] {'rows'}, dimensions={0} | all-to-all | bytes 262144 | tf_op jit(solution)/shard_map/all_to_all | solution.py:288
  196.2 33.6 %row_step.5 = f32[8,16,128]{2,1,0:T(8,128)S(1)} custom-call(f32[32,8,128]{2,1,0:T(8,128)S(1)} %all_to_all.45.got_ref.cols_ref, s32[1,1]{1,0:T(1,128)} %get-tuple-element.11.ok_ref, f32[1024,2048]{1,0:T(8,128)} %get-tuple-element.12.k_ref), custom_call_target="tpu_custom_call" | custom-call | tf_op jit(solution)/shard_map/row_step/pallas_call | solution.py:289
  229.8 8.0 %all_to_all.46.rows_ref = f32[8,16,128]{2,1,0:T(8,128)S(1)} all-to-all(f32[8,16,128]{2,1,0:T(8,128)S(1)} %row_step.5), channel_id=1, replica_groups=mesh['rows'=32,'cols'=8] {'cols'}, dimensions={0} | all-to-all | bytes 131072 | tf_op jit(solution)/shard_map/all_to_all | solution.py:298
  237.8 13.5 %weighted_sums.1 = (f32[1024,768]{1,0:T(8,128)}, f32[8,128]{1,0:T(8,128)S(1)}, f32[16,128]{1,0:T(8,128)}, f32[8,128]{1,0:T(8,128)}) custom-call(f32[32,8,128]{2,1,0:T(8,128)S(1)} %all_to_all.45.got_ref.cols_ref, f32[8,16,128]{2,1,0:T(8,128)S(1)} %all_to_all.46.rows_ref, s32[1,1]{1,0:T(1,128)} %get-tuple-element.11.ok_ref, ...), custom_call_target="tpu_custom_call" | custom-call | tf_op jit(solution)/shard_map/weighted_sums/pallas_call | solution.py:300
  251.4 0.0 all-reduce.2.cloned.1.call-update
  251.4 14.4 %all_to_all.47 = f32[32,8,128]{2,1,0:T(8,128)S(1)} all-to-all(f32[32,8,128]{2,1,0:T(8,128)S(1)} %broadcast_in_dim.2), channel_id=1, replica_groups=mesh['rows'=32,'cols'=8] {'rows'}, dimensions={0} | all-to-all | bytes 262144 | tf_op jit(solution)/shard_map/all_to_all | solution.py:315
  265.9 138.4 %all-reduce.2.cloned.1.call-done = f32[1024,768]{1,0:T(8,128)} async-done(((f32[1024,768]{1,0:T(8,128)}), f32[1024,768]{1,0:T(8,128)}) %all-reduce.2.cloned.1.call-update) | async-done | bytes 3145744 | tf_op jit(solution)/shard_map/psum | solution.py:319
  404.3 3.8 broadcast_divide_fusion
  (2 shorter events, 0.0 us)
Async XLA Ops:
  7.2 397.1 %all-reduce.2.cloned.1.call-start = ((), (), s32[]{:S(2)}) async-start(), calls=%async_computation.8 | async-start | bytes 6291456 | tf_op jit(solution)/shard_map/psum | solution.py:319
  7.2 1.9 copy-start
  9.1 1.4 copy-start.1
Sparse Core Ops, SparseCore 0:
  251.5 152.7 all-reduce.1

commit v2 on v1

--- a/solution.py
+++ b/solution.py
@@ -11,8 +11,12 @@
 ITERS = 3
 LANES = 128
 LIM = 40.0
-VMEM_LIMIT = 48 * 1024 * 1024
+VMEM_LIMIT = 32 * 1024 * 1024
 F32 = jnp.float32
+XS, ZS = 4, 8
+BLOCK = 32
+PARTS = BLOCK // 8
+XB1, XB2, ZB1, ZB2 = range(4)
 
 
 def combine_lse(parts):
@@ -184,9 +188,9 @@
     put_copies(out_ref, lse_ref[...])
 
 
-def final_kernel(
-    log_target, cols_ref, rows_ref, ok_ref, k_ref, vec_ref,
-    weighted_ref, mass_ref, row_pot_ref, col_pot_ref, scale_ref, plan_ref,
+def plan_kernel(
+    log_target, bits_ref, cols_ref, rows_ref, ok_ref, k_ref, vec_ref,
+    send_a_ref, send_b_ref, plan_ref, mass_ref, row_pot_ref, col_pot_ref, scale_ref,
 ):
     tiles, groups = k_ref.shape[0] // LANES, k_ref.shape[1] // LANES
     col_pot = log_target - combine_lse(cols_ref[...])
@@ -204,7 +208,14 @@
             plan = block(g)
             total = total + plan
             plan_ref[row_tile(t), lane_group(g)] = plan.astype(jnp.bfloat16)
-        mass_ref[pl.ds(t, 1), :] = jnp.sum(jnp.transpose(total), axis=0, keepdims=True)
+        mass = jnp.broadcast_to(jnp.sum(total, axis=1, keepdims=True), (LANES, LANES))
+        spot = lax.broadcasted_iota(jnp.int32, (8, LANES), 1) // (LANES // PARTS)
+        for b in range(LANES // BLOCK):
+            unit = mass[b * BLOCK : b * BLOCK + 8, :]
+            for k in range(1, PARTS):
+                at = b * BLOCK + 8 * k
+                unit = jnp.where(spot == k, mass[at : at + 8, :], unit)
+            mass_ref[t * (LANES // BLOCK) + b] = unit
 
     @pl.when(fast)
     def _():
@@ -233,10 +244,193 @@
 
         lax.fori_loop(0, tiles, tile, 0)
 
-    step = 256
-    for t in range(k_ref.shape[0] // step):
-        at = slice(t * step, (t + 1) * step)
-        weighted_ref[at, :] = jnp.dot(plan_ref[at, :], vec_ref[...], preferred_element_type=F32)
+    half_sums(1 - bits_ref[XB1], 1 - bits_ref[ZB1], plan_ref, mass_ref, vec_ref, send_a_ref, send_b_ref)
+
+
+def keep_kernel(bits_ref, plan_ref, mass_ref, vec_ref, keep_a_ref, keep_b_ref):
+    half_sums(bits_ref[XB1], bits_ref[ZB1], plan_ref, mass_ref, vec_ref, keep_a_ref, keep_b_ref)
+
+
+def half_sums(half_a, half_b, plan_ref, mass_ref, vec_ref, a_ref, b_ref):
+    blocks = a_ref.shape[0]
+    size = blocks * BLOCK
+    for chain, (half, out_ref) in enumerate(((half_a, a_ref), (half_b, b_ref))):
+        first = chain * 2 * blocks + half * blocks
+        at = pl.ds(pl.multiple_of(first * BLOCK, size), size)
+        sums = jnp.dot(plan_ref[at, :], vec_ref[...], preferred_element_type=F32)
+        for b in range(blocks):
+            for k in range(PARTS):
+                row = b * BLOCK + 8 * k
+                for g in range(sums.shape[1] // LANES):
+                    out_ref[b, k * (sums.shape[1] // LANES) + g] = sums[row : row + 8, lane_group(g)]
+            out_ref[b, out_ref.shape[1] - 1] = mass_ref[first + b]
+
+
+def fold_kernel(which, bits_ref, keep_ref, got_ref, send_ref, kept_ref):
+    half = send_ref.shape[0]
+    mine = bits_ref[which] * half
+    other = (1 - bits_ref[which]) * half
+    for b in range(half):
+        send_ref[b] = keep_ref[other + b] + got_ref[other + b]
+        kept_ref[b] = keep_ref[mine + b] + got_ref[mine + b]
+
+
+def pair_kernel(keep_a_ref, got_a_ref, keep_b_ref, got_b_ref, out_ref):
+    out_ref[0] = keep_a_ref[0] + got_a_ref[0]
+    out_ref[1] = keep_b_ref[0] + got_b_ref[0]
+
+
+def mean_kernel(sum_ref, got_ref, a_ref, b_ref):
+    units = a_ref.shape[1]
+    width = LANES // PARTS
+    for chain, out_ref in enumerate((a_ref, b_ref)):
+        mass = sum_ref[chain, units] + got_ref[chain, units]
+        for k in range(PARTS):
+            part = jnp.broadcast_to(mass[:, k * width : k * width + 1], (8, LANES))
+            for g in range(units // PARTS):
+                u = k * (units // PARTS) + g
+                out_ref[0, u] = (sum_ref[chain, u] + got_ref[chain, u]) / part
+
+
+def join_kernel(which, bits_ref, mine_ref, got_ref, out_ref):
+    half = mine_ref.shape[0]
+    mine = bits_ref[which] * half
+    other = (1 - bits_ref[which]) * half
+    for b in range(half):
+        out_ref[mine + b] = mine_ref[b]
+        out_ref[other + b] = got_ref[b]
+
+
+def output_kernel(bits_ref, mine_a_ref, got_a_ref, mine_b_ref, got_b_ref, out_ref):
+    half, units = mine_a_ref.shape[:2]
+    across = units // PARTS
+    for chain, (mine_ref, got_ref, bit) in enumerate(
+        ((mine_a_ref, got_a_ref, bits_ref[XB1]), (mine_b_ref, got_b_ref, bits_ref[ZB1]))
+    ):
+        for side, part_ref in ((bit, mine_ref), (1 - bit, got_ref)):
+            for b in range(half):
+                first = (chain * 2 * half + side * half + b) * BLOCK
+                for k in range(PARTS):
+                    at = pl.ds(pl.multiple_of(first + 8 * k, 8), 8)
+                    for g in range(across):
+                        out_ref[at, lane_group(g)] = part_ref[b, k * across + g]
+
+
+def place(row, core):
+    return (row // ZS + (XS - 1) * core) % XS, (row % ZS + (ZS - 1) * core) % ZS
+
+
+def pairs(partner, n_cols):
+    out = []
+    for row in range(XS * ZS):
+        for col in range(n_cols):
+            core = col % 2
+            x, z = partner(*place(row, core))
+            to = (x + core) % XS * ZS + (z + core) % ZS
+            out.append((row * n_cols + col, to * n_cols + col))
+    return out
+
+
+def exchange(x, partner):
+    return lax.ppermute(x, ("rows", "cols"), pairs(partner, lax.axis_size("cols")))
+
+
+def x_first(x, z):
+    return x ^ 1, z
+
+
+def x_second(x, z):
+    return XS - 1 - x, z
+
+
+def z_first(x, z):
+    return x, z ^ 1
+
+
+def z_second(x, z):
+    return x, (z - 1 + 2 * (z % 2)) % ZS
+
+
+def z_third(x, z):
+    return x, {0: 3, 3: 0, 1: 6, 6: 1, 2: 5, 5: 2, 4: 7, 7: 4}[z]
+
+
+def position_bits():
+    x, z = place(lax.axis_index("rows"), lax.axis_index("cols") % 2)
+    return jnp.stack([(x ^ (x >> 1)) & 1, x >> 1, ((z + 1) >> 1) & 1, (0xB4 >> z) & 1]).astype(jnp.int32)
+
+
+def halve(which, bits, keep, got):
+    half = jax.ShapeDtypeStruct((keep.shape[0] // 2, *keep.shape[1:]), F32)
+    return pl.pallas_call(
+        functools.partial(fold_kernel, which),
+        out_shape=(half, half),
+        in_specs=[smem(), vmem(), vmem()],
+        out_specs=(vmem(), vmem()),
+        compiler_params=params(),
+        name="fold",
+    )(bits, keep, got)
+
+
+def join(which, bits, mine, got):
+    return pl.pallas_call(
+        functools.partial(join_kernel, which),
+        out_shape=jax.ShapeDtypeStruct((2 * mine.shape[0], *mine.shape[1:]), F32),
+        in_specs=[smem(), vmem(), vmem()],
+        out_specs=vmem(),
+        compiler_params=params(),
+        name="join",
+    )(bits, mine, got)
+
+
+def mean_over_rows(bits, send_a, keep_a, send_b, keep_b, cents, width):
+    got_a, got_b = exchange(send_a, x_first), exchange(send_b, z_first)
+    send_a, keep_a = halve(XB2, bits, keep_a, got_a)
+    send_b, keep_b = halve(ZB2, bits, keep_b, got_b)
+    got_a, got_b = exchange(send_a, x_second), exchange(send_b, z_second)
+    send_a, keep_a = halve(ZB1, bits, keep_a, got_a)
+    send_b, keep_b = halve(XB1, bits, keep_b, got_b)
+    got_a, got_b = exchange(send_a, z_first), exchange(send_b, x_first)
+    send_a, keep_a = halve(ZB2, bits, keep_a, got_a)
+    send_b, keep_b = halve(XB2, bits, keep_b, got_b)
+    got_a, got_b = exchange(send_a, z_second), exchange(send_b, x_second)
+    block = keep_a.shape[1:]
+    sums = pl.pallas_call(
+        pair_kernel,
+        out_shape=jax.ShapeDtypeStruct((2, *block), F32),
+        in_specs=[vmem()] * 4,
+        out_specs=vmem(),
+        compiler_params=params(),
+        name="pair",
+    )(keep_a, got_a, keep_b, got_b)
+    got = exchange(sums, z_third)
+    one = jax.ShapeDtypeStruct((1, block[0] - 1, *block[1:]), F32)
+    mine_a, mine_b = pl.pallas_call(
+        mean_kernel,
+        out_shape=(one, one),
+        in_specs=[vmem()] * 2,
+        out_specs=(vmem(), vmem()),
+        compiler_params=params(),
+        name="mean",
+    )(sums, got)
+    got_a, got_b = exchange(mine_a, z_second), exchange(mine_b, x_second)
+    mine_a = join(ZB2, bits, mine_a, got_a)
+    mine_b = join(XB2, bits, mine_b, got_b)
+    got_a, got_b = exchange(mine_a, z_first), exchange(mine_b, x_first)
+    mine_a = join(ZB1, bits, mine_a, got_a)
+    mine_b = join(XB1, bits, mine_b, got_b)
+    got_a, got_b = exchange(mine_a, x_second), exchange(mine_b, z_second)
+    mine_a = join(XB2, bits, mine_a, got_a)
+    mine_b = join(ZB2, bits, mine_b, got_b)
+    got_a, got_b = exchange(mine_a, x_first), exchange(mine_b, z_first)
+    return pl.pallas_call(
+        output_kernel,
+        out_shape=jax.ShapeDtypeStruct((cents, width), F32),
+        in_specs=[smem()] + [vmem()] * 4,
+        out_specs=vmem(),
+        compiler_params=params(),
+        name="output",
+    )(bits, mine_a, got_a, mine_b, got_b)
 
 
 def vmem():
@@ -263,6 +457,8 @@
     col_parts = jax.ShapeDtypeStruct((n_rows, tiles, LANES), F32)
     row_scratch = pltpu.VMEM((groups, LANES), F32)
     col_scratch = pltpu.VMEM((tiles, LANES), F32)
+
+    bits = position_bits()
 
     kernel, ok, part = pl.pallas_call(
         logits_kernel,
@@ -297,27 +493,34 @@
         )(col_got, ok, kernel)
     row_got = lax.all_to_all(part, "cols", 0, 0, tiled=True)
 
-    weighted, mass, row_pot, col_pot = pl.pallas_call(
-        functools.partial(final_kernel, log_target),
+    part_units = PARTS * (width // LANES) + 1
+    halves = jax.ShapeDtypeStruct((cents // BLOCK // 4, part_units, 8, LANES), F32)
+    send_a, send_b, plan, mass, row_pot, col_pot = pl.pallas_call(
+        functools.partial(plan_kernel, log_target),
         out_shape=(
-            jax.ShapeDtypeStruct((cents, width), F32),
-            jax.ShapeDtypeStruct((tiles, LANES), F32),
+            halves,
+            halves,
+            jax.ShapeDtypeStruct((cents, rows), jnp.bfloat16),
+            jax.ShapeDtypeStruct((cents // BLOCK, 8, LANES), F32),
             jax.ShapeDtypeStruct((groups, LANES), F32),
             jax.ShapeDtypeStruct((tiles, LANES), F32),
         ),
-        in_specs=[vmem(), vmem(), smem(), vmem(), vmem()],
-        out_specs=(vmem(), vmem(), vmem(), vmem()),
-        scratch_shapes=[col_scratch, pltpu.VMEM((cents, rows), jnp.bfloat16)],
-        compiler_params=params(),
-        name="weighted_sums",
-    )(col_got, row_got, ok, kernel, vectors)
-
-    masses = lax.all_to_all(
-        jnp.broadcast_to(mass[None], (n_rows, tiles, LANES)), "rows", 0, 0, tiled=True
-    )
-    full_mass = jnp.sum(masses, axis=0).reshape(cents)
-    full_sum = lax.psum(weighted, "rows")
-    new_centroids = full_sum / full_mass[:, None]
+        in_specs=[smem(), vmem(), vmem(), smem(), vmem(), vmem()],
+        out_specs=(vmem(),) * 6,
+        scratch_shapes=[col_scratch],
+        compiler_params=params(),
+        name="plan",
+    )(bits, col_got, row_got, ok, kernel, vectors)
+    keep_a, keep_b = pl.pallas_call(
+        keep_kernel,
+        out_shape=(halves, halves),
+        in_specs=[smem(), vmem(), vmem(), vmem()],
+        out_specs=(vmem(), vmem()),
+        compiler_params=params(),
+        cost_estimate=pl.CostEstimate(flops=rows * cents * width, bytes_accessed=8 << 20, transcendentals=0),
+        name="keep",
+    )(bits, plan, mass, vectors)
+    new_centroids = mean_over_rows(bits, send_a, keep_a, send_b, keep_b, cents, width)
     return (new_centroids, row_pot.reshape(rows), col_pot.reshape(cents))
 
 

time: 416 us -> 320 us (0.77)
  waiting for transfers between devices: 138 us -> 64.6 us
  starting transfers between devices: 0.04 us -> 38.8 us
  blocking collectives: 96.6 us -> 60.1 us
  Pallas kernels: 159 us -> 142 us
  between operations: 14.1 us -> 0.89 us
  local copies, waits for them, and re-layouts: 3.3 us -> 10.1 us
    psum x1 -> x0, waiting for transfers between devices: 138 us -> none  [per_device(): full_sum = lax.psum(weighted, 'rows')]
    ppermute x0 -> x17, waiting for transfers between devices: none -> 50.2 us  [exchange(): lax.ppermute(x, ('rows', 'cols'), pairs(partner, lax.axis_size('cols')))]
    ppermute x0 -> x17, starting transfers between devices: none -> 30.1 us  [exchange(): lax.ppermute(x, ('rows', 'cols'), pairs(partner, lax.axis_size('cols')))]
    all_to_all x0 -> x2, waiting for transfers between devices: none -> 14.4 us  [the longest x1 10.3 us: per_device(): col_got = lax.all_to_all(part, 'rows', 0, 0, tiled=True)]
    all_to_all x1 -> x0, blocking collectives: 14.4 us -> none  [per_device(): lax.all_to_all(jnp.broadcast_to(mass[None], (n_rows, tiles, LANES)), 'row...]
    all_to_all x3 -> x2, blocking collectives: 49.3 us -> 35.2 us  [per_device(): col_got = lax.all_to_all(part, 'rows', 0, 0, tiled=True)]
    pallas_call x3, Pallas kernels: 22.6 us -> 13.1 us  [per_device(): pl.pallas_call(col_kernel, out_shape=col_parts, in_specs=[vmem(), smem(),...]
    pallas_call x3, Pallas kernels: 101 us -> 91.5 us  [per_device(): pl.pallas_call(functools.partial(row_kernel, log_target), out_shape=row_p...]
  transfers between devices with their start and end apart: 1 -> 19, of which waited for: 1 -> 15; matrix products, arithmetic and copies ran while one was open for 0% -> 0% of each run, Pallas kernels for 0% -> 3%
where the time goes in v2:
time: 320 us; the launch traced here: 317 us
  Pallas kernels  142 us (44%)
  waiting for transfers between devices  64.6 us (20%)
  blocking collectives  60.1 us (19%)
  starting transfers between devices  38.8 us (12%)
  local copies, waits for them, and re-layouts  10.1 us (3%)
    pallas_call x3, Pallas kernels, per_device(): pl.pallas_call(functools.partial(row_kernel, log_target), out_shape=row_p...  91.5 us
    ppermute x17, waiting for transfers between devices, exchange(): lax.ppermute(x, ('rows', 'cols'), pairs(partner, lax.axis_size('cols')))  50.2 us
    all_to_all x2, blocking collectives, per_device(): col_got = lax.all_to_all(part, 'rows', 0, 0, tiled=True)  35.2 us
    ppermute x17, starting transfers between devices, exchange(): lax.ppermute(x, ('rows', 'cols'), pairs(partner, lax.axis_size('cols')))  30.1 us
    all_to_all x3, blocking collectives, per_device(): row_got = lax.all_to_all(part, 'cols', 0, 0, tiled=True)  24.9 us
    pallas_call x1, Pallas kernels, per_device(): pl.pallas_call(logits_kernel, out_shape=(kept, ok_type, row_parts), in_sp...  18.9 us
    pallas_call x3, Pallas kernels, per_device(): pl.pallas_call(col_kernel, out_shape=col_parts, in_specs=[vmem(), smem(),...  13.1 us
    all_to_all x1, waiting for transfers between devices, per_device(): col_got = lax.all_to_all(part, 'rows', 0, 0, tiled=True)  10.3 us
  transfers between devices with their start and end apart: 19, of which 15 were waited for; matrix products, arithmetic and copies ran while one was open for 0% of the time, Pallas kernels for 3%

profile of v2, /device:TPU:8, one launch (start us, length us, event | category | flops | bytes accessed | tf_op | source)
XLA Modules:
  0.0 316.9 jit_solution(691851930262556128)
XLA Ops:
  0.6 1.9 copy-done.3
  2.5 1.4 copy-done.5
  3.9 18.9 %logits.1 = (f32[1024,2048]{1,0:T(8,128)S(1)}, s32[1,1]{1,0:T(1,128)}, f32[8,16,128]{2,1,0:T(8,128)S(1)}) custom-call(bf16[1024,768]{1,0:T(8,128)(2,1)S(1)} %copy-done.5, bf16[2048,768]{1,0:T(8,128)(2,1)S(1)} %copy-done.3), custom_call_target="tpu_custom_call" | custom-call | tf_op jit(solution)/shard_map/logits/pallas_call | solution.py:463
  22.8 8.9 %all_to_all.35.got_ref = f32[8,16,128]{2,1,0:T(8,128)S(1)} all-to-all(f32[8,16,128]{2,1,0:T(8,128)S(1)} %get-tuple-element.28), channel_id=1, replica_groups=mesh['rows'=32,'cols'=8] {'cols'}, dimensions={0} | all-to-all | bytes 131072 | tf_op jit(solution)/shard_map/all_to_all | solution.py:474
  31.7 4.1 %col_step.3 = f32[32,8,128]{2,1,0:T(8,128)S(1)} custom-call(f32[8,16,128]{2,1,0:T(8,128)S(1)} %all_to_all.35.got_ref, s32[1,1]{1,0:T(1,128)} %get-tuple-element.29.ok_ref, f32[1024,2048]{1,0:T(8,128)S(1)} %get-tuple-element.30.k_ref), custom_call_target="tpu_custom_call" | custom-call | tf_op jit(solution)/shard_map/col_step/pallas_call | solution.py:475
  35.8 21.4 %all_to_all.36.got_ref = f32[32,8,128]{2,1,0:T(8,128)S(1)} all-to-all(f32[32,8,128]{2,1,0:T(8,128)S(1)} %col_step.3), channel_id=1, replica_groups=mesh['rows'=32,'cols'=8] {'rows'}, dimensions={0} | all-to-all | bytes 262144 | tf_op jit(solution)/shard_map/all_to_all | solution.py:484
  57.2 30.2 %row_step.3 = f32[8,16,128]{2,1,0:T(8,128)S(1)} custom-call(f32[32,8,128]{2,1,0:T(8,128)S(1)} %all_to_all.36.got_ref, s32[1,1]{1,0:T(1,128)} %get-tuple-element.29.ok_ref, f32[1024,2048]{1,0:T(8,128)S(1)} %get-tuple-element.30.k_ref), custom_call_target="tpu_custom_call" | custom-call | tf_op jit(solution)/shard_map/row_step/pallas_call | solution.py:485
  87.5 8.0 %all_to_all.37.got_ref = f32[8,16,128]{2,1,0:T(8,128)S(1)} all-to-all(f32[8,16,128]{2,1,0:T(8,128)S(1)} %row_step.3), channel_id=1, replica_groups=mesh['rows'=32,'cols'=8] {'cols'}, dimensions={0} | all-to-all | bytes 131072 | tf_op jit(solution)/shard_map/all_to_all | solution.py:474
  95.5 4.1 %col_step.4 = f32[32,8,128]{2,1,0:T(8,128)S(1)} custom-call(f32[8,16,128]{2,1,0:T(8,128)S(1)} %all_to_all.37.got_ref, s32[1,1]{1,0:T(1,128)} %get-tuple-element.29.ok_ref, f32[1024,2048]{1,0:T(8,128)S(1)} %get-tuple-element.30.k_ref), custom_call_target="tpu_custom_call" | custom-call | tf_op jit(solution)/shard_map/col_step/pallas_call | solution.py:475
  99.6 13.9 %all_to_all.38.got_ref = f32[32,8,128]{2,1,0:T(8,128)S(1)} all-to-all(f32[32,8,128]{2,1,0:T(8,128)S(1)} %col_step.4), channel_id=1, replica_groups=mesh['rows'=32,'cols'=8] {'rows'}, dimensions={0} | all-to-all | bytes 262144 | tf_op jit(solution)/shard_map/all_to_all | solution.py:484
  113.5 30.2 %row_step.4 = f32[8,16,128]{2,1,0:T(8,128)S(1)} custom-call(f32[32,8,128]{2,1,0:T(8,128)S(1)} %all_to_all.38.got_ref, s32[1,1]{1,0:T(1,128)} %get-tuple-element.29.ok_ref, f32[1024,2048]{1,0:T(8,128)S(1)} %get-tuple-element.30.k_ref), custom_call_target="tpu_custom_call" | custom-call | tf_op jit(solution)/shard_map/row_step/pallas_call | solution.py:485
  143.7 8.0 %all_to_all.39.got_ref = f32[8,16,128]{2,1,0:T(8,128)S(1)} all-to-all(f32[8,16,128]{2,1,0:T(8,128)S(1)} %row_step.4), channel_id=1, replica_groups=mesh['rows'=32,'cols'=8] {'cols'}, dimensions={0} | all-to-all | bytes 131072 | tf_op jit(solution)/shard_map/all_to_all | solution.py:474
  151.7 4.8 %col_step.5 = f32[32,8,128]{2,1,0:T(8,128)} custom-call(f32[8,16,128]{2,1,0:T(8,128)S(1)} %all_to_all.39.got_ref, s32[1,1]{1,0:T(1,128)} %get-tuple-element.29.ok_ref, f32[1024,2048]{1,0:T(8,128)S(1)} %get-tuple-element.30.k_ref), custom_call_target="tpu_custom_call" | custom-call | tf_op jit(solution)/shard_map/col_step/pallas_call | solution.py:475
  156.5 4.0 %all-to-all-start.5 = ((f32[32,8,128]{2,1,0:T(8,128)}), f32[32,8,128]{2,1,0:T(8,128)S(1)}, u32[]{:S(2)}, u32[]{:S(2)}) async-start(f32[32,8,128]{2,1,0:T(8,128)} %col_step.5), calls=%async_computation.5 | async-start | bytes 262144 | tf_op jit(solution)/shard_map/all_to_all | solution.py:484
  160.6 10.3 %all-to-all-done.5.got_ref.cols_ref = f32[32,8,128]{2,1,0:T(8,128)S(1)} async-done(((f32[32,8,128]{2,1,0:T(8,128)}), f32[32,8,128]{2,1,0:T(8,128)S(1)}, u32[]{:S(2)}, u32[]{:S(2)}) %all-to-all-start.5) | async-done | bytes 131104 | tf_op jit(solution)/shard_map/all_to_all | solution.py:484
  170.9 3.4 %copy-done.1 = f32[1024,2048]{1,0:T(8,128)S(1)} copy-done((f32[1024,2048]{1,0:T(8,128)S(1)}, f32[1024,2048]{1,0:T(8,128)}, u32[]{:S(2)}) %copy-start.1) | copy-done | bytes 8388632
  174.3 31.0 %row_step.5 = f32[8,16,128]{2,1,0:T(8,128)} custom-call(f32[32,8,128]{2,1,0:T(8,128)S(1)} %all-to-all-done.5.got_ref.cols_ref, s32[1,1]{1,0:T(1,128)} %get-tuple-element.29.ok_ref, f32[1024,2048]{1,0:T(8,128)S(1)} %copy-done.1), custom_call_target="tpu_custom_call" | custom-call | tf_op jit(solution)/shard_map/row_step/pallas_call | solution.py:485
  205.3 4.7 %all-to-all-start.6 = ((f32[8,16,128]{2,1,0:T(8,128)}), f32[8,16,128]{2,1,0:T(8,128)S(1)}, u32[]{:S(2)}, u32[]{:S(2)}) async-start(f32[8,16,128]{2,1,0:T(8,128)} %row_step.5), calls=%async_computation.6 | async-start | bytes 131072 | tf_op jit(solution)/shard_map/all_to_all | solution.py:494
  210.1 4.1 %all-to-all-done.6.rows_ref = f32[8,16,128]{2,1,0:T(8,128)S(1)} async-done(((f32[8,16,128]{2,1,0:T(8,128)}), f32[8,16,128]{2,1,0:T(8,128)S(1)}, u32[]{:S(2)}, u32[]{:S(2)}) %all-to-all-start.6) | async-done | bytes 65568 | tf_op jit(solution)/shard_map/all_to_all | solution.py:494
  214.3 3.4 %copy-done.2 = f32[1024,2048]{1,0:T(8,128)S(1)} copy-done((f32[1024,2048]{1,0:T(8,128)S(1)}, f32[1024,2048]{1,0:T(8,128)}, u32[]{:S(2)}) %copy-start.2) | copy-done | bytes 8388632
  217.6 6.9 %plan.1 = (f32[8,25,8,128]{3,2,1,0:T(8,128)S(1)}, f32[8,25,8,128]{3,2,1,0:T(8,128)S(1)}, bf16[1024,2048]{1,0:T(8,128)(2,1)S(1)}, f32[32,8,128]{2,1,0:T(8,128)S(1)}, f32[16,128]{1,0:T(8,128)}, /*index=5*/f32[8,128]{1,0:T(8,128)}) custom-call(s32[4]{0:T(128)S(1)} %pad_add_fusion.bits_ref, f32[32,8,128]{2,1,0:T(8,128)S(1)} %all-to-all-done.5.got_ref.cols_ref, ...), custom_call_target="tpu_custom_call" | custom-call | tf_op jit(solution)/shard_map/plan/pallas_call | solution.py:498
  224.5 0.6 collective-permute-start
  225.2 1.3 collective-permute-start.4
  226.4 2.4 keep.1
  228.8 8.0 %collective-permute-done.got_ref = f32[8,25,8,128]{3,2,1,0:T(8,128)S(1)} collective-permute-done((f32[8,25,8,128]{3,2,1,0:T(8,128)S(1)}, f32[8,25,8,128]{3,2,1,0:T(8,128)S(1)}, u32[]{:S(2)}, u32[]{:S(2)}) %collective-permute-start) | collective-permute-done | bytes 819232 | tf_op jit(solution)/shard_map/ppermute | solution.py:335
  236.9 0.6 fold.6
  237.5 1.2 collective-permute-start.1
  238.7 0.6 fold.9
  239.4 0.7 collective-permute-start.5
  240.1 6.7 %collective-permute-done.1.got_ref = f32[4,25,8,128]{3,2,1,0:T(8,128)S(1)} collective-permute-done((f32[4,25,8,128]{3,2,1,0:T(8,128)S(1)}, f32[4,25,8,128]{3,2,1,0:T(8,128)S(1)}, u32[]{:S(2)}, u32[]{:S(2)}) %collective-permute-start.1) | collective-permute-done | bytes 409632 | tf_op jit(solution)/shard_map/ppermute | solution.py:335
  246.8 0.6 fold.7
  247.3 1.4 collective-permute-start.2
  248.7 0.6 fold.10
  249.3 0.3 collective-permute-start.6
  249.6 3.6 %collective-permute-done.2.got_ref = f32[2,25,8,128]{3,2,1,0:T(8,128)S(1)} collective-permute-done((f32[2,25,8,128]{3,2,1,0:T(8,128)S(1)}, f32[2,25,8,128]{3,2,1,0:T(8,128)S(1)}, u32[]{:S(2)}, u32[]{:S(2)}) %collective-permute-start.2) | collective-permute-done | bytes 204832 | tf_op jit(solution)/shard_map/ppermute | solution.py:335
  253.2 0.6 fold.8
  253.8 0.4 collective-permute-start.3
  254.2 1.0 collective-permute-done.6.got_ref
  255.2 0.6 fold.11
  255.8 3.1 collective-permute-start.7
  258.8 0.9 collective-permute-done.3.got_a_ref
  259.7 2.0 collective-permute-done.7.got_b_ref
  261.7 1.8 collective-permute-start.8
  263.6 6.0 %collective-permute-done.8.got_ref = f32[2,25,8,128]{3,2,1,0:T(8,128)S(1)} collective-permute-done((f32[2,25,8,128]{3,2,1,0:T(8,128)S(1)}, f32[2,25,8,128]{3,2,1,0:T(8,128)S(1)}, u32[]{:S(2)}, u32[]{:S(2)}) %collective-permute-start.8) | collective-permute-done | bytes 204832 | tf_op jit(solution)/shard_map/ppermute | solution.py:335
  269.7 3.1 collective-permute-start.13
  272.8 3.1 collective-permute-start.9
  275.9 0.7 collective-permute-done.13.got_ref
  276.6 0.6 join.9.mine_ref
  277.1 0.1 collective-permute-start.14
  277.2 2.4 collective-permute-done.9.got_ref
  279.6 0.6 join.6.mine_ref
  280.2 1.4 collective-permute-start.10
  281.6 1.3 collective-permute-done.14.got_ref
  282.9 0.6 join.10.mine_ref
  283.5 4.2 %collective-permute-start.15 = (f32[4,24,8,128]{3,2,1,0:T(8,128)S(1)}, f32[4,24,8,128]{3,2,1,0:T(8,128)S(1)}, u32[]{:S(2)}, u32[]{:S(2)}) collective-permute-start(f32[4,24,8,128]{3,2,1,0:T(8,128)S(1)} %join.10.mine_ref), channel_id=1, source_target_pairs={{0,56},{1,9},{2,58},{3,11},{4,60},{5,13},{6,62},{7,15},{8,16},{9,1... | collective-permute-start | bytes 1179656 | tf_op jit(solution)/shard_map/ppermute | solution.py:335
  287.7 0.6 join.7.mine_ref
  288.2 3.3 %collective-permute-start.11 = (f32[4,24,8,128]{3,2,1,0:T(8,128)S(1)}, f32[4,24,8,128]{3,2,1,0:T(8,128)S(1)}, u32[]{:S(2)}, u32[]{:S(2)}) collective-permute-start(f32[4,24,8,128]{3,2,1,0:T(8,128)S(1)} %join.7.mine_ref), channel_id=1, source_target_pairs={{0,192},{1,65},{2,194},{3,67},{4,196},{5,69},{6,198},{7,71},{8,200... | collective-permute-start | bytes 1179656 | tf_op jit(solution)/shard_map/ppermute | solution.py:335
  291.5 5.6 %collective-permute-done.15.got_ref = f32[4,24,8,128]{3,2,1,0:T(8,128)S(1)} collective-permute-done((f32[4,24,8,128]{3,2,1,0:T(8,128)S(1)}, f32[4,24,8,128]{3,2,1,0:T(8,128)S(1)}, u32[]{:S(2)}, u32[]{:S(2)}) %collective-permute-start.15) | collective-permute-done | bytes 393248 | tf_op jit(solution)/shard_map/ppermute | solution.py:335
  297.1 0.6 join.11.mine_b_ref
  297.7 4.1 %collective-permute-start.16 = (f32[8,24,8,128]{3,2,1,0:T(8,128)S(1)}, f32[8,24,8,128]{3,2,1,0:T(8,128)S(1)}, u32[]{:S(2)}, u32[]{:S(2)}) collective-permute-start(f32[8,24,8,128]{3,2,1,0:T(8,128)S(1)} %join.11.mine_b_ref), channel_id=1, source_target_pairs={{0,8},{1,57},{2,10},{3,59},{4,12},{5,61},{6,14},{7,63},{8,0},{9,17... | collective-permute-start | bytes 2359304 | tf_op jit(solution)/shard_map/ppermute | solution.py:335
  301.7 0.6 join.8.mine_a_ref
  302.4 9.3 %collective-permute-done.16.got_b_ref = f32[8,24,8,128]{3,2,1,0:T(8,128)S(1)} collective-permute-done((f32[8,24,8,128]{3,2,1,0:T(8,128)S(1)}, f32[8,24,8,128]{3,2,1,0:T(8,128)S(1)}, u32[]{:S(2)}, u32[]{:S(2)}) %collective-permute-start.16) | collective-permute-done | bytes 786464 | tf_op jit(solution)/shard_map/ppermute | solution.py:335
  311.7 2.7 collective-permute-done.12.got_a_ref
  314.4 2.5 output.1
  (16 shorter events, 0.3 us)
Async XLA Ops:
  0.6 1.9 copy-start.3
  2.5 1.4 copy-start.5
  22.8 128.9 %copy-start = (f32[1024,2048]{1,0:T(8,128)}, f32[1024,2048]{1,0:T(8,128)S(1)}, u32[]{:S(2)}) copy-start(f32[1024,2048]{1,0:T(8,128)S(1)} %get-tuple-element.30.k_ref) | copy-start | bytes 25165828
  156.5 14.4 %all-to-all-start.5 = ((f32[32,8,128]{2,1,0:T(8,128)}), f32[32,8,128]{2,1,0:T(8,128)S(1)}, u32[]{:S(2)}, u32[]{:S(2)}) async-start(f32[32,8,128]{2,1,0:T(8,128)} %col_step.5), calls=%async_computation.5 | async-start | bytes 262144 | tf_op jit(solution)/shard_map/all_to_all | solution.py:484
  170.9 3.4 %copy-start.1 = (f32[1024,2048]{1,0:T(8,128)S(1)}, f32[1024,2048]{1,0:T(8,128)}, u32[]{:S(2)}) copy-start(f32[1024,2048]{1,0:T(8,128)} %copy-done) | copy-start | bytes 25165828
  174.3 39.9 %copy-start.4 = (bf16[2048,768]{1,0:T(8,128)(2,1)S(1)}, bf16[2048,768]{1,0:T(8,128)(2,1)}, u32[]{:S(2)}) copy-start(bf16[2048,768]{1,0:T(8,128)(2,1)} %vec_ref.5) | copy-start | bytes 9437188
  205.3 8.9 %all-to-all-start.6 = ((f32[8,16,128]{2,1,0:T(8,128)}), f32[8,16,128]{2,1,0:T(8,128)S(1)}, u32[]{:S(2)}, u32[]{:S(2)}) async-start(f32[8,16,128]{2,1,0:T(8,128)} %row_step.5), calls=%async_computation.6 | async-start | bytes 131072 | tf_op jit(solution)/shard_map/all_to_all | solution.py:494
  214.3 3.4 %copy-start.2 = (f32[1024,2048]{1,0:T(8,128)S(1)}, f32[1024,2048]{1,0:T(8,128)}, u32[]{:S(2)}) copy-start(f32[1024,2048]{1,0:T(8,128)} %copy-done) | copy-start | bytes 25165828
  224.5 12.3 %collective-permute-start = (f32[8,25,8,128]{3,2,1,0:T(8,128)S(1)}, f32[8,25,8,128]{3,2,1,0:T(8,128)S(1)}, u32[]{:S(2)}, u32[]{:S(2)}) collective-permute-start(f32[8,25,8,128]{3,2,1,0:T(8,128)S(1)} %get-tuple-element.34), channel_id=1, source_target_pairs={{0,64},{1,193},{2,66},{3,195},{4,68},{5,197},{6,70},{7,199},{8,72}... | collective-permute-start | bytes 2457608 | tf_op jit(solution)/shard_map/ppermute | solution.py:335
  225.2 13.6 %collective-permute-start.4 = (f32[8,25,8,128]{3,2,1,0:T(8,128)S(1)}, f32[8,25,8,128]{3,2,1,0:T(8,128)S(1)}, u32[]{:S(2)}, u32[]{:S(2)}) collective-permute-start(f32[8,25,8,128]{3,2,1,0:T(8,128)S(1)} %get-tuple-element.42), channel_id=1, source_target_pairs={{0,8},{1,57},{2,10},{3,59},{4,12},{5,61},{6,14},{7,63},{8,0},{9,17... | collective-permute-start | bytes 2457608 | tf_op jit(solution)/shard_map/ppermute | solution.py:335
  237.5 9.2 %collective-permute-start.1 = (f32[4,25,8,128]{3,2,1,0:T(8,128)S(1)}, f32[4,25,8,128]{3,2,1,0:T(8,128)S(1)}, u32[]{:S(2)}, u32[]{:S(2)}) collective-permute-start(f32[4,25,8,128]{3,2,1,0:T(8,128)S(1)} %get-tuple-element.36), channel_id=1, source_target_pairs={{0,192},{1,65},{2,194},{3,67},{4,196},{5,69},{6,198},{7,71},{8,200... | collective-permute-start | bytes 1228808 | tf_op jit(solution)/shard_map/ppermute | solution.py:335
  239.4 9.4 %collective-permute-start.5 = (f32[4,25,8,128]{3,2,1,0:T(8,128)S(1)}, f32[4,25,8,128]{3,2,1,0:T(8,128)S(1)}, u32[]{:S(2)}, u32[]{:S(2)}) collective-permute-start(f32[4,25,8,128]{3,2,1,0:T(8,128)S(1)} %get-tuple-element.44), channel_id=1, source_target_pairs={{0,56},{1,9},{2,58},{3,11},{4,60},{5,13},{6,62},{7,15},{8,16},{9,1... | collective-permute-start | bytes 1228808 | tf_op jit(solution)/shard_map/ppermute | solution.py:335
  247.3 5.8 %collective-permute-start.2 = (f32[2,25,8,128]{3,2,1,0:T(8,128)S(1)}, f32[2,25,8,128]{3,2,1,0:T(8,128)S(1)}, u32[]{:S(2)}, u32[]{:S(2)}) collective-permute-start(f32[2,25,8,128]{3,2,1,0:T(8,128)S(1)} %get-tuple-element.38), channel_id=1, source_target_pairs={{0,8},{1,57},{2,10},{3,59},{4,12},{5,61},{6,14},{7,63},{8,0},{9,17... | collective-permute-start | bytes 614408 | tf_op jit(solution)/shard_map/ppermute | solution.py:335
  249.3 5.9 %collective-permute-start.6 = (f32[2,25,8,128]{3,2,1,0:T(8,128)S(1)}, f32[2,25,8,128]{3,2,1,0:T(8,128)S(1)}, u32[]{:S(2)}, u32[]{:S(2)}) collective-permute-start(f32[2,25,8,128]{3,2,1,0:T(8,128)S(1)} %get-tuple-element.46), channel_id=1, source_target_pairs={{0,64},{1,193},{2,66},{3,195},{4,68},{5,197},{6,70},{7,199},{8,72}... | collective-permute-start | bytes 614408 | tf_op jit(solution)/shard_map/ppermute | solution.py:335
  253.8 6.0 %collective-permute-start.3 = (f32[1,25,8,128]{3,2,1,0:T(8,128)S(1)}, f32[1,25,8,128]{3,2,1,0:T(8,128)S(1)}, u32[]{:S(2)}, u32[]{:S(2)}) collective-permute-start(f32[1,25,8,128]{3,2,1,0:T(8,128)S(1)} %get-tuple-element.40), channel_id=1, source_target_pairs={{0,56},{1,9},{2,58},{3,11},{4,60},{5,13},{6,62},{7,15},{8,16},{9,1... | collective-permute-start | bytes 307208 | tf_op jit(solution)/shard_map/ppermute | solution.py:335
  255.8 6.0 %collective-permute-start.7 = (f32[1,25,8,128]{3,2,1,0:T(8,128)S(1)}, f32[1,25,8,128]{3,2,1,0:T(8,128)S(1)}, u32[]{:S(2)}, u32[]{:S(2)}) collective-permute-start(f32[1,25,8,128]{3,2,1,0:T(8,128)S(1)} %get-tuple-element.48), channel_id=1, source_target_pairs={{0,192},{1,65},{2,194},{3,67},{4,196},{5,69},{6,198},{7,71},{8,200... | collective-permute-start | bytes 307208 | tf_op jit(solution)/shard_map/ppermute | solution.py:335
  261.7 7.8 %collective-permute-start.8 = (f32[2,25,8,128]{3,2,1,0:T(8,128)S(1)}, f32[2,25,8,128]{3,2,1,0:T(8,128)S(1)}, u32[]{:S(2)}, u32[]{:S(2)}) collective-permute-start(f32[2,25,8,128]{3,2,1,0:T(8,128)S(1)} %pair.1.sum_ref), channel_id=1, source_target_pairs={{0,24},{1,41},{2,26},{3,43},{4,28},{5,45},{6,30},{7,47},{8,48},{9,... | collective-permute-start | bytes 614408 | tf_op jit(solution)/shard_map/ppermute | solution.py:335
  269.7 6.9 %collective-permute-start.13 = (f32[1,24,8,128]{3,2,1,0:T(8,128)S(1)}, f32[1,24,8,128]{3,2,1,0:T(8,128)S(1)}, u32[]{:S(2)}, u32[]{:S(2)}) collective-permute-start(f32[1,24,8,128]{3,2,1,0:T(8,128)S(1)} %get-tuple-element.50.mine_ref), channel_id=1, source_target_pairs={{0,192},{1,65},{2,194},{3,67},{4,196},{5,69},{6,198},{7,71},{8,200... | collective-permute-start | bytes 294920 | tf_op jit(solution)/shard_map/ppermute | solution.py:335
  272.8 6.9 %collective-permute-start.9 = (f32[1,24,8,128]{3,2,1,0:T(8,128)S(1)}, f32[1,24,8,128]{3,2,1,0:T(8,128)S(1)}, u32[]{:S(2)}, u32[]{:S(2)}) collective-permute-start(f32[1,24,8,128]{3,2,1,0:T(8,128)S(1)} %get-tuple-element.49.mine_ref), channel_id=1, source_target_pairs={{0,56},{1,9},{2,58},{3,11},{4,60},{5,13},{6,62},{7,15},{8,16},{9,1... | collective-permute-start | bytes 294920 | tf_op jit(solution)/shard_map/ppermute | solution.py:335
  277.1 5.8 %collective-permute-start.14 = (f32[2,24,8,128]{3,2,1,0:T(8,128)S(1)}, f32[2,24,8,128]{3,2,1,0:T(8,128)S(1)}, u32[]{:S(2)}, u32[]{:S(2)}) collective-permute-start(f32[2,24,8,128]{3,2,1,0:T(8,128)S(1)} %join.9.mine_ref), channel_id=1, source_target_pairs={{0,64},{1,193},{2,66},{3,195},{4,68},{5,197},{6,70},{7,199},{8,72}... | collective-permute-start | bytes 589832 | tf_op jit(solution)/shard_map/ppermute | solution.py:335
  280.2 7.4 %collective-permute-start.10 = (f32[2,24,8,128]{3,2,1,0:T(8,128)S(1)}, f32[2,24,8,128]{3,2,1,0:T(8,128)S(1)}, u32[]{:S(2)}, u32[]{:S(2)}) collective-permute-start(f32[2,24,8,128]{3,2,1,0:T(8,128)S(1)} %join.6.mine_ref), channel_id=1, source_target_pairs={{0,8},{1,57},{2,10},{3,59},{4,12},{5,61},{6,14},{7,63},{8,0},{9,17... | collective-permute-start | bytes 589832 | tf_op jit(solution)/shard_map/ppermute | solution.py:335
  283.5 13.6 %collective-permute-start.15 = (f32[4,24,8,128]{3,2,1,0:T(8,128)S(1)}, f32[4,24,8,128]{3,2,1,0:T(8,128)S(1)}, u32[]{:S(2)}, u32[]{:S(2)}) collective-permute-start(f32[4,24,8,128]{3,2,1,0:T(8,128)S(1)} %join.10.mine_ref), channel_id=1, source_target_pairs={{0,56},{1,9},{2,58},{3,11},{4,60},{5,13},{6,62},{7,15},{8,16},{9,1... | collective-permute-start | bytes 1179656 | tf_op jit(solution)/shard_map/ppermute | solution.py:335
  288.2 13.5 %collective-permute-start.11 = (f32[4,24,8,128]{3,2,1,0:T(8,128)S(1)}, f32[4,24,8,128]{3,2,1,0:T(8,128)S(1)}, u32[]{:S(2)}, u32[]{:S(2)}) collective-permute-start(f32[4,24,8,128]{3,2,1,0:T(8,128)S(1)} %join.7.mine_ref), channel_id=1, source_target_pairs={{0,192},{1,65},{2,194},{3,67},{4,196},{5,69},{6,198},{7,71},{8,200... | collective-permute-start | bytes 1179656 | tf_op jit(solution)/shard_map/ppermute | solution.py:335
  297.7 14.0 %collective-permute-start.16 = (f32[8,24,8,128]{3,2,1,0:T(8,128)S(1)}, f32[8,24,8,128]{3,2,1,0:T(8,128)S(1)}, u32[]{:S(2)}, u32[]{:S(2)}) collective-permute-start(f32[8,24,8,128]{3,2,1,0:T(8,128)S(1)} %join.11.mine_b_ref), channel_id=1, source_target_pairs={{0,8},{1,57},{2,10},{3,59},{4,12},{5,61},{6,14},{7,63},{8,0},{9,17... | collective-permute-start | bytes 2359304 | tf_op jit(solution)/shard_map/ppermute | solution.py:335
  302.3 12.1 %collective-permute-start.12 = (f32[8,24,8,128]{3,2,1,0:T(8,128)S(1)}, f32[8,24,8,128]{3,2,1,0:T(8,128)S(1)}, u32[]{:S(2)}, u32[]{:S(2)}) collective-permute-start(f32[8,24,8,128]{3,2,1,0:T(8,128)S(1)} %join.8.mine_a_ref), channel_id=1, source_target_pairs={{0,64},{1,193},{2,66},{3,195},{4,68},{5,197},{6,70},{7,199},{8,72}... | collective-permute-start | bytes 2359304 | tf_op jit(solution)/shard_map/ppermute | solution.py:335

commit v3 on v1

v3 whole, which is shorter than its diff:
```python
import functools
import math

import jax
import jax.numpy as jnp
from jax import lax
from jax.experimental import pallas as pl
from jax.experimental.pallas import tpu as pltpu
from jax.sharding import PartitionSpec as P

ITERS = 3
LANES = 128
LIM = 40.0
MIB = 1024 * 1024
F32 = jnp.float32
XS, ZS = 4, 8
BLOCK = 32
PARTS = BLOCK // 8
CHUNKS = 4
XB1, XB2, ZB1, ZB2 = range(4)


def combine_lse(parts):
    top = jnp.max(parts, axis=0)
    return top + jnp.log(jnp.sum(jnp.exp(parts - top[None]), axis=0))


def lane_to_sublane(row):
    return jnp.transpose(jnp.broadcast_to(row, (LANES, LANES)))


def fold(x):
    return jnp.sum(x.reshape(x.shape[0] // 8, 8, x.shape[1]), axis=0)


def lane_group(g):
    return slice(g * LANES, (g + 1) * LANES)


def row_tile(t):
    return pl.ds(pl.multiple_of(t * LANES, LANES), LANES)


def put_copies(out_ref, value):
    for k in range(out_ref.shape[0]):
        out_ref[k] = value


def logit_block(k_ref, ok, t, g):
    block = k_ref[row_tile(t), lane_group(g)]
    return jnp.where(ok != 0, jnp.log(block), block)


def row_lse_exact(k_ref, ok, pot_ref, out_ref):
    tiles, groups = k_ref.shape[0] // LANES, k_ref.shape[1] // LANES

    def shifted(t, g):
        z = logit_block(k_ref, ok, t, g)
        return z if pot_ref is None else z + lane_to_sublane(pot_ref[pl.ds(t, 1), :])

    for g in range(groups):
        def top_of(t, top, g=g):
            return jnp.maximum(top, jnp.max(shifted(t, g), axis=0, keepdims=True))

        top = lax.fori_loop(0, tiles, top_of, jnp.full((1, LANES), -3.0e38, F32))

        def sum_of(t, total, g=g, top=top):
            return total + jnp.sum(jnp.exp(shifted(t, g) - top), axis=0, keepdims=True)

        total = lax.fori_loop(0, tiles, sum_of, jnp.zeros((1, LANES), F32))
        out_ref[g : g + 1, :] = top + jnp.log(total)


def col_lse_exact(k_ref, ok, pot, out_ref):
    tiles, groups = k_ref.shape[0] // LANES, k_ref.shape[1] // LANES

    def tile(t, carry):
        top = jnp.full((LANES, LANES), -3.0e38, F32)
        for g in range(groups):
            top = jnp.maximum(top, logit_block(k_ref, ok, t, g) + pot[g : g + 1, :])
        top = jnp.broadcast_to(jnp.max(top, axis=1, keepdims=True), (LANES, LANES))
        total = jnp.zeros((LANES, LANES), F32)
        for g in range(groups):
            total = total + jnp.exp(logit_block(k_ref, ok, t, g) + pot[g : g + 1, :] - top)
        total = jnp.sum(jnp.transpose(total), axis=0, keepdims=True)
        out_ref[pl.ds(t, 1), :] = jnp.transpose(top)[0:1, :] + jnp.log(total)
        return carry

    lax.fori_loop(0, tiles, tile, 0)


def logits_kernel(_, cent_hbm, vec_hbm, k_ref, ok_ref, out_ref, lse_ref, cent_ref, vec_ref, sems):
    cents, rows = k_ref.shape
    groups = rows // LANES
    step, chunk = cents // CHUNKS, rows // CHUNKS

    def pieces(hbm_ref, vmem_ref, first, size):
        return [
            pltpu.make_async_copy(
                hbm_ref.at[pl.ds(c * size, size), :], vmem_ref.at[pl.ds(c * size, size), :], sems.at[first + c]
            )
            for c in range(CHUNKS)
        ]

    vec_copies = pieces(vec_hbm, vec_ref, 0, chunk)
    cent_copies = pieces(cent_hbm, cent_ref, CHUNKS, step)
    for copy in vec_copies[:1] + cent_copies + vec_copies[1:]:
        copy.start()

    peak = jnp.zeros((8, LANES), F32)
    for c in range(CHUNKS):
        vec_copies[c].wait()
        if c == 0:
            for copy in cent_copies:
                copy.wait()
        block = lax.dot_general(
            cent_ref[...], vec_ref[c * chunk : (c + 1) * chunk, :],
            (((1,), (1,)), ((), ())), preferred_element_type=F32,
        )
        for g in range(chunk // LANES):
            group = c * (chunk // LANES) + g
            total = jnp.zeros((8, LANES), F32)
            for t in range(cents // LANES):
                part = 4.0 * block[t * LANES : (t + 1) * LANES, lane_group(g)]
                peak = jnp.maximum(peak, jnp.max(jnp.abs(part).reshape(LANES // 8, 8, LANES), axis=0))
                part = jnp.exp(part)
                k_ref[t * LANES : (t + 1) * LANES, lane_group(group)] = part
                total = total + fold(part)
            lse_ref[group : group + 1, :] = jnp.sum(total, axis=0, keepdims=True)
    lse_ref[...] = jnp.log(lse_ref[...])
    ok = jnp.max(peak) <= LIM
    ok_ref[0, 0] = ok.astype(jnp.int32)

    @pl.when(jnp.logical_not(ok))
    def _():
        def tile(t, carry):
            at = row_tile(t)
            for g in range(groups):
                k_ref[at, lane_group(g)] = 4.0 * lax.dot_general(
                    cent_ref[at, :], vec_ref[lane_group(g), :],
                    (((1,), (1,)), ((), ())), preferred_element_type=F32,
                )
            return carry

        lax.fori_loop(0, cents // LANES, tile, 0)
        row_lse_exact(k_ref, 0, None, lse_ref)

    put_copies(out_ref, lse_ref[...])


def row_kernel(log_target, got_ref, ok_ref, k_ref, out_ref, pot_ref, lse_ref):
    tiles, groups = k_ref.shape[0] // LANES, k_ref.shape[1] // LANES
    pot = log_target - combine_lse(got_ref[...])
    ok = ok_ref[0, 0]
    fast = jnp.logical_and(ok != 0, jnp.max(jnp.abs(pot)) <= LIM)

    @pl.when(fast)
    def _():
        scales = jnp.exp(pot)
        sums = [jnp.zeros((8, LANES), F32)] * groups
        for t in range(tiles):
            scale = lane_to_sublane(scales[t : t + 1, :])
            for g in range(groups):
                sums[g] = sums[g] + fold(k_ref[t * LANES : (t + 1) * LANES, lane_group(g)] * scale)
        for g in range(groups):
            lse_ref[g : g + 1, :] = jnp.sum(sums[g], axis=0, keepdims=True)
        lse_ref[...] = jnp.log(lse_ref[...])

    @pl.when(jnp.logical_not(fast))
    def _():
        pot_ref[...] = pot
        row_lse_exact(k_ref, ok, pot_ref, lse_ref)

    put_copies(out_ref, lse_ref[...])


def col_kernel(got_ref, ok_ref, k_ref, out_ref, lse_ref):
    tiles, groups = k_ref.shape[0] // LANES, k_ref.shape[1] // LANES
    pot = -combine_lse(got_ref[...])
    ok = ok_ref[0, 0]
    fast = jnp.logical_and(ok != 0, jnp.max(jnp.abs(pot)) <= LIM)

    @pl.when(fast)
    def _():
        scale = jnp.exp(pot)

        for t in range(tiles):
            total = jnp.zeros((LANES, LANES), F32)
            for g in range(groups):
                total = total + k_ref[t * LANES : (t + 1) * LANES, lane_group(g)] * scale[g : g + 1, :]
            lse_ref[t : t + 1, :] = jnp.sum(jnp.transpose(total), axis=0, keepdims=True)
        lse_ref[...] = jnp.log(lse_ref[...])

    @pl.when(jnp.logical_not(fast))
    def _():
        col_lse_exact(k_ref, ok, pot, lse_ref)

    put_copies(out_ref, lse_ref[...])


def half_kernel(
    log_target, keep, bits_ref, cols_ref, rows_ref, ok_ref, k_ref, vec_ref,
    a_ref, b_ref, *rest,
):
    scale_ref, plan_ref, mass_ref = rest[-3:]
    groups = k_ref.shape[1] // LANES
    col_pot = log_target - combine_lse(cols_ref[...])
    row_pot = -combine_lse(rows_ref[...])
    if not keep:
        rest[0][...] = row_pot
        rest[1][...] = col_pot
    ok = ok_ref[0, 0]
    fast = jnp.logical_and(
        ok != 0, jnp.maximum(jnp.max(jnp.abs(col_pot)), jnp.max(jnp.abs(row_pot))) <= LIM
    )
    scale_ref[...] = jnp.where(fast, jnp.exp(col_pot), col_pot)
    row_scale = jnp.exp(row_pot)
    blocks = a_ref.shape[0]
    tiles = blocks * BLOCK // LANES

    def plan_tile(spot, block):
        total = jnp.zeros((LANES, LANES), F32)
        for g in range(groups):
            plan = block(g)
            total = total + plan
            plan_ref[row_tile(spot), lane_group(g)] = plan.astype(jnp.bfloat16)
        mass = jnp.broadcast_to(jnp.sum(total, axis=1, keepdims=True), (LANES, LANES))
        lane = lax.broadcasted_iota(jnp.int32, (8, LANES), 1) // (LANES // PARTS)
        for b in range(LANES // BLOCK):
            unit = mass[b * BLOCK : b * BLOCK + 8, :]
            for k in range(1, PARTS):
                at = b * BLOCK + 8 * k
                unit = jnp.where(lane == k, mass[at : at + 8, :], unit)
            mass_ref[spot * (LANES // BLOCK) + b] = unit

    firsts = []
    for chain, which in enumerate((XB1, ZB1)):
        bit = bits_ref[which] if keep else 1 - bits_ref[which]
        firsts.append((chain * 2 + bit) * tiles)

    def sums():
        size = blocks * BLOCK
        for chain, out_ref in enumerate((a_ref, b_ref)):
            block = jnp.dot(
                plan_ref[chain * size : (chain + 1) * size, :], vec_ref[...], preferred_element_type=F32
            )
            across = block.shape[1] // LANES
            for b in range(blocks):
                for k in range(PARTS):
                    row = b * BLOCK + 8 * k
                    for g in range(across):
                        out_ref[b, k * across + g] = block[row : row + 8, lane_group(g)]
                out_ref[b, out_ref.shape[1] - 1] = mass_ref[chain * blocks + b]

    @pl.when(fast)
    def _():
        for chain, first in enumerate(firsts):
            for t in range(tiles):
                scale = lane_to_sublane(scale_ref[pl.ds(first + t, 1), :])
                plan_tile(
                    chain * tiles + t,
                    lambda g: k_ref[row_tile(first + t), lane_group(g)] * row_scale[g : g + 1, :] * scale,
                )
        sums()

    @pl.when(jnp.logical_not(fast))
    def _():
        for chain, first in enumerate(firsts):
            def tile(t, carry):
                shift = lane_to_sublane(scale_ref[pl.ds(first + t, 1), :])
                plan_tile(
                    chain * tiles + t,
                    lambda g: jnp.exp(
                        logit_block(k_ref, ok, first + t, g) + row_pot[g : g + 1, :] + shift
                    ),
                )
                return carry

            lax.fori_loop(0, tiles, tile, 0)
        sums()


def fold_kernel(which, bits_ref, keep_ref, got_ref, send_ref, kept_ref):
    half = send_ref.shape[0]
    mine = bits_ref[which] * half
    other = (1 - bits_ref[which]) * half
    for b in range(half):
        send_ref[b] = keep_ref[other + b] + got_ref[other + b]
        kept_ref[b] = keep_ref[mine + b] + got_ref[mine + b]


def quarter_kernel(keep_a_ref, got_a_ref, keep_b_ref, got_b_ref, out_ref):
    for p in range(out_ref.shape[0]):
        out_ref[p, 0] = keep_a_ref[p] + got_a_ref[p]
        out_ref[p, 1] = keep_b_ref[p] + got_b_ref[p]


def four_kernel(got_ref, out_ref):
    out_ref[...] = (got_ref[0] + got_ref[1]) + (got_ref[2] + got_ref[3])


def mean_kernel(sum_ref, got_ref, out_ref):
    copies, chains, _, width = out_ref.shape
    units = sum_ref.shape[1] - 1
    across = width // LANES
    lanes = LANES // PARTS
    for chain in range(chains):
        mass = sum_ref[chain, units] + got_ref[chain, units]
        for k in range(PARTS):
            part = jnp.broadcast_to(mass[:, k * lanes : k * lanes + 1], (8, LANES))
            for g in range(across):
                u = k * across + g
                mean = (sum_ref[chain, u] + got_ref[chain, u]) / part
                for copy in range(copies):
                    out_ref[copy, chain, 8 * k : 8 * k + 8, lane_group(g)] = mean


def part_kernel(got_ref, a_ref, b_ref):
    for p in range(got_ref.shape[0]):
        at = slice(p * BLOCK, (p + 1) * BLOCK)
        a_ref[at, :] = got_ref[p, 0]
        b_ref[at, :] = got_ref[p, 1]


def join_kernel(which, bits_ref, mine_ref, got_ref, out_ref):
    size = mine_ref.shape[0]
    bit = bits_ref[which]
    out_ref[pl.ds(pl.multiple_of(bit * size, size), size), :] = mine_ref[...]
    out_ref[pl.ds(pl.multiple_of((1 - bit) * size, size), size), :] = got_ref[...]


def place_kernel(own, bits_ref, a_ref, b_ref, *rest):
    out_ref, sems = rest[-2:]
    size = a_ref.shape[0]
    copies = []
    for chain, (which, part_ref) in enumerate(((XB1, a_ref), (ZB1, b_ref))):
        side = bits_ref[which] if own else 1 - bits_ref[which]
        at = pl.ds(pl.multiple_of((2 * chain + side) * size, size), size)
        copies.append(pltpu.make_async_copy(part_ref, out_ref.at[at, :], sems.at[chain]))
    for copy in copies:
        copy.start()
    for copy in copies:
        copy.wait()


def place(row, core):
    return (row // ZS + (XS - 1) * core) % XS, (row % ZS + (ZS - 1) * core) % ZS


def pairs(partner, n_cols):
    out = []
    for row in range(XS * ZS):
        for col in range(n_cols):
            core = col % 2
            x, z = partner(*place(row, core))
            to = (x + core) % XS * ZS + (z + core) % ZS
            out.append((row * n_cols + col, to * n_cols + col))
    return out


def exchange(x, partner):
    return lax.ppermute(x, ("rows", "cols"), pairs(partner, lax.axis_size("cols")))


def x_first(x, z):
    return x ^ 1, z


def x_second(x, z):
    return XS - 1 - x, z


def z_first(x, z):
    return x, z ^ 1


def z_second(x, z):
    return x, (z - 1 + 2 * (z % 2)) % ZS


def z_third(x, z):
    return x, {0: 3, 3: 0, 1: 6, 6: 1, 2: 5, 5: 2, 4: 7, 7: 4}[z]


def position_bits():
    x, z = place(lax.axis_index("rows"), lax.axis_index("cols") % 2)
    return jnp.stack([(x ^ (x >> 1)) & 1, x >> 1, ((z + 1) >> 1) & 1, (0xB4 >> z) & 1]).astype(jnp.int32)


def quads(n_cols):
    groups = {}
    for row in range(XS * ZS):
        for col in range(n_cols):
            x, z = place(row, col % 2)
            key = (col, min(x, x_second(x, z)[0]), min(z, z_second(x, z)[1]))
            groups.setdefault(key, []).append(((x >> 1) * 2 + ((0xB4 >> z) & 1), row * n_cols + col))
    return [[device for _, device in sorted(groups[key])] for key in sorted(groups)]


def trade(x):
    return lax.all_to_all(
        x, ("rows", "cols"), 0, 0, tiled=True, axis_index_groups=quads(lax.axis_size("cols"))
    )


def halve(which, bits, keep, got):
    half = jax.ShapeDtypeStruct((keep.shape[0] // 2, *keep.shape[1:]), F32)
    return pl.pallas_call(
        functools.partial(fold_kernel, which),
        out_shape=(half, half),
        in_specs=[smem(), vmem(), vmem()],
        out_specs=(vmem(), vmem()),
        compiler_params=params(4),
        name="fold",
    )(bits, keep, got)


def join(which, bits, mine, got):
    return pl.pallas_call(
        functools.partial(join_kernel, which),
        out_shape=jax.ShapeDtypeStruct((2 * mine.shape[0], *mine.shape[1:]), F32),
        in_specs=[smem(), vmem(), vmem()],
        out_specs=vmem(),
        compiler_params=params(4),
        name="join",
    )(bits, mine, got)


def put(own, bits, a, b, cents, *before):
    return pl.pallas_call(
        functools.partial(place_kernel, own),
        out_shape=jax.ShapeDtypeStruct((cents, a.shape[1]), F32),
        in_specs=[smem(), vmem(), vmem()] + [hbm()] * len(before),
        out_specs=hbm(),
        scratch_shapes=[pltpu.SemaphoreType.DMA((2,))],
        input_output_aliases={3: 0} if before else {},
        compiler_params=params(4),
        name="place",
    )(bits, a, b, *before)


def mean_over_rows(bits, send_a, keep_a, send_b, keep_b, cents, width):
    got_a, got_b = exchange(send_a, x_first), exchange(send_b, z_first)
    send_a, keep_a = halve(ZB1, bits, keep_a, got_a)
    send_b, keep_b = halve(XB1, bits, keep_b, got_b)
    got_a, got_b = exchange(send_a, z_first), exchange(send_b, x_first)
    block = keep_a.shape[1:]
    quarter = pl.pallas_call(
        quarter_kernel,
        out_shape=jax.ShapeDtypeStruct((4, 2, *block), F32),
        in_specs=[vmem()] * 4,
        out_specs=vmem(),
        compiler_params=params(4),
        name="quarter",
    )(keep_a, got_a, keep_b, got_b)
    sums = pl.pallas_call(
        four_kernel,
        out_shape=jax.ShapeDtypeStruct((2, *block), F32),
        in_specs=[vmem()],
        out_specs=vmem(),
        compiler_params=params(4),
        name="four",
    )(trade(quarter))
    mean = pl.pallas_call(
        mean_kernel,
        out_shape=jax.ShapeDtypeStruct((4, 2, BLOCK, width), F32),
        in_specs=[vmem()] * 2,
        out_specs=vmem(),
        compiler_params=params(4),
        name="mean",
    )(sums, exchange(sums, z_third))
    part = jax.ShapeDtypeStruct((4 * BLOCK, width), F32)
    mine_a, mine_b = pl.pallas_call(
        part_kernel,
        out_shape=(part, part),
        in_specs=[vmem()],
        out_specs=(vmem(), vmem()),
        compiler_params=params(4),
        name="part",
    )(trade(mean))
    got_a, got_b = exchange(mine_a, z_first), exchange(mine_b, x_first)
    mine_a = join(ZB1, bits, mine_a, got_a)
    mine_b = join(XB1, bits, mine_b, got_b)
    got_a, got_b = exchange(mine_a, x_first), exchange(mine_b, z_first)
    return put(False, bits, got_a, got_b, cents, put(True, bits, mine_a, mine_b, cents))


def vmem():
    return pl.BlockSpec(memory_space=pltpu.VMEM)


def hbm():
    return pl.BlockSpec(memory_space=pltpu.HBM)


def smem():
    return pl.BlockSpec(memory_space=pltpu.SMEM)


def pinned(x):
    return pltpu.with_memory_space_constraint(x, pltpu.VMEM)


def params(mib):
    return pltpu.CompilerParams(vmem_limit_bytes=mib * MIB)


def per_device(vectors, centroids):
    n_rows, n_cols = lax.axis_size("rows"), lax.axis_size("cols")
    rows, width = vectors.shape
    cents = centroids.shape[0]
    log_target = math.log(rows * n_rows / (cents * n_cols))
    groups, tiles = rows // LANES, cents // LANES
    kept = pltpu.VMEM((cents, rows), F32)
    ok_type = jax.ShapeDtypeStruct((1, 1), jnp.int32)
    row_parts = jax.ShapeDtypeStruct((n_cols, groups, LANES), F32)
    col_parts = jax.ShapeDtypeStruct((n_rows, tiles, LANES), F32)
    row_scratch = pltpu.VMEM((groups, LANES), F32)
    col_scratch = pltpu.VMEM((tiles, LANES), F32)

    bits = position_bits()

    kernel, ok, part = pl.pallas_call(
        logits_kernel,
        out_shape=(kept, ok_type, row_parts),
        in_specs=[smem(), hbm(), hbm()],
        out_specs=(vmem(), smem(), vmem()),
        scratch_shapes=[
            row_scratch,
            pltpu.VMEM((cents, width), jnp.bfloat16),
            pltpu.VMEM((rows, width), jnp.bfloat16),
            pltpu.SemaphoreType.DMA((2 * CHUNKS,)),
        ],
        compiler_params=params(24),
        name="logits",
    )(bits, *(pltpu.with_memory_space_constraint(x, pltpu.HBM) for x in (centroids, vectors)))

    for step in range(ITERS):
        row_got = lax.all_to_all(part, "cols", 0, 0, tiled=True)
        part = pl.pallas_call(
            col_kernel,
            out_shape=col_parts,
            in_specs=[vmem(), smem(), vmem()],
            out_specs=vmem(),
            scratch_shapes=[col_scratch],
            compiler_params=params(4),
            name="col_step",
        )(row_got, ok, pinned(kernel))
        col_got = lax.all_to_all(part, "rows", 0, 0, tiled=True)
        part = pl.pallas_call(
            functools.partial(row_kernel, log_target),
            out_shape=row_parts,
            in_specs=[vmem(), smem(), vmem()],
            out_specs=vmem(),
            scratch_shapes=[col_scratch, row_scratch],
            compiler_params=params(4),
            name="row_step",
        )(col_got, ok, pinned(kernel))
    row_got = lax.all_to_all(part, "cols", 0, 0, tiled=True)

    part_units = PARTS * (width // LANES) + 1
    halves = jax.ShapeDtypeStruct((cents // BLOCK // 4, part_units, 8, LANES), F32)

    def half(keep):
        pots = (jax.ShapeDtypeStruct((groups, LANES), F32), jax.ShapeDtypeStruct((tiles, LANES), F32))
        return pl.pallas_call(
            functools.partial(half_kernel, log_target, keep),
            out_shape=(halves, halves) + (() if keep else pots),
            in_specs=[smem(), vmem(), vmem(), smem(), vmem(), vmem()],
            out_specs=(vmem(),) * (2 if keep else 4),
            scratch_shapes=[
                col_scratch,
                pltpu.VMEM((cents // 2, rows), jnp.bfloat16),
                pltpu.VMEM((cents // BLOCK // 2, 8, LANES), F32),
            ],
            compiler_params=params(12),
            cost_estimate=pl.CostEstimate(
                flops=rows * cents * width, bytes_accessed=8 * MIB, transcendentals=0
            ),
            name="keep" if keep else "send",
        )(bits, col_got, row_got, ok, pinned(kernel), vectors)

    send_a, send_b, row_pot, col_pot = half(False)
    keep_a, keep_b = half(True)
    new_centroids = mean_over_rows(bits, send_a, keep_a, send_b, keep_b, cents, width)
    return (new_centroids, row_pot.reshape(rows), col_pot.reshape(cents))


def solution(mesh):
    return jax.shard_map(
        per_device,
        mesh=mesh,
        in_specs=(P("rows", None), P("cols", None)),
        out_specs=(P("cols", None), P("rows"), P("cols")),
        check_vma=False,
    )
```

time: 416 us -> 301 us (0.72)
  waiting for transfers between devices: 138 us -> 35.8 us
  Pallas kernels: 159 us -> 143 us
  blocking collectives: 96.6 us -> 112 us
  between operations: 14.1 us -> 1.03 us
  starting transfers between devices: 0.04 us -> 7.24 us
    psum x1 -> x0, waiting for transfers between devices: 138 us -> none  [per_device(): full_sum = lax.psum(weighted, 'rows')]
    ppermute x0 -> x9, waiting for transfers between devices: none -> 35.8 us  [exchange(): lax.ppermute(x, ('rows', 'cols'), pairs(partner, lax.axis_size('cols')))]
    all_to_all x1 -> x2, blocking collectives: 14.4 us -> 30.1 us  [trade(): lax.all_to_all(x, ('rows', 'cols'), 0, 0, tiled=True, axis_index_groups=q...]
    pallas_call x3, Pallas kernels: 22.6 us -> 12.7 us  [per_device(): pl.pallas_call(col_kernel, out_shape=col_parts, in_specs=[vmem(), smem(),...]
    pallas_call x3, Pallas kernels: 101 us -> 91.3 us  [per_device(): pl.pallas_call(functools.partial(row_kernel, log_target), out_shape=row_p...]
    ppermute x0 -> x9, starting transfers between devices: none -> 7.24 us  [exchange(): lax.ppermute(x, ('rows', 'cols'), pairs(partner, lax.axis_size('cols')))]
    pallas_call x1 -> x12, Pallas kernels: 13.5 us -> 16.8 us  [the longest x2 10.7 us: half(): pl.pallas_call(functools.partial(half_kernel, log_target, keep), out_shap...]
  transfers between devices with their start and end apart: 1 -> 9, of which waited for: 1 -> 7; matrix products, arithmetic and copies ran while one was open for 0% -> 0% of each run, Pallas kernels for 0% -> 3%
where the time goes in v3:
time: 301 us; the launch traced here: 299 us
  Pallas kernels  143 us (48%)
  blocking collectives  112 us (37%)
  waiting for transfers between devices  35.8 us (12%)
  starting transfers between devices  7.24 us (2%)
    pallas_call x3, Pallas kernels, per_device(): pl.pallas_call(functools.partial(row_kernel, log_target), out_shape=row_p...  91.3 us
    all_to_all x3, blocking collectives, per_device(): col_got = lax.all_to_all(part, 'rows', 0, 0, tiled=True)  49.1 us
    ppermute x9, waiting for transfers between devices, exchange(): lax.ppermute(x, ('rows', 'cols'), pairs(partner, lax.axis_size('cols')))  35.8 us
    all_to_all x4, blocking collectives, per_device(): row_got = lax.all_to_all(part, 'cols', 0, 0, tiled=True)  32.9 us
    all_to_all x2, blocking collectives, trade(): lax.all_to_all(x, ('rows', 'cols'), 0, 0, tiled=True, axis_index_groups=q...  30.1 us
    pallas_call x1, Pallas kernels, per_device(): pl.pallas_call(logits_kernel, out_shape=(kept, ok_type, row_parts), in_sp...  22.1 us
    pallas_call x3, Pallas kernels, per_device(): pl.pallas_call(col_kernel, out_shape=col_parts, in_specs=[vmem(), smem(),...  12.7 us
    pallas_call x2, Pallas kernels, half(): pl.pallas_call(functools.partial(half_kernel, log_target, keep), out_shap...  10.7 us
  transfers between devices with their start and end apart: 9, of which 7 were waited for; matrix products, arithmetic and copies ran while one was open for 0% of the time, Pallas kernels for 3%

profile of v3, /device:TPU:8, one launch (start us, length us, event | category | flops | bytes accessed | tf_op | source)
XLA Modules:
  0.0 299.1 jit_solution(18267667740682596818)
XLA Ops:
  0.7 0.1 pad_add_fusion._.bits_ref
  0.8 22.1 %logits.1 = (f32[1024,2048]{1,0:T(8,128)S(1)}, s32[1,1]{1,0:T(1,128)}, f32[8,16,128]{2,1,0:T(8,128)S(1)}) custom-call(s32[4]{0:T(128)S(1)} %pad_add_fusion._.bits_ref, bf16[1024,768]{1,0:T(8,128)(2,1)} %cent_hbm.1, bf16[2048,768]{1,0:T(8,128)(2,1)} %vec_ref.3), custom_call_target="tpu_custom_call" | custom-call | tf_op jit(solution)/shard_map/logits/pallas_call | solution.py:523
  22.9 8.9 %all_to_all.45.got_ref = f32[8,16,128]{2,1,0:T(8,128)S(1)} all-to-all(f32[8,16,128]{2,1,0:T(8,128)S(1)} %get-tuple-element.18), channel_id=1, replica_groups=mesh['rows'=32,'cols'=8] {'cols'}, dimensions={0} | all-to-all | bytes 131072 | tf_op jit(solution)/shard_map/all_to_all | solution.py:539
  31.8 4.2 %col_step.3 = f32[32,8,128]{2,1,0:T(8,128)S(1)} custom-call(f32[8,16,128]{2,1,0:T(8,128)S(1)} %all_to_all.45.got_ref, s32[1,1]{1,0:T(1,128)} %get-tuple-element.19.ok_ref, f32[1024,2048]{1,0:T(8,128)S(1)} %get-tuple-element.20.k_ref), custom_call_target="tpu_custom_call" | custom-call | tf_op jit(solution)/shard_map/col_step/pallas_call | solution.py:540
  36.0 21.4 %all_to_all.46.got_ref = f32[32,8,128]{2,1,0:T(8,128)S(1)} all-to-all(f32[32,8,128]{2,1,0:T(8,128)S(1)} %col_step.3), channel_id=1, replica_groups=mesh['rows'=32,'cols'=8] {'rows'}, dimensions={0} | all-to-all | bytes 262144 | tf_op jit(solution)/shard_map/all_to_all | solution.py:549
  57.4 30.3 %row_step.3 = f32[8,16,128]{2,1,0:T(8,128)S(1)} custom-call(f32[32,8,128]{2,1,0:T(8,128)S(1)} %all_to_all.46.got_ref, s32[1,1]{1,0:T(1,128)} %get-tuple-element.19.ok_ref, f32[1024,2048]{1,0:T(8,128)S(1)} %get-tuple-element.20.k_ref), custom_call_target="tpu_custom_call" | custom-call | tf_op jit(solution)/shard_map/row_step/pallas_call | solution.py:550
  87.7 8.0 %all_to_all.47.got_ref = f32[8,16,128]{2,1,0:T(8,128)S(1)} all-to-all(f32[8,16,128]{2,1,0:T(8,128)S(1)} %row_step.3), channel_id=1, replica_groups=mesh['rows'=32,'cols'=8] {'cols'}, dimensions={0} | all-to-all | bytes 131072 | tf_op jit(solution)/shard_map/all_to_all | solution.py:539
  95.7 4.2 %col_step.4 = f32[32,8,128]{2,1,0:T(8,128)S(1)} custom-call(f32[8,16,128]{2,1,0:T(8,128)S(1)} %all_to_all.47.got_ref, s32[1,1]{1,0:T(1,128)} %get-tuple-element.19.ok_ref, f32[1024,2048]{1,0:T(8,128)S(1)} %get-tuple-element.20.k_ref), custom_call_target="tpu_custom_call" | custom-call | tf_op jit(solution)/shard_map/col_step/pallas_call | solution.py:540
  100.0 13.9 %all_to_all.48.got_ref = f32[32,8,128]{2,1,0:T(8,128)S(1)} all-to-all(f32[32,8,128]{2,1,0:T(8,128)S(1)} %col_step.4), channel_id=1, replica_groups=mesh['rows'=32,'cols'=8] {'rows'}, dimensions={0} | all-to-all | bytes 262144 | tf_op jit(solution)/shard_map/all_to_all | solution.py:549
  113.8 30.5 %row_step.4 = f32[8,16,128]{2,1,0:T(8,128)S(1)} custom-call(f32[32,8,128]{2,1,0:T(8,128)S(1)} %all_to_all.48.got_ref, s32[1,1]{1,0:T(1,128)} %get-tuple-element.19.ok_ref, f32[1024,2048]{1,0:T(8,128)S(1)} %get-tuple-element.20.k_ref), custom_call_target="tpu_custom_call" | custom-call | tf_op jit(solution)/shard_map/row_step/pallas_call | solution.py:550
  144.3 8.0 %all_to_all.49.got_ref = f32[8,16,128]{2,1,0:T(8,128)S(1)} all-to-all(f32[8,16,128]{2,1,0:T(8,128)S(1)} %row_step.4), channel_id=1, replica_groups=mesh['rows'=32,'cols'=8] {'cols'}, dimensions={0} | all-to-all | bytes 131072 | tf_op jit(solution)/shard_map/all_to_all | solution.py:539
  152.3 4.2 %col_step.5 = f32[32,8,128]{2,1,0:T(8,128)S(1)} custom-call(f32[8,16,128]{2,1,0:T(8,128)S(1)} %all_to_all.49.got_ref, s32[1,1]{1,0:T(1,128)} %get-tuple-element.19.ok_ref, f32[1024,2048]{1,0:T(8,128)S(1)} %get-tuple-element.20.k_ref), custom_call_target="tpu_custom_call" | custom-call | tf_op jit(solution)/shard_map/col_step/pallas_call | solution.py:540
  156.6 13.9 %all_to_all.50.got_ref.cols_ref = f32[32,8,128]{2,1,0:T(8,128)S(1)} all-to-all(f32[32,8,128]{2,1,0:T(8,128)S(1)} %col_step.5), channel_id=1, replica_groups=mesh['rows'=32,'cols'=8] {'rows'}, dimensions={0} | all-to-all | bytes 262144 | tf_op jit(solution)/shard_map/all_to_all | solution.py:549
  170.4 0.0 copy-start
  170.4 30.5 %row_step.5 = f32[8,16,128]{2,1,0:T(8,128)S(1)} custom-call(f32[32,8,128]{2,1,0:T(8,128)S(1)} %all_to_all.50.got_ref.cols_ref, s32[1,1]{1,0:T(1,128)} %get-tuple-element.19.ok_ref, f32[1024,2048]{1,0:T(8,128)S(1)} %get-tuple-element.20.k_ref), custom_call_target="tpu_custom_call" | custom-call | tf_op jit(solution)/shard_map/row_step/pallas_call | solution.py:550
  200.9 8.0 %all_to_all.51.rows_ref = f32[8,16,128]{2,1,0:T(8,128)S(1)} all-to-all(f32[8,16,128]{2,1,0:T(8,128)S(1)} %row_step.5), channel_id=1, replica_groups=mesh['rows'=32,'cols'=8] {'cols'}, dimensions={0} | all-to-all | bytes 131072 | tf_op jit(solution)/shard_map/all_to_all | solution.py:559
  208.9 0.0 copy-done
  208.9 5.5 %send.1 = (f32[8,25,8,128]{3,2,1,0:T(8,128)S(1)}, f32[8,25,8,128]{3,2,1,0:T(8,128)S(1)}, f32[16,128]{1,0:T(8,128)}, f32[8,128]{1,0:T(8,128)}) custom-call(s32[4]{0:T(128)S(1)} %pad_add_fusion._.bits_ref, f32[32,8,128]{2,1,0:T(8,128)S(1)} %all_to_all.50.got_ref.cols_ref, f32[8,16,128]{2,1,0:T(8,128)S(1)} %all_to_all.51.rows_ref, ...), custom_call_target="tpu_custom_call" | custom-call | flops 1610612736 | bytes 8388608 | tf_op jit(solution)/shard_map/send/pallas_call | solution.py:566
  214.5 0.6 collective-permute-start
  215.1 1.3 collective-permute-start.2
  216.3 5.1 %keep.1 = (f32[8,25,8,128]{3,2,1,0:T(8,128)S(1)}, f32[8,25,8,128]{3,2,1,0:T(8,128)S(1)}) custom-call(s32[4]{0:T(128)S(1)} %pad_add_fusion._.bits_ref, f32[32,8,128]{2,1,0:T(8,128)S(1)} %all_to_all.50.got_ref.cols_ref, f32[8,16,128]{2,1,0:T(8,128)S(1)} %all_to_all.51.rows_ref, s32[1,1]{1,0:T(1,128)} %get-tuple-element.19.ok_ref, ...), custom_call_target="tpu_custom_call" | custom-call | flops 1610612736 | bytes 8388608 | tf_op jit(solution)/shard_map/keep/pallas_call | solution.py:566
  221.5 5.3 %collective-permute-done.got_ref = f32[8,25,8,128]{3,2,1,0:T(8,128)S(1)} collective-permute-done((f32[8,25,8,128]{3,2,1,0:T(8,128)S(1)}, f32[8,25,8,128]{3,2,1,0:T(8,128)S(1)}, u32[]{:S(2)}, u32[]{:S(2)}) %collective-permute-start) | collective-permute-done | bytes 819232 | tf_op jit(solution)/shard_map/ppermute | solution.py:362
  226.8 0.6 fold.2
  227.4 1.3 collective-permute-start.1
  228.8 0.0 collective-permute-done.2.got_ref
  228.8 0.6 fold.3
  229.4 0.7 collective-permute-start.3
  230.1 5.3 %collective-permute-done.1.got_a_ref = f32[4,25,8,128]{3,2,1,0:T(8,128)S(1)} collective-permute-done((f32[4,25,8,128]{3,2,1,0:T(8,128)S(1)}, f32[4,25,8,128]{3,2,1,0:T(8,128)S(1)}, u32[]{:S(2)}, u32[]{:S(2)}) %collective-permute-start.1) | collective-permute-done | bytes 409632 | tf_op jit(solution)/shard_map/ppermute | solution.py:362
  235.5 2.0 collective-permute-done.3.got_b_ref
  237.4 0.1 quarter.1
  237.5 13.8 %all_to_all.52.got_ref = f32[4,2,25,8,128]{4,3,2,1,0:T(8,128)S(1)} all-to-all(f32[4,2,25,8,128]{4,3,2,1,0:T(8,128)S(1)} %quarter.1), channel_id=1, replica_groups={{0,56,192,248},{8,16,200,208},{24,32,216,224},{48,40,240,232},{64,120,1..., dimensions={0} | all-to-all | bytes 1638400 | tf_op jit(solution)/shard_map/all_to_all | solution.py:401
  251.4 1.6 collective-permute-start.4
  253.0 6.5 %collective-permute-done.4.got_ref = f32[2,25,8,128]{3,2,1,0:T(8,128)S(1)} collective-permute-done((f32[2,25,8,128]{3,2,1,0:T(8,128)S(1)}, f32[2,25,8,128]{3,2,1,0:T(8,128)S(1)}, u32[]{:S(2)}, u32[]{:S(2)}) %collective-permute-start.4) | collective-permute-done | bytes 204832 | tf_op jit(solution)/shard_map/ppermute | solution.py:362
  259.5 0.1 mean.1
  259.6 16.3 %all_to_all.53.got_ref = f32[4,2,32,768]{3,2,1,0:T(8,128)S(1)} all-to-all(f32[4,2,32,768]{3,2,1,0:T(8,128)S(1)} %mean.1), channel_id=1, replica_groups={{0,56,192,248},{8,16,200,208},{24,32,216,224},{48,40,240,232},{64,120,1..., dimensions={0} | all-to-all | bytes 1572864 | tf_op jit(solution)/shard_map/all_to_all | solution.py:401
  275.9 0.1 part.1
  276.0 0.1 collective-permute-start.7
  276.1 0.1 collective-permute-start.5
  276.2 7.7 %collective-permute-done.7.got_ref = f32[128,768]{1,0:T(8,128)S(1)} collective-permute-done((f32[128,768]{1,0:T(8,128)S(1)}, f32[128,768]{1,0:T(8,128)S(1)}, u32[]{:S(2)}, u32[]{:S(2)}) %collective-permute-start.7) | collective-permute-done | bytes 393248 | tf_op jit(solution)/shard_map/ppermute | solution.py:362
  283.8 0.6 join.3.b_ref
  284.4 0.1 collective-permute-start.8
  284.5 0.0 collective-permute-done.5.got_ref
  284.6 0.6 join.2.a_ref
  285.2 1.4 collective-permute-start.6
  286.6 1.7 place.2.rest_0_
  288.3 8.3 %collective-permute-done.8.b_ref = f32[256,768]{1,0:T(8,128)S(1)} collective-permute-done((f32[256,768]{1,0:T(8,128)S(1)}, f32[256,768]{1,0:T(8,128)S(1)}, u32[]{:S(2)}, u32[]{:S(2)}) %collective-permute-start.8) | collective-permute-done | bytes 786464 | tf_op jit(solution)/shard_map/ppermute | solution.py:362
  296.5 0.7 collective-permute-done.6.a_ref
  297.2 1.7 place.3
  (1 shorter events, 0.0 us)
Async XLA Ops:
  170.4 38.5 %copy-start = (bf16[2048,768]{1,0:T(8,128)(2,1)S(1)}, bf16[2048,768]{1,0:T(8,128)(2,1)}, u32[]{:S(2)}) copy-start(bf16[2048,768]{1,0:T(8,128)(2,1)} %vec_ref.3) | copy-start | bytes 9437188
  214.5 12.3 %collective-permute-start = (f32[8,25,8,128]{3,2,1,0:T(8,128)S(1)}, f32[8,25,8,128]{3,2,1,0:T(8,128)S(1)}, u32[]{:S(2)}, u32[]{:S(2)}) collective-permute-start(f32[8,25,8,128]{3,2,1,0:T(8,128)S(1)} %get-tuple-element.22), channel_id=1, source_target_pairs={{0,64},{1,193},{2,66},{3,195},{4,68},{5,197},{6,70},{7,199},{8,72}... | collective-permute-start | bytes 2457608 | tf_op jit(solution)/shard_map/ppermute | solution.py:362
  215.1 13.7 %collective-permute-start.2 = (f32[8,25,8,128]{3,2,1,0:T(8,128)S(1)}, f32[8,25,8,128]{3,2,1,0:T(8,128)S(1)}, u32[]{:S(2)}, u32[]{:S(2)}) collective-permute-start(f32[8,25,8,128]{3,2,1,0:T(8,128)S(1)} %get-tuple-element.26), channel_id=1, source_target_pairs={{0,8},{1,57},{2,10},{3,59},{4,12},{5,61},{6,14},{7,63},{8,0},{9,17... | collective-permute-start | bytes 2457608 | tf_op jit(solution)/shard_map/ppermute | solution.py:362
  227.4 8.0 %collective-permute-start.1 = (f32[4,25,8,128]{3,2,1,0:T(8,128)S(1)}, f32[4,25,8,128]{3,2,1,0:T(8,128)S(1)}, u32[]{:S(2)}, u32[]{:S(2)}) collective-permute-start(f32[4,25,8,128]{3,2,1,0:T(8,128)S(1)} %get-tuple-element.24), channel_id=1, source_target_pairs={{0,8},{1,57},{2,10},{3,59},{4,12},{5,61},{6,14},{7,63},{8,0},{9,17... | collective-permute-start | bytes 1228808 | tf_op jit(solution)/shard_map/ppermute | solution.py:362
  229.4 8.0 %collective-permute-start.3 = (f32[4,25,8,128]{3,2,1,0:T(8,128)S(1)}, f32[4,25,8,128]{3,2,1,0:T(8,128)S(1)}, u32[]{:S(2)}, u32[]{:S(2)}) collective-permute-start(f32[4,25,8,128]{3,2,1,0:T(8,128)S(1)} %get-tuple-element.28), channel_id=1, source_target_pairs={{0,64},{1,193},{2,66},{3,195},{4,68},{5,197},{6,70},{7,199},{8,72}... | collective-permute-start | bytes 1228808 | tf_op jit(solution)/shard_map/ppermute | solution.py:362
  251.4 8.1 %collective-permute-start.4 = (f32[2,25,8,128]{3,2,1,0:T(8,128)S(1)}, f32[2,25,8,128]{3,2,1,0:T(8,128)S(1)}, u32[]{:S(2)}, u32[]{:S(2)}) collective-permute-start(f32[2,25,8,128]{3,2,1,0:T(8,128)S(1)} %four.1.sum_ref), channel_id=1, source_target_pairs={{0,24},{1,41},{2,26},{3,43},{4,28},{5,45},{6,30},{7,47},{8,48},{9,... | collective-permute-start | bytes 614408 | tf_op jit(solution)/shard_map/ppermute | solution.py:362
  276.0 7.9 %collective-permute-start.7 = (f32[128,768]{1,0:T(8,128)S(1)}, f32[128,768]{1,0:T(8,128)S(1)}, u32[]{:S(2)}, u32[]{:S(2)}) collective-permute-start(f32[128,768]{1,0:T(8,128)S(1)} %get-tuple-element.30.mine_ref), channel_id=1, source_target_pairs={{0,64},{1,193},{2,66},{3,195},{4,68},{5,197},{6,70},{7,199},{8,72}... | collective-permute-start | bytes 1179656 | tf_op jit(solution)/shard_map/ppermute | solution.py:362
  276.1 8.5 %collective-permute-start.5 = (f32[128,768]{1,0:T(8,128)S(1)}, f32[128,768]{1,0:T(8,128)S(1)}, u32[]{:S(2)}, u32[]{:S(2)}) collective-permute-start(f32[128,768]{1,0:T(8,128)S(1)} %get-tuple-element.29.mine_ref), channel_id=1, source_target_pairs={{0,8},{1,57},{2,10},{3,59},{4,12},{5,61},{6,14},{7,63},{8,0},{9,17... | collective-permute-start | bytes 1179656 | tf_op jit(solution)/shard_map/ppermute | solution.py:362
  284.4 12.1 %collective-permute-start.8 = (f32[256,768]{1,0:T(8,128)S(1)}, f32[256,768]{1,0:T(8,128)S(1)}, u32[]{:S(2)}, u32[]{:S(2)}) collective-permute-start(f32[256,768]{1,0:T(8,128)S(1)} %join.3.b_ref), channel_id=1, source_target_pairs={{0,8},{1,57},{2,10},{3,59},{4,12},{5,61},{6,14},{7,63},{8,0},{9,17... | collective-permute-start | bytes 2359304 | tf_op jit(solution)/shard_map/ppermute | solution.py:362
  285.2 12.1 %collective-permute-start.6 = (f32[256,768]{1,0:T(8,128)S(1)}, f32[256,768]{1,0:T(8,128)S(1)}, u32[]{:S(2)}, u32[]{:S(2)}) collective-permute-start(f32[256,768]{1,0:T(8,128)S(1)} %join.2.a_ref), channel_id=1, source_target_pairs={{0,64},{1,193},{2,66},{3,195},{4,68},{5,197},{6,70},{7,199},{8,72}... | collective-permute-start | bytes 2359304 | tf_op jit(solution)/shard_map/ppermute | solution.py:362

commit v4 on v3

--- a/solution.py
+++ b/solution.py
@@ -48,7 +48,15 @@
 
 def logit_block(k_ref, ok, t, g):
     block = k_ref[row_tile(t), lane_group(g)]
-    return jnp.where(ok != 0, jnp.log(block), block)
+    return jnp.where(ok, jnp.log(block), block)
+
+
+def within(peak, *pots):
+    for pot in pots:
+        pot = jnp.abs(pot)
+        for k in range(pot.shape[0] // 8):
+            peak = jnp.maximum(peak, pot[8 * k : 8 * k + 8, :])
+    return jnp.max(peak) <= LIM
 
 
 def row_lse_exact(k_ref, ok, pot_ref, out_ref):
@@ -89,7 +97,7 @@
     lax.fori_loop(0, tiles, tile, 0)
 
 
-def logits_kernel(_, cent_hbm, vec_hbm, k_ref, ok_ref, out_ref, lse_ref, cent_ref, vec_ref, sems):
+def logits_kernel(cent_hbm, vec_hbm, k_ref, peak_ref, out_ref, lse_ref, cent_ref, vec_ref, sems):
     cents, rows = k_ref.shape
     groups = rows // LANES
     step, chunk = cents // CHUNKS, rows // CHUNKS
@@ -128,10 +136,9 @@
                 total = total + fold(part)
             lse_ref[group : group + 1, :] = jnp.sum(total, axis=0, keepdims=True)
     lse_ref[...] = jnp.log(lse_ref[...])
-    ok = jnp.max(peak) <= LIM
-    ok_ref[0, 0] = ok.astype(jnp.int32)
-
-    @pl.when(jnp.logical_not(ok))
+    peak_ref[...] = peak
+
+    @pl.when(jnp.logical_not(within(peak)))
     def _():
         def tile(t, carry):
             at = row_tile(t)
@@ -143,16 +150,15 @@
             return carry
 
         lax.fori_loop(0, cents // LANES, tile, 0)
-        row_lse_exact(k_ref, 0, None, lse_ref)
+        row_lse_exact(k_ref, False, None, lse_ref)
 
     put_copies(out_ref, lse_ref[...])
 
 
-def row_kernel(log_target, got_ref, ok_ref, k_ref, out_ref, pot_ref, lse_ref):
+def row_kernel(log_target, got_ref, peak_ref, k_ref, out_ref, pot_ref, lse_ref):
     tiles, groups = k_ref.shape[0] // LANES, k_ref.shape[1] // LANES
     pot = log_target - combine_lse(got_ref[...])
-    ok = ok_ref[0, 0]
-    fast = jnp.logical_and(ok != 0, jnp.max(jnp.abs(pot)) <= LIM)
+    fast = within(peak_ref[...], pot)
 
     @pl.when(fast)
     def _():
@@ -169,16 +175,15 @@
     @pl.when(jnp.logical_not(fast))
     def _():
         pot_ref[...] = pot
-        row_lse_exact(k_ref, ok, pot_ref, lse_ref)
+        row_lse_exact(k_ref, within(peak_ref[...]), pot_ref, lse_ref)
 
     put_copies(out_ref, lse_ref[...])
 
 
-def col_kernel(got_ref, ok_ref, k_ref, out_ref, lse_ref):
+def col_kernel(got_ref, peak_ref, k_ref, out_ref, lse_ref):
     tiles, groups = k_ref.shape[0] // LANES, k_ref.shape[1] // LANES
     pot = -combine_lse(got_ref[...])
-    ok = ok_ref[0, 0]
-    fast = jnp.logical_and(ok != 0, jnp.max(jnp.abs(pot)) <= LIM)
+    fast = within(peak_ref[...], pot)
 
     @pl.when(fast)
     def _():
@@ -193,13 +198,13 @@
 
     @pl.when(jnp.logical_not(fast))
     def _():
-        col_lse_exact(k_ref, ok, pot, lse_ref)
+        col_lse_exact(k_ref, within(peak_ref[...]), pot, lse_ref)
 
     put_copies(out_ref, lse_ref[...])
 
 
 def half_kernel(
-    log_target, keep, bits_ref, cols_ref, rows_ref, ok_ref, k_ref, vec_ref,
+    log_target, keep, cols_ref, rows_ref, peak_ref, k_ref, vec_ref,
     a_ref, b_ref, *rest,
 ):
     scale_ref, plan_ref, mass_ref = rest[-3:]
@@ -209,10 +214,7 @@
     if not keep:
         rest[0][...] = row_pot
         rest[1][...] = col_pot
-    ok = ok_ref[0, 0]
-    fast = jnp.logical_and(
-        ok != 0, jnp.maximum(jnp.max(jnp.abs(col_pot)), jnp.max(jnp.abs(row_pot))) <= LIM
-    )
+    fast = within(peak_ref[...], col_pot, row_pot)
     scale_ref[...] = jnp.where(fast, jnp.exp(col_pot), col_pot)
     row_scale = jnp.exp(row_pot)
     blocks = a_ref.shape[0]
@@ -233,9 +235,10 @@
                 unit = jnp.where(lane == k, mass[at : at + 8, :], unit)
             mass_ref[spot * (LANES // BLOCK) + b] = unit
 
+    bits = position_bits()
     firsts = []
     for chain, which in enumerate((XB1, ZB1)):
-        bit = bits_ref[which] if keep else 1 - bits_ref[which]
+        bit = bits[which] if keep else 1 - bits[which]
         firsts.append((chain * 2 + bit) * tiles)
 
     def sums():
@@ -265,6 +268,7 @@
 
     @pl.when(jnp.logical_not(fast))
     def _():
+        ok = within(peak_ref[...])
         for chain, first in enumerate(firsts):
             def tile(t, carry):
                 shift = lane_to_sublane(scale_ref[pl.ds(first + t, 1), :])
@@ -280,10 +284,10 @@
         sums()
 
 
-def fold_kernel(which, bits_ref, keep_ref, got_ref, send_ref, kept_ref):
+def fold_kernel(which, keep_ref, got_ref, send_ref, kept_ref):
     half = send_ref.shape[0]
-    mine = bits_ref[which] * half
-    other = (1 - bits_ref[which]) * half
+    bit = position_bits()[which]
+    mine, other = bit * half, (1 - bit) * half
     for b in range(half):
         send_ref[b] = keep_ref[other + b] + got_ref[other + b]
         kept_ref[b] = keep_ref[mine + b] + got_ref[mine + b]
@@ -322,19 +326,20 @@
         b_ref[at, :] = got_ref[p, 1]
 
 
-def join_kernel(which, bits_ref, mine_ref, got_ref, out_ref):
+def join_kernel(which, mine_ref, got_ref, out_ref):
     size = mine_ref.shape[0]
-    bit = bits_ref[which]
+    bit = position_bits()[which]
     out_ref[pl.ds(pl.multiple_of(bit * size, size), size), :] = mine_ref[...]
     out_ref[pl.ds(pl.multiple_of((1 - bit) * size, size), size), :] = got_ref[...]
 
 
-def place_kernel(own, bits_ref, a_ref, b_ref, *rest):
+def place_kernel(own, a_ref, b_ref, *rest):
     out_ref, sems = rest[-2:]
     size = a_ref.shape[0]
+    bits = position_bits()
     copies = []
     for chain, (which, part_ref) in enumerate(((XB1, a_ref), (ZB1, b_ref))):
-        side = bits_ref[which] if own else 1 - bits_ref[which]
+        side = bits[which] if own else 1 - bits[which]
         at = pl.ds(pl.multiple_of((2 * chain + side) * size, size), size)
         copies.append(pltpu.make_async_copy(part_ref, out_ref.at[at, :], sems.at[chain]))
     for copy in copies:
@@ -383,8 +388,11 @@
 
 
 def position_bits():
-    x, z = place(lax.axis_index("rows"), lax.axis_index("cols") % 2)
-    return jnp.stack([(x ^ (x >> 1)) & 1, x >> 1, ((z + 1) >> 1) & 1, (0xB4 >> z) & 1]).astype(jnp.int32)
+    core = lax.axis_index("cols") & 1
+    row = lax.axis_index("rows")
+    x = ((row >> 3) + (XS - 1) * core) & (XS - 1)
+    z = (row + (ZS - 1) * core) & (ZS - 1)
+    return (x ^ (x >> 1)) & 1, x >> 1, ((z + 1) >> 1) & 1, (0xB4 >> z) & 1
 
 
 def quads(n_cols):
@@ -403,46 +411,46 @@
     )
 
 
-def halve(which, bits, keep, got):
+def halve(which, keep, got):
     half = jax.ShapeDtypeStruct((keep.shape[0] // 2, *keep.shape[1:]), F32)
     return pl.pallas_call(
         functools.partial(fold_kernel, which),
         out_shape=(half, half),
-        in_specs=[smem(), vmem(), vmem()],
+        in_specs=[vmem(), vmem()],
         out_specs=(vmem(), vmem()),
         compiler_params=params(4),
         name="fold",
-    )(bits, keep, got)
-
-
-def join(which, bits, mine, got):
+    )(keep, got)
+
+
+def join(which, mine, got):
     return pl.pallas_call(
         functools.partial(join_kernel, which),
         out_shape=jax.ShapeDtypeStruct((2 * mine.shape[0], *mine.shape[1:]), F32),
-        in_specs=[smem(), vmem(), vmem()],
+        in_specs=[vmem(), vmem()],
         out_specs=vmem(),
         compiler_params=params(4),
         name="join",
-    )(bits, mine, got)
-
-
-def put(own, bits, a, b, cents, *before):
+    )(mine, got)
+
+
+def put(own, a, b, cents, *before):
     return pl.pallas_call(
         functools.partial(place_kernel, own),
         out_shape=jax.ShapeDtypeStruct((cents, a.shape[1]), F32),
-        in_specs=[smem(), vmem(), vmem()] + [hbm()] * len(before),
+        in_specs=[vmem(), vmem()] + [hbm()] * len(before),
         out_specs=hbm(),
         scratch_shapes=[pltpu.SemaphoreType.DMA((2,))],
-        input_output_aliases={3: 0} if before else {},
+        input_output_aliases={2: 0} if before else {},
         compiler_params=params(4),
         name="place",
-    )(bits, a, b, *before)
-
-
-def mean_over_rows(bits, send_a, keep_a, send_b, keep_b, cents, width):
+    )(a, b, *before)
+
+
+def mean_over_rows(send_a, keep_a, send_b, keep_b, cents, width):
     got_a, got_b = exchange(send_a, x_first), exchange(send_b, z_first)
-    send_a, keep_a = halve(ZB1, bits, keep_a, got_a)
-    send_b, keep_b = halve(XB1, bits, keep_b, got_b)
+    send_a, keep_a = halve(ZB1, keep_a, got_a)
+    send_b, keep_b = halve(XB1, keep_b, got_b)
     got_a, got_b = exchange(send_a, z_first), exchange(send_b, x_first)
     block = keep_a.shape[1:]
     quarter = pl.pallas_call(
@@ -479,10 +487,10 @@
         name="part",
     )(trade(mean))
     got_a, got_b = exchange(mine_a, z_first), exchange(mine_b, x_first)
-    mine_a = join(ZB1, bits, mine_a, got_a)
-    mine_b = join(XB1, bits, mine_b, got_b)
+    mine_a = join(ZB1, mine_a, got_a)
+    mine_b = join(XB1, mine_b, got_b)
     got_a, got_b = exchange(mine_a, x_first), exchange(mine_b, z_first)
-    return put(False, bits, got_a, got_b, cents, put(True, bits, mine_a, mine_b, cents))
+    return put(False, got_a, got_b, cents, put(True, mine_a, mine_b, cents))
 
 
 def vmem():
@@ -491,10 +499,6 @@
 
 def hbm():
     return pl.BlockSpec(memory_space=pltpu.HBM)
-
-
-def smem():
-    return pl.BlockSpec(memory_space=pltpu.SMEM)
 
 
 def pinned(x):
@@ -512,19 +516,17 @@
     log_target = math.log(rows * n_rows / (cents * n_cols))
     groups, tiles = rows // LANES, cents // LANES
     kept = pltpu.VMEM((cents, rows), F32)
-    ok_type = jax.ShapeDtypeStruct((1, 1), jnp.int32)
+    peak_type = jax.ShapeDtypeStruct((8, LANES), F32)
     row_parts = jax.ShapeDtypeStruct((n_cols, groups, LANES), F32)
     col_parts = jax.ShapeDtypeStruct((n_rows, tiles, LANES), F32)
     row_scratch = pltpu.VMEM((groups, LANES), F32)
     col_scratch = pltpu.VMEM((tiles, LANES), F32)
 
-    bits = position_bits()
-
-    kernel, ok, part = pl.pallas_call(
+    kernel, peak, part = pl.pallas_call(
         logits_kernel,
-        out_shape=(kept, ok_type, row_parts),
-        in_specs=[smem(), hbm(), hbm()],
-        out_specs=(vmem(), smem(), vmem()),
+        out_shape=(kept, peak_type, row_parts),
+        in_specs=[hbm(), hbm()],
+        out_specs=(vmem(), vmem(), vmem()),
         scratch_shapes=[
             row_scratch,
             pltpu.VMEM((cents, width), jnp.bfloat16),
@@ -533,29 +535,29 @@
         ],
         compiler_params=params(24),
         name="logits",
-    )(bits, *(pltpu.with_memory_space_constraint(x, pltpu.HBM) for x in (centroids, vectors)))
+    )(*(pltpu.with_memory_space_constraint(x, pltpu.HBM) for x in (centroids, vectors)))
 
     for step in range(ITERS):
         row_got = lax.all_to_all(part, "cols", 0, 0, tiled=True)
         part = pl.pallas_call(
             col_kernel,
             out_shape=col_parts,
-            in_specs=[vmem(), smem(), vmem()],
+            in_specs=[vmem(), vmem(), vmem()],
             out_specs=vmem(),
             scratch_shapes=[col_scratch],
             compiler_params=params(4),
             name="col_step",
-        )(row_got, ok, pinned(kernel))
+        )(row_got, peak, pinned(kernel))
         col_got = lax.all_to_all(part, "rows", 0, 0, tiled=True)
         part = pl.pallas_call(
             functools.partial(row_kernel, log_target),
             out_shape=row_parts,
-            in_specs=[vmem(), smem(), vmem()],
+            in_specs=[vmem(), vmem(), vmem()],
             out_specs=vmem(),
             scratch_shapes=[col_scratch, row_scratch],
             compiler_params=params(4),
             name="row_step",
-        )(col_got, ok, pinned(kernel))
+        )(col_got, peak, pinned(kernel))
     row_got = lax.all_to_all(part, "cols", 0, 0, tiled=True)
 
     part_units = PARTS * (width // LANES) + 1
@@ -566,7 +568,7 @@
         return pl.pallas_call(
             functools.partial(half_kernel, log_target, keep),
             out_shape=(halves, halves) + (() if keep else pots),
-            in_specs=[smem(), vmem(), vmem(), smem(), vmem(), vmem()],
+            in_specs=[vmem()] * 5,
             out_specs=(vmem(),) * (2 if keep else 4),
             scratch_shapes=[
                 col_scratch,
@@ -578,11 +580,11 @@
                 flops=rows * cents * width, bytes_accessed=8 * MIB, transcendentals=0
             ),
             name="keep" if keep else "send",
-        )(bits, col_got, row_got, ok, pinned(kernel), vectors)
+        )(col_got, row_got, peak, pinned(kernel), vectors)
 
     send_a, send_b, row_pot, col_pot = half(False)
     keep_a, keep_b = half(True)
-    new_centroids = mean_over_rows(bits, send_a, keep_a, send_b, keep_b, cents, width)
+    new_centroids = mean_over_rows(send_a, keep_a, send_b, keep_b, cents, width)
     return (new_centroids, row_pot.reshape(rows), col_pot.reshape(cents))
 
 

time: 301 us -> 293 us (0.973)
  Pallas kernels: 143 us -> 133 us
  transfers between devices with their start and end apart: 9 -> 9, of which waited for: 7 -> 7; matrix products, arithmetic and copies ran while one was open for 0% -> 0% of each run, Pallas kernels for 3% -> 2%
where the time goes in v4:
time: 293 us; the launch traced here: 292 us
  Pallas kernels  133 us (45%)
  blocking collectives  111 us (38%)
  waiting for transfers between devices  38.6 us (13%)
  starting transfers between devices  7.77 us (3%)
    pallas_call x3, Pallas kernels, per_device(): pl.pallas_call(functools.partial(row_kernel, log_target), out_shape=row_p...  89.6 us
    all_to_all x3, blocking collectives, per_device(): col_got = lax.all_to_all(part, 'rows', 0, 0, tiled=True)  49.1 us
    ppermute x9, waiting for transfers between devices, exchange(): lax.ppermute(x, ('rows', 'cols'), pairs(partner, lax.axis_size('cols')))  38.6 us
    all_to_all x4, blocking collectives, per_device(): row_got = lax.all_to_all(part, 'cols', 0, 0, tiled=True)  32.9 us
    all_to_all x2, blocking collectives, trade(): lax.all_to_all(x, ('rows', 'cols'), 0, 0, tiled=True, axis_index_groups=q...  29.1 us
    pallas_call x1, Pallas kernels, per_device(): pl.pallas_call(logits_kernel, out_shape=(kept, peak_type, row_parts), in_...  21.1 us
    pallas_call x3, Pallas kernels, per_device(): pl.pallas_call(col_kernel, out_shape=col_parts, in_specs=[vmem(), vmem(),...  11.1 us
    pallas_call x2, Pallas kernels, half(): pl.pallas_call(functools.partial(half_kernel, log_target, keep), out_shap...  8.44 us
  transfers between devices with their start and end apart: 9, of which 7 were waited for; matrix products, arithmetic and copies ran while one was open for 0% of the time, Pallas kernels for 2%

profile of v4, /device:TPU:8, one launch (start us, length us, event | category | flops | bytes accessed | tf_op | source)
XLA Modules:
  0.0 291.5 jit_solution(3806985471831758895)
XLA Ops:
  0.6 21.1 %logits.1 = (f32[1024,2048]{1,0:T(8,128)S(1)}, f32[8,128]{1,0:T(8,128)S(1)}, f32[8,16,128]{2,1,0:T(8,128)S(1)}) custom-call(bf16[1024,768]{1,0:T(8,128)(2,1)} %cent_hbm.1, bf16[2048,768]{1,0:T(8,128)(2,1)} %vec_ref.3), custom_call_target="tpu_custom_call" | custom-call | tf_op jit(solution)/shard_map/logits/pallas_call | solution.py:525
  21.7 8.9 %all_to_all.45.got_ref = f32[8,16,128]{2,1,0:T(8,128)S(1)} all-to-all(f32[8,16,128]{2,1,0:T(8,128)S(1)} %get-tuple-element.18), channel_id=1, replica_groups=mesh['rows'=32,'cols'=8] {'cols'}, dimensions={0} | all-to-all | bytes 131072 | tf_op jit(solution)/shard_map/all_to_all | solution.py:541
  30.6 3.7 %col_step.3 = f32[32,8,128]{2,1,0:T(8,128)S(1)} custom-call(f32[8,16,128]{2,1,0:T(8,128)S(1)} %all_to_all.45.got_ref, f32[8,128]{1,0:T(8,128)S(1)} %get-tuple-element.19.peak_ref, f32[1024,2048]{1,0:T(8,128)S(1)} %get-tuple-element.20.k_ref), custom_call_target="tpu_custom_call" | custom-call | tf_op jit(solution)/shard_map/col_step/pallas_call | solution.py:542
  34.3 21.4 %all_to_all.46.got_ref = f32[32,8,128]{2,1,0:T(8,128)S(1)} all-to-all(f32[32,8,128]{2,1,0:T(8,128)S(1)} %col_step.3), channel_id=1, replica_groups=mesh['rows'=32,'cols'=8] {'rows'}, dimensions={0} | all-to-all | bytes 262144 | tf_op jit(solution)/shard_map/all_to_all | solution.py:551
  55.7 29.8 %row_step.3 = f32[8,16,128]{2,1,0:T(8,128)S(1)} custom-call(f32[32,8,128]{2,1,0:T(8,128)S(1)} %all_to_all.46.got_ref, f32[8,128]{1,0:T(8,128)S(1)} %get-tuple-element.19.peak_ref, f32[1024,2048]{1,0:T(8,128)S(1)} %get-tuple-element.20.k_ref), custom_call_target="tpu_custom_call" | custom-call | tf_op jit(solution)/shard_map/row_step/pallas_call | solution.py:552
  85.5 8.0 %all_to_all.47.got_ref = f32[8,16,128]{2,1,0:T(8,128)S(1)} all-to-all(f32[8,16,128]{2,1,0:T(8,128)S(1)} %row_step.3), channel_id=1, replica_groups=mesh['rows'=32,'cols'=8] {'cols'}, dimensions={0} | all-to-all | bytes 131072 | tf_op jit(solution)/shard_map/all_to_all | solution.py:541
  93.5 3.7 %col_step.4 = f32[32,8,128]{2,1,0:T(8,128)S(1)} custom-call(f32[8,16,128]{2,1,0:T(8,128)S(1)} %all_to_all.47.got_ref, f32[8,128]{1,0:T(8,128)S(1)} %get-tuple-element.19.peak_ref, f32[1024,2048]{1,0:T(8,128)S(1)} %get-tuple-element.20.k_ref), custom_call_target="tpu_custom_call" | custom-call | tf_op jit(solution)/shard_map/col_step/pallas_call | solution.py:542
  97.2 13.9 %all_to_all.48.got_ref = f32[32,8,128]{2,1,0:T(8,128)S(1)} all-to-all(f32[32,8,128]{2,1,0:T(8,128)S(1)} %col_step.4), channel_id=1, replica_groups=mesh['rows'=32,'cols'=8] {'rows'}, dimensions={0} | all-to-all | bytes 262144 | tf_op jit(solution)/shard_map/all_to_all | solution.py:551
  111.0 30.0 %row_step.4 = f32[8,16,128]{2,1,0:T(8,128)S(1)} custom-call(f32[32,8,128]{2,1,0:T(8,128)S(1)} %all_to_all.48.got_ref, f32[8,128]{1,0:T(8,128)S(1)} %get-tuple-element.19.peak_ref, f32[1024,2048]{1,0:T(8,128)S(1)} %get-tuple-element.20.k_ref), custom_call_target="tpu_custom_call" | custom-call | tf_op jit(solution)/shard_map/row_step/pallas_call | solution.py:552
  141.0 8.0 %all_to_all.49.got_ref = f32[8,16,128]{2,1,0:T(8,128)S(1)} all-to-all(f32[8,16,128]{2,1,0:T(8,128)S(1)} %row_step.4), channel_id=1, replica_groups=mesh['rows'=32,'cols'=8] {'cols'}, dimensions={0} | all-to-all | bytes 131072 | tf_op jit(solution)/shard_map/all_to_all | solution.py:541
  149.0 3.7 %col_step.5 = f32[32,8,128]{2,1,0:T(8,128)S(1)} custom-call(f32[8,16,128]{2,1,0:T(8,128)S(1)} %all_to_all.49.got_ref, f32[8,128]{1,0:T(8,128)S(1)} %get-tuple-element.19.peak_ref, f32[1024,2048]{1,0:T(8,128)S(1)} %get-tuple-element.20.k_ref), custom_call_target="tpu_custom_call" | custom-call | tf_op jit(solution)/shard_map/col_step/pallas_call | solution.py:542
  152.7 13.9 %all_to_all.50.got_ref.cols_ref = f32[32,8,128]{2,1,0:T(8,128)S(1)} all-to-all(f32[32,8,128]{2,1,0:T(8,128)S(1)} %col_step.5), channel_id=1, replica_groups=mesh['rows'=32,'cols'=8] {'rows'}, dimensions={0} | all-to-all | bytes 262144 | tf_op jit(solution)/shard_map/all_to_all | solution.py:551
  166.6 0.0 copy-start
  166.6 29.8 %row_step.5 = f32[8,16,128]{2,1,0:T(8,128)S(1)} custom-call(f32[32,8,128]{2,1,0:T(8,128)S(1)} %all_to_all.50.got_ref.cols_ref, f32[8,128]{1,0:T(8,128)S(1)} %get-tuple-element.19.peak_ref, f32[1024,2048]{1,0:T(8,128)S(1)} %get-tuple-element.20.k_ref), custom_call_target="tpu_custom_call" | custom-call | tf_op jit(solution)/shard_map/row_step/pallas_call | solution.py:552
  196.4 8.0 %all_to_all.51.rows_ref = f32[8,16,128]{2,1,0:T(8,128)S(1)} all-to-all(f32[8,16,128]{2,1,0:T(8,128)S(1)} %row_step.5), channel_id=1, replica_groups=mesh['rows'=32,'cols'=8] {'cols'}, dimensions={0} | all-to-all | bytes 131072 | tf_op jit(solution)/shard_map/all_to_all | solution.py:561
  204.4 0.0 copy-done
  204.4 4.4 %send.1 = (f32[8,25,8,128]{3,2,1,0:T(8,128)S(1)}, f32[8,25,8,128]{3,2,1,0:T(8,128)S(1)}, f32[16,128]{1,0:T(8,128)}, f32[8,128]{1,0:T(8,128)}) custom-call(f32[32,8,128]{2,1,0:T(8,128)S(1)} %all_to_all.50.got_ref.cols_ref, f32[8,16,128]{2,1,0:T(8,128)S(1)} %all_to_all.51.rows_ref, f32[8,128]{1,0:T(8,128)S(1)} %get-tuple-element.19.peak_ref, ...), custom_call_target="tpu_custom_call" | custom-call | flops 1610612736 | bytes 8388608 | tf_op jit(solution)/shard_map/send/pallas_call | solution.py:568
  208.8 0.6 collective-permute-start
  209.4 1.3 collective-permute-start.2
  210.7 4.0 %keep.1 = (f32[8,25,8,128]{3,2,1,0:T(8,128)S(1)}, f32[8,25,8,128]{3,2,1,0:T(8,128)S(1)}) custom-call(f32[32,8,128]{2,1,0:T(8,128)S(1)} %all_to_all.50.got_ref.cols_ref, f32[8,16,128]{2,1,0:T(8,128)S(1)} %all_to_all.51.rows_ref, f32[8,128]{1,0:T(8,128)S(1)} %get-tuple-element.19.peak_ref, f32[1024,2048]{1,0:T(8,128)S(1)} %get-tuple-element.20.k_ref, ...), custom_call_target="tpu_custom_call" | custom-call | flops 1610612736 | bytes 8388608 | tf_op jit(solution)/shard_map/keep/pallas_call | solution.py:568
  214.7 6.4 %collective-permute-done.got_ref = f32[8,25,8,128]{3,2,1,0:T(8,128)S(1)} collective-permute-done((f32[8,25,8,128]{3,2,1,0:T(8,128)S(1)}, f32[8,25,8,128]{3,2,1,0:T(8,128)S(1)}, u32[]{:S(2)}, u32[]{:S(2)}) %collective-permute-start) | collective-permute-done | bytes 819232 | tf_op jit(solution)/shard_map/ppermute | solution.py:367
  221.1 0.1 fold.2
  221.2 1.3 collective-permute-start.1
  222.6 0.0 collective-permute-done.2.got_ref
  222.6 0.1 fold.3
  222.7 0.7 collective-permute-start.3
  223.4 5.9 %collective-permute-done.1.got_a_ref = f32[4,25,8,128]{3,2,1,0:T(8,128)S(1)} collective-permute-done((f32[4,25,8,128]{3,2,1,0:T(8,128)S(1)}, f32[4,25,8,128]{3,2,1,0:T(8,128)S(1)}, u32[]{:S(2)}, u32[]{:S(2)}) %collective-permute-start.1) | collective-permute-done | bytes 409632 | tf_op jit(solution)/shard_map/ppermute | solution.py:367
  229.3 1.4 collective-permute-done.3.got_b_ref
  230.7 0.1 quarter.1
  230.8 13.8 %all_to_all.52.got_ref = f32[4,2,25,8,128]{4,3,2,1,0:T(8,128)S(1)} all-to-all(f32[4,2,25,8,128]{4,3,2,1,0:T(8,128)S(1)} %quarter.1), channel_id=1, replica_groups={{0,56,192,248},{8,16,200,208},{24,32,216,224},{48,40,240,232},{64,120,1..., dimensions={0} | all-to-all | bytes 1638400 | tf_op jit(solution)/shard_map/all_to_all | solution.py:409
  244.6 1.6 collective-permute-start.4
  246.3 8.2 %collective-permute-done.4.got_ref = f32[2,25,8,128]{3,2,1,0:T(8,128)S(1)} collective-permute-done((f32[2,25,8,128]{3,2,1,0:T(8,128)S(1)}, f32[2,25,8,128]{3,2,1,0:T(8,128)S(1)}, u32[]{:S(2)}, u32[]{:S(2)}) %collective-permute-start.4) | collective-permute-done | bytes 204832 | tf_op jit(solution)/shard_map/ppermute | solution.py:367
  254.5 0.1 mean.1
  254.6 15.3 %all_to_all.53.got_ref = f32[4,2,32,768]{3,2,1,0:T(8,128)S(1)} all-to-all(f32[4,2,32,768]{3,2,1,0:T(8,128)S(1)} %mean.1), channel_id=1, replica_groups={{0,56,192,248},{8,16,200,208},{24,32,216,224},{48,40,240,232},{64,120,1..., dimensions={0} | all-to-all | bytes 1572864 | tf_op jit(solution)/shard_map/all_to_all | solution.py:409
  269.9 0.1 part.1
  270.0 0.1 collective-permute-start.7
  270.1 0.1 collective-permute-start.5
  270.2 7.7 %collective-permute-done.7.got_ref = f32[128,768]{1,0:T(8,128)S(1)} collective-permute-done((f32[128,768]{1,0:T(8,128)S(1)}, f32[128,768]{1,0:T(8,128)S(1)}, u32[]{:S(2)}, u32[]{:S(2)}) %collective-permute-start.7) | collective-permute-done | bytes 393248 | tf_op jit(solution)/shard_map/ppermute | solution.py:367
  277.8 0.1 join.3.b_ref
  277.9 0.1 collective-permute-start.8
  278.0 0.0 collective-permute-done.5.got_ref
  278.0 0.1 join.2.a_ref
  278.1 1.9 collective-permute-start.6
  280.0 1.2 place.2.rest_0_
  281.2 8.8 %collective-permute-done.8.b_ref = f32[256,768]{1,0:T(8,128)S(1)} collective-permute-done((f32[256,768]{1,0:T(8,128)S(1)}, f32[256,768]{1,0:T(8,128)S(1)}, u32[]{:S(2)}, u32[]{:S(2)}) %collective-permute-start.8) | collective-permute-done | bytes 786464 | tf_op jit(solution)/shard_map/ppermute | solution.py:367
  290.0 0.2 collective-permute-done.6.a_ref
  290.2 1.2 place.3
  (1 shorter events, 0.0 us)
Async XLA Ops:
  166.6 37.8 %copy-start = (bf16[2048,768]{1,0:T(8,128)(2,1)S(1)}, bf16[2048,768]{1,0:T(8,128)(2,1)}, u32[]{:S(2)}) copy-start(bf16[2048,768]{1,0:T(8,128)(2,1)} %vec_ref.3) | copy-start | bytes 9437188
  208.8 12.3 %collective-permute-start = (f32[8,25,8,128]{3,2,1,0:T(8,128)S(1)}, f32[8,25,8,128]{3,2,1,0:T(8,128)S(1)}, u32[]{:S(2)}, u32[]{:S(2)}) collective-permute-start(f32[8,25,8,128]{3,2,1,0:T(8,128)S(1)} %get-tuple-element.22), channel_id=1, source_target_pairs={{0,64},{1,193},{2,66},{3,195},{4,68},{5,197},{6,70},{7,199},{8,72}... | collective-permute-start | bytes 2457608 | tf_op jit(solution)/shard_map/ppermute | solution.py:367
  209.4 13.1 %collective-permute-start.2 = (f32[8,25,8,128]{3,2,1,0:T(8,128)S(1)}, f32[8,25,8,128]{3,2,1,0:T(8,128)S(1)}, u32[]{:S(2)}, u32[]{:S(2)}) collective-permute-start(f32[8,25,8,128]{3,2,1,0:T(8,128)S(1)} %get-tuple-element.26), channel_id=1, source_target_pairs={{0,8},{1,57},{2,10},{3,59},{4,12},{5,61},{6,14},{7,63},{8,0},{9,17... | collective-permute-start | bytes 2457608 | tf_op jit(solution)/shard_map/ppermute | solution.py:367
  221.2 8.0 %collective-permute-start.1 = (f32[4,25,8,128]{3,2,1,0:T(8,128)S(1)}, f32[4,25,8,128]{3,2,1,0:T(8,128)S(1)}, u32[]{:S(2)}, u32[]{:S(2)}) collective-permute-start(f32[4,25,8,128]{3,2,1,0:T(8,128)S(1)} %get-tuple-element.24), channel_id=1, source_target_pairs={{0,8},{1,57},{2,10},{3,59},{4,12},{5,61},{6,14},{7,63},{8,0},{9,17... | collective-permute-start | bytes 1228808 | tf_op jit(solution)/shard_map/ppermute | solution.py:367
  222.7 8.0 %collective-permute-start.3 = (f32[4,25,8,128]{3,2,1,0:T(8,128)S(1)}, f32[4,25,8,128]{3,2,1,0:T(8,128)S(1)}, u32[]{:S(2)}, u32[]{:S(2)}) collective-permute-start(f32[4,25,8,128]{3,2,1,0:T(8,128)S(1)} %get-tuple-element.28), channel_id=1, source_target_pairs={{0,64},{1,193},{2,66},{3,195},{4,68},{5,197},{6,70},{7,199},{8,72}... | collective-permute-start | bytes 1228808 | tf_op jit(solution)/shard_map/ppermute | solution.py:367
  244.6 9.8 %collective-permute-start.4 = (f32[2,25,8,128]{3,2,1,0:T(8,128)S(1)}, f32[2,25,8,128]{3,2,1,0:T(8,128)S(1)}, u32[]{:S(2)}, u32[]{:S(2)}) collective-permute-start(f32[2,25,8,128]{3,2,1,0:T(8,128)S(1)} %four.1.sum_ref), channel_id=1, source_target_pairs={{0,24},{1,41},{2,26},{3,43},{4,28},{5,45},{6,30},{7,47},{8,48},{9,... | collective-permute-start | bytes 614408 | tf_op jit(solution)/shard_map/ppermute | solution.py:367
  270.0 7.9 %collective-permute-start.7 = (f32[128,768]{1,0:T(8,128)S(1)}, f32[128,768]{1,0:T(8,128)S(1)}, u32[]{:S(2)}, u32[]{:S(2)}) collective-permute-start(f32[128,768]{1,0:T(8,128)S(1)} %get-tuple-element.30.mine_ref), channel_id=1, source_target_pairs={{0,64},{1,193},{2,66},{3,195},{4,68},{5,197},{6,70},{7,199},{8,72}... | collective-permute-start | bytes 1179656 | tf_op jit(solution)/shard_map/ppermute | solution.py:367
  270.1 7.9 %collective-permute-start.5 = (f32[128,768]{1,0:T(8,128)S(1)}, f32[128,768]{1,0:T(8,128)S(1)}, u32[]{:S(2)}, u32[]{:S(2)}) collective-permute-start(f32[128,768]{1,0:T(8,128)S(1)} %get-tuple-element.29.mine_ref), channel_id=1, source_target_pairs={{0,8},{1,57},{2,10},{3,59},{4,12},{5,61},{6,14},{7,63},{8,0},{9,17... | collective-permute-start | bytes 1179656 | tf_op jit(solution)/shard_map/ppermute | solution.py:367
  277.9 12.1 %collective-permute-start.8 = (f32[256,768]{1,0:T(8,128)S(1)}, f32[256,768]{1,0:T(8,128)S(1)}, u32[]{:S(2)}, u32[]{:S(2)}) collective-permute-start(f32[256,768]{1,0:T(8,128)S(1)} %join.3.b_ref), channel_id=1, source_target_pairs={{0,8},{1,57},{2,10},{3,59},{4,12},{5,61},{6,14},{7,63},{8,0},{9,17... | collective-permute-start | bytes 2359304 | tf_op jit(solution)/shard_map/ppermute | solution.py:367
  278.1 12.1 %collective-permute-start.6 = (f32[256,768]{1,0:T(8,128)S(1)}, f32[256,768]{1,0:T(8,128)S(1)}, u32[]{:S(2)}, u32[]{:S(2)}) collective-permute-start(f32[256,768]{1,0:T(8,128)S(1)} %join.2.a_ref), channel_id=1, source_target_pairs={{0,64},{1,193},{2,66},{3,195},{4,68},{5,197},{6,70},{7,199},{8,72}... | collective-permute-start | bytes 2359304 | tf_op jit(solution)/shard_map/ppermute | solution.py:367

commit v5 on v4

--- a/solution.py
+++ b/solution.py
@@ -13,6 +13,7 @@
 LIM = 40.0
 MIB = 1024 * 1024
 F32 = jnp.float32
+LOG2E = math.log2(math.e)
 XS, ZS = 4, 8
 BLOCK = 32
 PARTS = BLOCK // 8
@@ -115,26 +116,33 @@
     for copy in vec_copies[:1] + cent_copies + vec_copies[1:]:
         copy.start()
 
-    peak = jnp.zeros((8, LANES), F32)
-    for c in range(CHUNKS):
+    def dots(c):
         vec_copies[c].wait()
         if c == 0:
             for copy in cent_copies:
                 copy.wait()
-        block = lax.dot_general(
+        return lax.dot_general(
             cent_ref[...], vec_ref[c * chunk : (c + 1) * chunk, :],
             (((1,), (1,)), ((), ())), preferred_element_type=F32,
         )
+
+    peak = jnp.zeros((8, LANES), F32)
+    ahead = dots(0)
+    for c in range(CHUNKS):
+        block = ahead
+        if c + 1 < CHUNKS:
+            ahead = dots(c + 1)
         for g in range(chunk // LANES):
             group = c * (chunk // LANES) + g
             total = jnp.zeros((8, LANES), F32)
             for t in range(cents // LANES):
-                part = 4.0 * block[t * LANES : (t + 1) * LANES, lane_group(g)]
+                part = block[t * LANES : (t + 1) * LANES, lane_group(g)]
                 peak = jnp.maximum(peak, jnp.max(jnp.abs(part).reshape(LANES // 8, 8, LANES), axis=0))
-                part = jnp.exp(part)
+                part = jnp.exp2(part * (4.0 * LOG2E))
                 k_ref[t * LANES : (t + 1) * LANES, lane_group(group)] = part
                 total = total + fold(part)
             lse_ref[group : group + 1, :] = jnp.sum(total, axis=0, keepdims=True)
+    peak = 4.0 * peak
     lse_ref[...] = jnp.log(lse_ref[...])
     peak_ref[...] = peak
 
@@ -203,29 +211,37 @@
     put_copies(out_ref, lse_ref[...])
 
 
-def half_kernel(
-    log_target, keep, cols_ref, rows_ref, peak_ref, k_ref, vec_ref,
-    a_ref, b_ref, *rest,
-):
-    scale_ref, plan_ref, mass_ref = rest[-3:]
+def sums_kernel(log_target, flips, *refs):
+    first_call = log_target is not None
+    cols_ref, rows_ref, peak_ref, k_ref, vec_ref, a_ref, b_ref = refs[:7]
+    plan_ref, scale_ref = refs[-2:]
     groups = k_ref.shape[1] // LANES
-    col_pot = log_target - combine_lse(cols_ref[...])
-    row_pot = -combine_lse(rows_ref[...])
-    if not keep:
-        rest[0][...] = row_pot
-        rest[1][...] = col_pot
+    if first_call:
+        col_pot = log_target - combine_lse(cols_ref[...])
+        row_pot = -combine_lse(rows_ref[...])
+        for pot_ref in refs[7:9]:
+            pot_ref[...] = col_pot
+        for pot_ref in refs[9:11]:
+            pot_ref[...] = row_pot
+    else:
+        col_pot, row_pot = cols_ref[...], rows_ref[...]
     fast = within(peak_ref[...], col_pot, row_pot)
     scale_ref[...] = jnp.where(fast, jnp.exp(col_pot), col_pot)
     row_scale = jnp.exp(row_pot)
-    blocks = a_ref.shape[0]
-    tiles = blocks * BLOCK // LANES
-
-    def plan_tile(spot, block):
+    bits = position_bits()
+    x1, z1 = bits[XB1], bits[ZB1]
+    tiles = []
+    for chain, (first, second) in enumerate(((x1, z1), (z1, x1))):
+        first = 1 - first if flips[0] else first
+        second = 1 - second if flips[1] else second
+        tiles.append(chain * 4 + first * 2 + second)
+
+    def plan_tile(chain, out_ref, block):
         total = jnp.zeros((LANES, LANES), F32)
         for g in range(groups):
             plan = block(g)
             total = total + plan
-            plan_ref[row_tile(spot), lane_group(g)] = plan.astype(jnp.bfloat16)
+            plan_ref[chain * LANES : (chain + 1) * LANES, lane_group(g)] = plan.astype(jnp.bfloat16)
         mass = jnp.broadcast_to(jnp.sum(total, axis=1, keepdims=True), (LANES, LANES))
         lane = lax.broadcasted_iota(jnp.int32, (8, LANES), 1) // (LANES // PARTS)
         for b in range(LANES // BLOCK):
@@ -233,70 +249,50 @@
             for k in range(1, PARTS):
                 at = b * BLOCK + 8 * k
                 unit = jnp.where(lane == k, mass[at : at + 8, :], unit)
-            mass_ref[spot * (LANES // BLOCK) + b] = unit
-
-    bits = position_bits()
-    firsts = []
-    for chain, which in enumerate((XB1, ZB1)):
-        bit = bits[which] if keep else 1 - bits[which]
-        firsts.append((chain * 2 + bit) * tiles)
+            out_ref[b, out_ref.shape[1] - 1] = unit
 
     def sums():
-        size = blocks * BLOCK
+        block = jnp.dot(plan_ref[...], vec_ref[...], preferred_element_type=F32)
+        across = block.shape[1] // LANES
         for chain, out_ref in enumerate((a_ref, b_ref)):
-            block = jnp.dot(
-                plan_ref[chain * size : (chain + 1) * size, :], vec_ref[...], preferred_element_type=F32
-            )
-            across = block.shape[1] // LANES
-            for b in range(blocks):
+            for b in range(LANES // BLOCK):
                 for k in range(PARTS):
-                    row = b * BLOCK + 8 * k
+                    row = chain * LANES + b * BLOCK + 8 * k
                     for g in range(across):
                         out_ref[b, k * across + g] = block[row : row + 8, lane_group(g)]
-                out_ref[b, out_ref.shape[1] - 1] = mass_ref[chain * blocks + b]
 
     @pl.when(fast)
     def _():
-        for chain, first in enumerate(firsts):
-            for t in range(tiles):
-                scale = lane_to_sublane(scale_ref[pl.ds(first + t, 1), :])
-                plan_tile(
-                    chain * tiles + t,
-                    lambda g: k_ref[row_tile(first + t), lane_group(g)] * row_scale[g : g + 1, :] * scale,
-                )
+        for chain, (tile, out_ref) in enumerate(zip(tiles, (a_ref, b_ref))):
+            scale = lane_to_sublane(scale_ref[pl.ds(tile, 1), :])
+            plan_tile(
+                chain,
+                out_ref,
+                lambda g: k_ref[row_tile(tile), lane_group(g)] * row_scale[g : g + 1, :] * scale,
+            )
         sums()
 
     @pl.when(jnp.logical_not(fast))
     def _():
         ok = within(peak_ref[...])
-        for chain, first in enumerate(firsts):
-            def tile(t, carry):
-                shift = lane_to_sublane(scale_ref[pl.ds(first + t, 1), :])
-                plan_tile(
-                    chain * tiles + t,
-                    lambda g: jnp.exp(
-                        logit_block(k_ref, ok, first + t, g) + row_pot[g : g + 1, :] + shift
-                    ),
-                )
-                return carry
-
-            lax.fori_loop(0, tiles, tile, 0)
+        for chain, (tile, out_ref) in enumerate(zip(tiles, (a_ref, b_ref))):
+            shift = lane_to_sublane(scale_ref[pl.ds(tile, 1), :])
+            plan_tile(
+                chain,
+                out_ref,
+                lambda g: jnp.exp(logit_block(k_ref, ok, tile, g) + row_pot[g : g + 1, :] + shift),
+            )
         sums()
 
 
-def fold_kernel(which, keep_ref, got_ref, send_ref, kept_ref):
-    half = send_ref.shape[0]
-    bit = position_bits()[which]
-    mine, other = bit * half, (1 - bit) * half
-    for b in range(half):
-        send_ref[b] = keep_ref[other + b] + got_ref[other + b]
-        kept_ref[b] = keep_ref[mine + b] + got_ref[mine + b]
-
-
-def quarter_kernel(keep_a_ref, got_a_ref, keep_b_ref, got_b_ref, out_ref):
+def add_kernel(mine_ref, got_ref, out_ref):
+    out_ref[...] = mine_ref[...] + got_ref[...]
+
+
+def quarter_kernel(mine_a_ref, first_a_ref, second_a_ref, mine_b_ref, first_b_ref, second_b_ref, out_ref):
     for p in range(out_ref.shape[0]):
-        out_ref[p, 0] = keep_a_ref[p] + got_a_ref[p]
-        out_ref[p, 1] = keep_b_ref[p] + got_b_ref[p]
+        out_ref[p, 0] = mine_a_ref[p] + first_a_ref[p] + second_a_ref[p]
+        out_ref[p, 1] = mine_b_ref[p] + first_b_ref[p] + second_b_ref[p]
 
 
 def four_kernel(got_ref, out_ref):
@@ -326,22 +322,18 @@
         b_ref[at, :] = got_ref[p, 1]
 
 
-def join_kernel(which, mine_ref, got_ref, out_ref):
-    size = mine_ref.shape[0]
-    bit = position_bits()[which]
-    out_ref[pl.ds(pl.multiple_of(bit * size, size), size), :] = mine_ref[...]
-    out_ref[pl.ds(pl.multiple_of((1 - bit) * size, size), size), :] = got_ref[...]
-
-
-def place_kernel(own, a_ref, b_ref, *rest):
-    out_ref, sems = rest[-2:]
-    size = a_ref.shape[0]
+def place_kernel(spots, *refs):
+    out_ref, sems = refs[-2:]
     bits = position_bits()
+    x1, z1 = bits[XB1], bits[ZB1]
     copies = []
-    for chain, (which, part_ref) in enumerate(((XB1, a_ref), (ZB1, b_ref))):
-        side = bits[which] if own else 1 - bits[which]
-        at = pl.ds(pl.multiple_of((2 * chain + side) * size, size), size)
-        copies.append(pltpu.make_async_copy(part_ref, out_ref.at[at, :], sems.at[chain]))
+    for n, ((chain, flips), part_ref) in enumerate(zip(spots, refs)):
+        size = part_ref.shape[0]
+        first, second = (z1, x1) if chain else (x1, z1)
+        first = 1 - first if flips[0] else first
+        second = 1 - second if flips[1] else second
+        at = pl.ds(pl.multiple_of((chain * 4 + first * 2 + second) * size, size), size)
+        copies.append(pltpu.make_async_copy(part_ref, out_ref.at[at, :], sems.at[n]))
     for copy in copies:
         copy.start()
     for copy in copies:
@@ -411,56 +403,48 @@
     )
 
 
-def halve(which, keep, got):
-    half = jax.ShapeDtypeStruct((keep.shape[0] // 2, *keep.shape[1:]), F32)
+def add(mine, got):
     return pl.pallas_call(
-        functools.partial(fold_kernel, which),
-        out_shape=(half, half),
-        in_specs=[vmem(), vmem()],
-        out_specs=(vmem(), vmem()),
-        compiler_params=params(4),
-        name="fold",
-    )(keep, got)
-
-
-def join(which, mine, got):
-    return pl.pallas_call(
-        functools.partial(join_kernel, which),
-        out_shape=jax.ShapeDtypeStruct((2 * mine.shape[0], *mine.shape[1:]), F32),
+        add_kernel,
+        out_shape=jax.ShapeDtypeStruct(mine.shape, F32),
         in_specs=[vmem(), vmem()],
         out_specs=vmem(),
         compiler_params=params(4),
-        name="join",
+        name="add",
     )(mine, got)
 
 
-def put(own, a, b, cents, *before):
+def put(spots, parts, cents, *before):
     return pl.pallas_call(
-        functools.partial(place_kernel, own),
-        out_shape=jax.ShapeDtypeStruct((cents, a.shape[1]), F32),
-        in_specs=[vmem(), vmem()] + [hbm()] * len(before),
+        functools.partial(place_kernel, spots),
+        out_shape=jax.ShapeDtypeStruct((cents, parts[0].shape[1]), F32),
+        in_specs=[vmem()] * len(parts) + [hbm()] * len(before),
         out_specs=hbm(),
-        scratch_shapes=[pltpu.SemaphoreType.DMA((2,))],
-        input_output_aliases={2: 0} if before else {},
+        scratch_shapes=[pltpu.SemaphoreType.DMA((len(parts),))],
+        input_output_aliases={len(parts): 0} if before else {},
         compiler_params=params(4),
         name="place",
-    )(a, b, *before)
-
-
-def mean_over_rows(send_a, keep_a, send_b, keep_b, cents, width):
-    got_a, got_b = exchange(send_a, x_first), exchange(send_b, z_first)
-    send_a, keep_a = halve(ZB1, keep_a, got_a)
-    send_b, keep_b = halve(XB1, keep_b, got_b)
-    got_a, got_b = exchange(send_a, z_first), exchange(send_b, x_first)
-    block = keep_a.shape[1:]
+    )(*parts, *before)
+
+
+def mean_over_rows(quarter_sums, cents, width):
+    pass_a, pass_b = quarter_sums((True, True))
+    pass_a, pass_b = exchange(pass_a, x_first), exchange(pass_b, z_first)
+    stay_a, stay_b = quarter_sums((True, False))
+    stay_a, stay_b = exchange(stay_a, x_first), exchange(stay_b, z_first)
+    mine_a, mine_b = quarter_sums((False, True))
+    next_a = exchange(add(mine_a, pass_a), z_first)
+    next_b = exchange(add(mine_b, pass_b), x_first)
+    mine_a, mine_b = quarter_sums((False, False))
+    block = mine_a.shape[1:]
     quarter = pl.pallas_call(
         quarter_kernel,
         out_shape=jax.ShapeDtypeStruct((4, 2, *block), F32),
-        in_specs=[vmem()] * 4,
+        in_specs=[vmem()] * 6,
         out_specs=vmem(),
         compiler_params=params(4),
         name="quarter",
-    )(keep_a, got_a, keep_b, got_b)
+    )(mine_a, stay_a, next_a, mine_b, stay_b, next_b)
     sums = pl.pallas_call(
         four_kernel,
         out_shape=jax.ShapeDtypeStruct((2, *block), F32),
@@ -486,11 +470,13 @@
         compiler_params=params(4),
         name="part",
     )(trade(mean))
-    got_a, got_b = exchange(mine_a, z_first), exchange(mine_b, x_first)
-    mine_a = join(ZB1, mine_a, got_a)
-    mine_b = join(XB1, mine_b, got_b)
-    got_a, got_b = exchange(mine_a, x_first), exchange(mine_b, z_first)
-    return put(False, got_a, got_b, cents, put(True, mine_a, mine_b, cents))
+    next_a, next_b = exchange(mine_a, z_first), exchange(mine_b, x_first)
+    stay_a, stay_b = exchange(mine_a, x_first), exchange(mine_b, z_first)
+    pass_a, pass_b = exchange(next_a, x_first), exchange(next_b, z_first)
+    out = put(((0, (False, False)), (1, (False, False))), (mine_a, mine_b), cents)
+    out = put(((0, (False, True)), (1, (False, True))), (next_a, next_b), cents, out)
+    out = put(((0, (True, False)), (1, (True, False))), (stay_a, stay_b), cents, out)
+    return put(((0, (True, True)), (1, (True, True))), (pass_a, pass_b), cents, out)
 
 
 def vmem():
@@ -560,31 +546,29 @@
         )(col_got, peak, pinned(kernel))
     row_got = lax.all_to_all(part, "cols", 0, 0, tiled=True)
 
-    part_units = PARTS * (width // LANES) + 1
-    halves = jax.ShapeDtypeStruct((cents // BLOCK // 4, part_units, 8, LANES), F32)
-
-    def half(keep):
-        pots = (jax.ShapeDtypeStruct((groups, LANES), F32), jax.ShapeDtypeStruct((tiles, LANES), F32))
-        return pl.pallas_call(
-            functools.partial(half_kernel, log_target, keep),
-            out_shape=(halves, halves) + (() if keep else pots),
+    quarter = jax.ShapeDtypeStruct((LANES // BLOCK, PARTS * (width // LANES) + 1, 8, LANES), F32)
+    pots = []
+
+    def quarter_sums(flips):
+        first = not pots
+        pot_types = tuple(jax.ShapeDtypeStruct((n, LANES), F32) for n in (tiles, tiles, groups, groups))
+        a, b, *new = pl.pallas_call(
+            functools.partial(sums_kernel, log_target if first else None, flips),
+            out_shape=(quarter, quarter) + (pot_types if first else ()),
             in_specs=[vmem()] * 5,
-            out_specs=(vmem(),) * (2 if keep else 4),
-            scratch_shapes=[
-                col_scratch,
-                pltpu.VMEM((cents // 2, rows), jnp.bfloat16),
-                pltpu.VMEM((cents // BLOCK // 2, 8, LANES), F32),
-            ],
-            compiler_params=params(12),
+            out_specs=(vmem(),) * (6 if first else 2),
+            scratch_shapes=[pltpu.VMEM((2 * LANES, rows), jnp.bfloat16), col_scratch],
+            compiler_params=params(8),
             cost_estimate=pl.CostEstimate(
-                flops=rows * cents * width, bytes_accessed=8 * MIB, transcendentals=0
+                flops=rows * cents * width // 2, bytes_accessed=4 * MIB, transcendentals=0
             ),
-            name="keep" if keep else "send",
-        )(col_got, row_got, peak, pinned(kernel), vectors)
-
-    send_a, send_b, row_pot, col_pot = half(False)
-    keep_a, keep_b = half(True)
-    new_centroids = mean_over_rows(send_a, keep_a, send_b, keep_b, cents, width)
+            name="sums",
+        )(*(pots[1::2] or (col_got, row_got)), peak, pinned(kernel), vectors)
+        pots.extend(new)
+        return a, b
+
+    new_centroids = mean_over_rows(quarter_sums, cents, width)
+    col_pot, row_pot = pots[0::2]
     return (new_centroids, row_pot.reshape(rows), col_pot.reshape(cents))
 
 

time: 293 us -> 284 us (0.969)
  waiting for transfers between devices: 38.6 us -> 22.5 us
  starting transfers between devices: 7.77 us -> 13.5 us
    ppermute x9 -> x13, waiting for transfers between devices: 38.6 us -> 22.5 us  [exchange(): lax.ppermute(x, ('rows', 'cols'), pairs(partner, lax.axis_size('cols')))]
    ppermute x9 -> x13, starting transfers between devices: 7.77 us -> 13.5 us  [exchange(): lax.ppermute(x, ('rows', 'cols'), pairs(partner, lax.axis_size('cols')))]
    pallas_call x8 -> x10, Pallas kernels: 11.1 us -> 12 us  [the longest x4 8.28 us: quarter_sums(): pl.pallas_call(functools.partial(sums_kernel, log_target if first else No...]
  transfers between devices with their start and end apart: 9 -> 13, of which waited for: 7 -> 8; matrix products, arithmetic and copies ran while one was open for 0% -> 0% of each run, Pallas kernels for 2% -> 3%
where the time goes in v5:
time: 284 us; the launch traced here: 282 us
  Pallas kernels  134 us (47%)
  blocking collectives  111 us (39%)
  waiting for transfers between devices  22.5 us (8%)
  starting transfers between devices  13.5 us (5%)
    pallas_call x3, Pallas kernels, per_device(): pl.pallas_call(functools.partial(row_kernel, log_target), out_shape=row_p...  89.6 us
    all_to_all x3, blocking collectives, per_device(): col_got = lax.all_to_all(part, 'rows', 0, 0, tiled=True)  49.1 us
    all_to_all x4, blocking collectives, per_device(): row_got = lax.all_to_all(part, 'cols', 0, 0, tiled=True)  32.9 us
    all_to_all x2, blocking collectives, trade(): lax.all_to_all(x, ('rows', 'cols'), 0, 0, tiled=True, axis_index_groups=q...  29.1 us
    ppermute x13, waiting for transfers between devices, exchange(): lax.ppermute(x, ('rows', 'cols'), pairs(partner, lax.axis_size('cols')))  22.5 us
    pallas_call x1, Pallas kernels, per_device(): pl.pallas_call(logits_kernel, out_shape=(kept, peak_type, row_parts), in_...  21.2 us
    ppermute x13, starting transfers between devices, exchange(): lax.ppermute(x, ('rows', 'cols'), pairs(partner, lax.axis_size('cols')))  13.5 us
    pallas_call x3, Pallas kernels, per_device(): pl.pallas_call(col_kernel, out_shape=col_parts, in_specs=[vmem(), vmem(),...  11.1 us
  transfers between devices with their start and end apart: 13, of which 8 were waited for; matrix products, arithmetic and copies ran while one was open for 0% of the time, Pallas kernels for 3%

profile of v5, /device:TPU:8, one launch (start us, length us, event | category | flops | bytes accessed | tf_op | source)
XLA Modules:
  0.0 282.2 jit_solution(11250663905884773943)
XLA Ops:
  0.6 21.2 %logits.1 = (f32[1024,2048]{1,0:T(8,128)S(1)}, f32[8,128]{1,0:T(8,128)S(1)}, f32[8,16,128]{2,1,0:T(8,128)S(1)}) custom-call(bf16[1024,768]{1,0:T(8,128)(2,1)} %cent_hbm.1, bf16[2048,768]{1,0:T(8,128)(2,1)} %refs_4_.7), custom_call_target="tpu_custom_call" | custom-call | tf_op jit(solution)/shard_map/logits/pallas_call | solution.py:511
  21.8 8.9 %all_to_all.45.got_ref = f32[8,16,128]{2,1,0:T(8,128)S(1)} all-to-all(f32[8,16,128]{2,1,0:T(8,128)S(1)} %get-tuple-element.20), channel_id=1, replica_groups=mesh['rows'=32,'cols'=8] {'cols'}, dimensions={0} | all-to-all | bytes 131072 | tf_op jit(solution)/shard_map/all_to_all | solution.py:527
  30.7 3.7 %col_step.3 = f32[32,8,128]{2,1,0:T(8,128)S(1)} custom-call(f32[8,16,128]{2,1,0:T(8,128)S(1)} %all_to_all.45.got_ref, f32[8,128]{1,0:T(8,128)S(1)} %get-tuple-element.21.peak_ref.refs_2_, f32[1024,2048]{1,0:T(8,128)S(1)} %get-tuple-element.22.k_ref.refs_3_), custom_call_target="tpu_custom_call" | custom-call | tf_op jit(solution)/shard_map/col_step/pallas_call | solution.py:528
  34.4 21.4 %all_to_all.46.got_ref = f32[32,8,128]{2,1,0:T(8,128)S(1)} all-to-all(f32[32,8,128]{2,1,0:T(8,128)S(1)} %col_step.3), channel_id=1, replica_groups=mesh['rows'=32,'cols'=8] {'rows'}, dimensions={0} | all-to-all | bytes 262144 | tf_op jit(solution)/shard_map/all_to_all | solution.py:537
  55.8 29.8 %row_step.3 = f32[8,16,128]{2,1,0:T(8,128)S(1)} custom-call(f32[32,8,128]{2,1,0:T(8,128)S(1)} %all_to_all.46.got_ref, f32[8,128]{1,0:T(8,128)S(1)} %get-tuple-element.21.peak_ref.refs_2_, f32[1024,2048]{1,0:T(8,128)S(1)} %get-tuple-element.22.k_ref.refs_3_), custom_call_target="tpu_custom_call" | custom-call | tf_op jit(solution)/shard_map/row_step/pallas_call | solution.py:538
  85.6 8.0 %all_to_all.47.got_ref = f32[8,16,128]{2,1,0:T(8,128)S(1)} all-to-all(f32[8,16,128]{2,1,0:T(8,128)S(1)} %row_step.3), channel_id=1, replica_groups=mesh['rows'=32,'cols'=8] {'cols'}, dimensions={0} | all-to-all | bytes 131072 | tf_op jit(solution)/shard_map/all_to_all | solution.py:527
  93.6 3.7 %col_step.4 = f32[32,8,128]{2,1,0:T(8,128)S(1)} custom-call(f32[8,16,128]{2,1,0:T(8,128)S(1)} %all_to_all.47.got_ref, f32[8,128]{1,0:T(8,128)S(1)} %get-tuple-element.21.peak_ref.refs_2_, f32[1024,2048]{1,0:T(8,128)S(1)} %get-tuple-element.22.k_ref.refs_3_), custom_call_target="tpu_custom_call" | custom-call | tf_op jit(solution)/shard_map/col_step/pallas_call | solution.py:528
  97.3 13.9 %all_to_all.48.got_ref = f32[32,8,128]{2,1,0:T(8,128)S(1)} all-to-all(f32[32,8,128]{2,1,0:T(8,128)S(1)} %col_step.4), channel_id=1, replica_groups=mesh['rows'=32,'cols'=8] {'rows'}, dimensions={0} | all-to-all | bytes 262144 | tf_op jit(solution)/shard_map/all_to_all | solution.py:537
  111.1 30.0 %row_step.4 = f32[8,16,128]{2,1,0:T(8,128)S(1)} custom-call(f32[32,8,128]{2,1,0:T(8,128)S(1)} %all_to_all.48.got_ref, f32[8,128]{1,0:T(8,128)S(1)} %get-tuple-element.21.peak_ref.refs_2_, f32[1024,2048]{1,0:T(8,128)S(1)} %get-tuple-element.22.k_ref.refs_3_), custom_call_target="tpu_custom_call" | custom-call | tf_op jit(solution)/shard_map/row_step/pallas_call | solution.py:538
  141.1 8.0 %all_to_all.49.got_ref = f32[8,16,128]{2,1,0:T(8,128)S(1)} all-to-all(f32[8,16,128]{2,1,0:T(8,128)S(1)} %row_step.4), channel_id=1, replica_groups=mesh['rows'=32,'cols'=8] {'cols'}, dimensions={0} | all-to-all | bytes 131072 | tf_op jit(solution)/shard_map/all_to_all | solution.py:527
  149.1 3.7 %col_step.5 = f32[32,8,128]{2,1,0:T(8,128)S(1)} custom-call(f32[8,16,128]{2,1,0:T(8,128)S(1)} %all_to_all.49.got_ref, f32[8,128]{1,0:T(8,128)S(1)} %get-tuple-element.21.peak_ref.refs_2_, f32[1024,2048]{1,0:T(8,128)S(1)} %get-tuple-element.22.k_ref.refs_3_), custom_call_target="tpu_custom_call" | custom-call | tf_op jit(solution)/shard_map/col_step/pallas_call | solution.py:528
  152.8 13.9 %all_to_all.50.got_ref.refs_0_ = f32[32,8,128]{2,1,0:T(8,128)S(1)} all-to-all(f32[32,8,128]{2,1,0:T(8,128)S(1)} %col_step.5), channel_id=1, replica_groups=mesh['rows'=32,'cols'=8] {'rows'}, dimensions={0} | all-to-all | bytes 262144 | tf_op jit(solution)/shard_map/all_to_all | solution.py:537
  166.7 0.0 copy-start
  166.7 29.8 %row_step.5 = f32[8,16,128]{2,1,0:T(8,128)S(1)} custom-call(f32[32,8,128]{2,1,0:T(8,128)S(1)} %all_to_all.50.got_ref.refs_0_, f32[8,128]{1,0:T(8,128)S(1)} %get-tuple-element.21.peak_ref.refs_2_, f32[1024,2048]{1,0:T(8,128)S(1)} %get-tuple-element.22.k_ref.refs_3_), custom_call_target="tpu_custom_call" | custom-call | tf_op jit(solution)/shard_map/row_step/pallas_call | solution.py:538
  196.5 8.0 %all_to_all.51.refs_1_ = f32[8,16,128]{2,1,0:T(8,128)S(1)} all-to-all(f32[8,16,128]{2,1,0:T(8,128)S(1)} %row_step.5), channel_id=1, replica_groups=mesh['rows'=32,'cols'=8] {'cols'}, dimensions={0} | all-to-all | bytes 131072 | tf_op jit(solution)/shard_map/all_to_all | solution.py:547
  204.5 0.0 copy-done
  204.5 2.5 sums.4
  207.0 1.2 collective-permute-start.4
  208.2 0.6 collective-permute-start.1
  208.9 2.1 sums.6
  210.9 1.5 collective-permute-start
  212.4 0.8 collective-permute-start.3
  213.2 1.8 sums.7
  215.1 0.0 collective-permute-done.4.got_ref
  215.1 0.7 collective-permute-start.5
  215.8 0.4 collective-permute-done.1.got_ref
  216.2 1.0 collective-permute-start.2
  217.2 1.8 sums.5
  219.1 1.5 collective-permute-done.first_a_ref
  220.6 0.0 collective-permute-done.3.first_b_ref
  220.6 4.4 %collective-permute-done.5.second_b_ref = f32[4,25,8,128]{3,2,1,0:T(8,128)S(1)} collective-permute-done((f32[4,25,8,128]{3,2,1,0:T(8,128)S(1)}, f32[4,25,8,128]{3,2,1,0:T(8,128)S(1)}, u32[]{:S(2)}, u32[]{:S(2)}) %collective-permute-start.5) | collective-permute-done | bytes 409632 | tf_op jit(solution)/shard_map/ppermute | solution.py:359
  225.0 0.0 collective-permute-done.2.second_a_ref
  225.0 0.1 quarter.1
  225.1 13.8 %all_to_all.52.got_ref = f32[4,2,25,8,128]{4,3,2,1,0:T(8,128)S(1)} all-to-all(f32[4,2,25,8,128]{4,3,2,1,0:T(8,128)S(1)} %quarter.1), channel_id=1, replica_groups={{0,56,192,248},{8,16,200,208},{24,32,216,224},{48,40,240,232},{64,120,1..., dimensions={0} | all-to-all | bytes 1638400 | tf_op jit(solution)/shard_map/all_to_all | solution.py:401
  238.9 1.6 collective-permute-start.6
  240.6 8.7 %collective-permute-done.6.got_ref = f32[2,25,8,128]{3,2,1,0:T(8,128)S(1)} collective-permute-done((f32[2,25,8,128]{3,2,1,0:T(8,128)S(1)}, f32[2,25,8,128]{3,2,1,0:T(8,128)S(1)}, u32[]{:S(2)}, u32[]{:S(2)}) %collective-permute-start.6) | collective-permute-done | bytes 204832 | tf_op jit(solution)/shard_map/ppermute | solution.py:359
  249.2 0.1 mean.1
  249.4 15.3 %all_to_all.53.got_ref = f32[4,2,32,768]{3,2,1,0:T(8,128)S(1)} all-to-all(f32[4,2,32,768]{3,2,1,0:T(8,128)S(1)} %mean.1), channel_id=1, replica_groups={{0,56,192,248},{8,16,200,208},{24,32,216,224},{48,40,240,232},{64,120,1..., dimensions={0} | all-to-all | bytes 1572864 | tf_op jit(solution)/shard_map/all_to_all | solution.py:401
  264.7 0.1 part.1
  264.8 0.1 collective-permute-start.7
  264.9 0.1 collective-permute-start.9
  265.0 2.0 collective-permute-start.11
  267.0 1.9 collective-permute-start.12
  268.9 3.7 %collective-permute-done.7.refs_0_ = f32[128,768]{1,0:T(8,128)S(1)} collective-permute-done((f32[128,768]{1,0:T(8,128)S(1)}, f32[128,768]{1,0:T(8,128)S(1)}, u32[]{:S(2)}, u32[]{:S(2)}) %collective-permute-start.7) | collective-permute-done | bytes 393248 | tf_op jit(solution)/shard_map/ppermute | solution.py:359
  272.6 0.0 collective-permute-start.8
  272.6 0.1 collective-permute-done.9.refs_1_
  272.7 1.9 collective-permute-start.10
  274.7 0.9 place.4.refs_2_
  275.6 0.9 place.5.refs_2_
  276.5 0.5 collective-permute-done.11.refs_0_
  276.9 0.0 collective-permute-done.12.refs_1_
  276.9 0.9 place.6.refs_2_
  277.8 3.3 %collective-permute-done.8.refs_0_ = f32[128,768]{1,0:T(8,128)S(1)} collective-permute-done((f32[128,768]{1,0:T(8,128)S(1)}, f32[128,768]{1,0:T(8,128)S(1)}, u32[]{:S(2)}, u32[]{:S(2)}) %collective-permute-start.8) | collective-permute-done | bytes 393248 | tf_op jit(solution)/shard_map/ppermute | solution.py:359
  281.2 0.0 collective-permute-done.10.refs_1_
  281.2 0.9 place.7
  (3 shorter events, 0.1 us)
Async XLA Ops:
  166.7 37.8 %copy-start = (bf16[2048,768]{1,0:T(8,128)(2,1)S(1)}, bf16[2048,768]{1,0:T(8,128)(2,1)}, u32[]{:S(2)}) copy-start(bf16[2048,768]{1,0:T(8,128)(2,1)} %refs_4_.7) | copy-start | bytes 9437188
  207.0 8.1 %collective-permute-start.4 = (f32[4,25,8,128]{3,2,1,0:T(8,128)S(1)}, f32[4,25,8,128]{3,2,1,0:T(8,128)S(1)}, u32[]{:S(2)}, u32[]{:S(2)}) collective-permute-start(f32[4,25,8,128]{3,2,1,0:T(8,128)S(1)} %get-tuple-element.32), channel_id=1, source_target_pairs={{0,8},{1,57},{2,10},{3,59},{4,12},{5,61},{6,14},{7,63},{8,0},{9,17... | collective-permute-start | bytes 1228808 | tf_op jit(solution)/shard_map/ppermute | solution.py:359
  208.2 8.0 %collective-permute-start.1 = (f32[4,25,8,128]{3,2,1,0:T(8,128)S(1)}, f32[4,25,8,128]{3,2,1,0:T(8,128)S(1)}, u32[]{:S(2)}, u32[]{:S(2)}) collective-permute-start(f32[4,25,8,128]{3,2,1,0:T(8,128)S(1)} %get-tuple-element.28), channel_id=1, source_target_pairs={{0,64},{1,193},{2,66},{3,195},{4,68},{5,197},{6,70},{7,199},{8,72}... | collective-permute-start | bytes 1228808 | tf_op jit(solution)/shard_map/ppermute | solution.py:359
  210.9 9.6 %collective-permute-start = (f32[4,25,8,128]{3,2,1,0:T(8,128)S(1)}, f32[4,25,8,128]{3,2,1,0:T(8,128)S(1)}, u32[]{:S(2)}, u32[]{:S(2)}) collective-permute-start(f32[4,25,8,128]{3,2,1,0:T(8,128)S(1)} %get-tuple-element.26), channel_id=1, source_target_pairs={{0,64},{1,193},{2,66},{3,195},{4,68},{5,197},{6,70},{7,199},{8,72}... | collective-permute-start | bytes 1228808 | tf_op jit(solution)/shard_map/ppermute | solution.py:359
  212.4 8.2 %collective-permute-start.3 = (f32[4,25,8,128]{3,2,1,0:T(8,128)S(1)}, f32[4,25,8,128]{3,2,1,0:T(8,128)S(1)}, u32[]{:S(2)}, u32[]{:S(2)}) collective-permute-start(f32[4,25,8,128]{3,2,1,0:T(8,128)S(1)} %get-tuple-element.30), channel_id=1, source_target_pairs={{0,8},{1,57},{2,10},{3,59},{4,12},{5,61},{6,14},{7,63},{8,0},{9,17... | collective-permute-start | bytes 1228808 | tf_op jit(solution)/shard_map/ppermute | solution.py:359
  215.1 9.8 %collective-permute-start.5 = (f32[4,25,8,128]{3,2,1,0:T(8,128)S(1)}, f32[4,25,8,128]{3,2,1,0:T(8,128)S(1)}, u32[]{:S(2)}, u32[]{:S(2)}) collective-permute-start(f32[4,25,8,128]{3,2,1,0:T(8,128)S(1)} %add.3), channel_id=1, source_target_pairs={{0,64},{1,193},{2,66},{3,195},{4,68},{5,197},{6,70},{7,199},{8,72}... | collective-permute-start | bytes 1228808 | tf_op jit(solution)/shard_map/ppermute | solution.py:359
  216.2 8.7 %collective-permute-start.2 = (f32[4,25,8,128]{3,2,1,0:T(8,128)S(1)}, f32[4,25,8,128]{3,2,1,0:T(8,128)S(1)}, u32[]{:S(2)}, u32[]{:S(2)}) collective-permute-start(f32[4,25,8,128]{3,2,1,0:T(8,128)S(1)} %add.2), channel_id=1, source_target_pairs={{0,8},{1,57},{2,10},{3,59},{4,12},{5,61},{6,14},{7,63},{8,0},{9,17... | collective-permute-start | bytes 1228808 | tf_op jit(solution)/shard_map/ppermute | solution.py:359
  238.9 10.3 %collective-permute-start.6 = (f32[2,25,8,128]{3,2,1,0:T(8,128)S(1)}, f32[2,25,8,128]{3,2,1,0:T(8,128)S(1)}, u32[]{:S(2)}, u32[]{:S(2)}) collective-permute-start(f32[2,25,8,128]{3,2,1,0:T(8,128)S(1)} %four.1.sum_ref), channel_id=1, source_target_pairs={{0,24},{1,41},{2,26},{3,43},{4,28},{5,45},{6,30},{7,47},{8,48},{9,... | collective-permute-start | bytes 614408 | tf_op jit(solution)/shard_map/ppermute | solution.py:359
  264.8 7.9 %collective-permute-start.7 = (f32[128,768]{1,0:T(8,128)S(1)}, f32[128,768]{1,0:T(8,128)S(1)}, u32[]{:S(2)}, u32[]{:S(2)}) collective-permute-start(f32[128,768]{1,0:T(8,128)S(1)} %get-tuple-element.33.refs_0_), channel_id=1, source_target_pairs={{0,8},{1,57},{2,10},{3,59},{4,12},{5,61},{6,14},{7,63},{8,0},{9,17... | collective-permute-start | bytes 1179656 | tf_op jit(solution)/shard_map/ppermute | solution.py:359
  264.9 7.9 %collective-permute-start.9 = (f32[128,768]{1,0:T(8,128)S(1)}, f32[128,768]{1,0:T(8,128)S(1)}, u32[]{:S(2)}, u32[]{:S(2)}) collective-permute-start(f32[128,768]{1,0:T(8,128)S(1)} %get-tuple-element.34.refs_1_), channel_id=1, source_target_pairs={{0,64},{1,193},{2,66},{3,195},{4,68},{5,197},{6,70},{7,199},{8,72}... | collective-permute-start | bytes 1179656 | tf_op jit(solution)/shard_map/ppermute | solution.py:359
  265.0 12.0 %collective-permute-start.11 = (f32[128,768]{1,0:T(8,128)S(1)}, f32[128,768]{1,0:T(8,128)S(1)}, u32[]{:S(2)}, u32[]{:S(2)}) collective-permute-start(f32[128,768]{1,0:T(8,128)S(1)} %get-tuple-element.33.refs_0_), channel_id=1, source_target_pairs={{0,64},{1,193},{2,66},{3,195},{4,68},{5,197},{6,70},{7,199},{8,72}... | collective-permute-start | bytes 1179656 | tf_op jit(solution)/shard_map/ppermute | solution.py:359
  267.0 10.0 %collective-permute-start.12 = (f32[128,768]{1,0:T(8,128)S(1)}, f32[128,768]{1,0:T(8,128)S(1)}, u32[]{:S(2)}, u32[]{:S(2)}) collective-permute-start(f32[128,768]{1,0:T(8,128)S(1)} %get-tuple-element.34.refs_1_), channel_id=1, source_target_pairs={{0,8},{1,57},{2,10},{3,59},{4,12},{5,61},{6,14},{7,63},{8,0},{9,17... | collective-permute-start | bytes 1179656 | tf_op jit(solution)/shard_map/ppermute | solution.py:359
  272.6 8.5 %collective-permute-start.8 = (f32[128,768]{1,0:T(8,128)S(1)}, f32[128,768]{1,0:T(8,128)S(1)}, u32[]{:S(2)}, u32[]{:S(2)}) collective-permute-start(f32[128,768]{1,0:T(8,128)S(1)} %collective-permute-done.7.refs_0_), channel_id=1, source_target_pairs={{0,64},{1,193},{2,66},{3,195},{4,68},{5,197},{6,70},{7,199},{8,72}... | collective-permute-start | bytes 1179656 | tf_op jit(solution)/shard_map/ppermute | solution.py:359
  272.7 8.4 %collective-permute-start.10 = (f32[128,768]{1,0:T(8,128)S(1)}, f32[128,768]{1,0:T(8,128)S(1)}, u32[]{:S(2)}, u32[]{:S(2)}) collective-permute-start(f32[128,768]{1,0:T(8,128)S(1)} %collective-permute-done.9.refs_1_), channel_id=1, source_target_pairs={{0,8},{1,57},{2,10},{3,59},{4,12},{5,61},{6,14},{7,63},{8,0},{9,17... | collective-permute-start | bytes 1179656 | tf_op jit(solution)/shard_map/ppermute | solution.py:359
